TPU v7x, 32 devices: a whole 2x2x4 slice. The times are simulated.
32 devices in a mesh: grp: 2 (over x), col: 16 (over z, y, core).
Axes of the slice: x: 2, y: 2, z: 4, core: 2. Of those that a mesh axis runs over, the one named last changes fastest.
Arguments:
- series: float32 [64, 8192], P(None, ('grp', 'col')), parts along dimension 1, as said below
- valid: int32 [64, 8192], P(None, ('grp', 'col')), parts along dimension 1, may hold values 0 or 1
- owners: int32 [8], P('grp'), parts along dimension 0, may hold values from 0 to 14, as said below
- blocks: int32 [8], P('grp'), parts along dimension 0, may hold values from 0 to 7, as said below
- excl: int32 [2], P('grp'), parts along dimension 0, may hold values from 32 to 256
Outputs:
- row_profile: float32 [8, 32], P('grp'), parts along dimension 0
- col_profile: float32 [8192], P(('grp', 'col')), parts along dimension 0
There are 2 independent parts, one for each index of `grp`. A program takes and returns all parts, laid end to end along the dimension named above; each array names one. Nothing has to cross between parts.
Inputs may be any that keep to these rules, and one draw needn't show every extreme that they name: `series`: samples of smooth periodic components plus independent noise; every channel's noise has a standard deviation of at least 0.3 times the factor by which that channel's samples are multiplied. `owners`: the owner of a turn is never the last index of col. `blocks`: block of the owner's own starts.
All inputs are finite; a program needn't handle non-finite values. No bound on the sum of `valid` on one device may be relied on, other than what follows from the above.
Results may differ from a plain program's by a relative error of at most 0.00029.
Values sent between devices are 32-bit elements; how exact they have to be, the bound alone decides.
No kernel may reach another device: no remote copies, remote signals or barrier semaphores. Data moves between devices by JAX's collectives and lax.ppermute only.
A program may use at most 192 MiB of HBM per device.

v0:
```python
import jax
import jax.numpy as jnp
from jax import lax
from jax.sharding import PartitionSpec as P

M = 256
QB = 32


highest = lax.Precision.HIGHEST


def passed_along(block, axis, distance):
    devices = range(lax.axis_size(axis))
    route = [(i - distance, i) for i in devices if i - distance in devices]
    return lax.ppermute(block, axis, route)


def spread_2(block, axis, holder):
    block = jnp.where(lax.axis_index(axis) == holder, block, jnp.zeros_like(block))
    return lax.psum(block, axis)


def slide(signal, kernels, groups):
    return lax.conv_general_dilated(
        signal[None], kernels, (1,), "VALID", feature_group_count=groups, precision=highest
    )[0]


def window_stats(extended, valid, count):
    channels = extended.shape[0]
    ones_kernel = jnp.ones((channels, 1, M), jnp.float32)
    first = slide(extended, ones_kernel, channels)[:, :count]
    second = slide(extended * extended, ones_kernel, channels)[:, :count]
    mean_all = first / M
    spread = second / M - mean_all * mean_all
    scale_all = valid.astype(jnp.float32) / jnp.sqrt(spread + 1e-05)
    return (mean_all, scale_all)


def column_windows(extended, count):
    channels = extended.shape[0]
    width = count + M
    repeated = jnp.tile(extended, (1, M + 1))[:, : M * (width + 1)]
    return repeated.reshape(channels, M, width + 1)[:, :, :count]


def turn_profile(hankel, mean_all, scale_all, samples, q_mean, q_scale):
    channels = hankel.shape[0]
    offsets = jnp.arange(QB)[:, None] + jnp.arange(M)[None, :]
    windows = samples[:, offsets]
    products = jnp.einsum(
        "cqk,ckj->cqj", windows, hankel, precision=highest, preferred_element_type=jnp.float32
    )
    centred = products - M * q_mean[:, :, None] * mean_all[:, None, :]
    summed = jnp.sum(centred * q_scale[:, :, None] * scale_all[:, None, :], axis=0)
    return 1.0 - summed / (M * channels)


def exclude(profile, queries, columns, excl, limit):
    banned = (jnp.abs(queries[:, None] - columns[None, :]) < excl[0]) | (columns > limit)[None, :]
    return jnp.where(banned, jnp.float32(4.0), profile)


def shards(series, valid, owners, blocks, excl):
    channels, seg_len = series.shape
    devices_col = lax.axis_size("col")
    position = lax.axis_index("col")
    following = passed_along(series, "col", -1)
    extended = jnp.concatenate([series, following], axis=1)
    mean_all, scale_all = window_stats(extended, valid, seg_len)
    hankel = column_windows(extended, seg_len)
    columns = position * seg_len + jnp.arange(seg_len, dtype=jnp.int32)
    limit = seg_len * devices_col - M
    turns = owners.shape[0]
    zero = jnp.zeros((), jnp.int32)

    def local_block(block_id):
        start = block_id * QB
        samples = lax.dynamic_slice(extended, (zero, start), (channels, QB + M - 1))
        q_mean = lax.dynamic_slice(mean_all, (zero, start), (channels, QB))
        q_scale = lax.dynamic_slice(scale_all, (zero, start), (channels, QB))
        return (samples, q_mean, q_scale)

    def fetch(turn):
        pieces = local_block(blocks[turn])
        return (
            spread_2(pieces[0], "col", owners[turn]),
            spread_2(pieces[1], "col", owners[turn]),
            spread_2(pieces[2], "col", owners[turn]),
        )

    def step(turn, carry):
        column_min, row_min = carry
        turn = turn.astype(jnp.int32)
        samples, q_mean, q_scale = fetch(turn)
        profile = turn_profile(hankel, mean_all, scale_all, samples, q_mean, q_scale)
        queries = owners[turn] * seg_len + blocks[turn] * QB + jnp.arange(QB, dtype=jnp.int32)
        profile = exclude(profile, queries, columns, excl, limit)
        column_min = jnp.minimum(column_min, jnp.min(profile, axis=0))
        best = jnp.min(profile, axis=1)
        best = lax.pmin(best, "col")
        row_min = lax.dynamic_update_slice(row_min, best[None, :], (turn, zero))
        return (column_min, row_min)

    start_carry = (jnp.full((seg_len,), 4.0, jnp.float32), jnp.zeros((turns, QB), jnp.float32))
    column_min, row_min = lax.fori_loop(0, turns, step, start_carry)
    col_profile = jnp.where(columns > limit, jnp.float32(0.0), column_min)
    return (row_min, col_profile)


def solution(mesh):
    return jax.shard_map(
        shards,
        mesh=mesh,
        in_specs=(P(None, ("grp", "col")), P(None, ("grp", "col")), P("grp"), P("grp"), P("grp")),
        out_specs=(P("grp", None), P(("grp", "col"))),
        check_vma=False,
    )
```

profile of v0, /device:TPU:0, one launch (start us, length us, event | category | flops | bytes accessed | tf_op | source)
XLA Modules:
  0.0 840.1 jit_solution(843079350736450547)
XLA Ops:
  7.2 1.3 collective-permute-start
  8.5 0.8 constant_dynamic-update-slice_fusion.1
  9.3 1.2 collective-permute-done
  10.5 4.4 tile.4
  15.0 21.6 %copy.40 = f32[8,8,257,512]{3,1,2,0:T(8,128)} copy(f32[8,8,257,512]{3,2,1,0:T(8,128)S(1)} %bitcast.43) | data formatting | bytes 67371008
  36.5 22.3 %slice.18 = f32[64,131328]{1,0:T(8,128)} slice(f32[64,131584]{1,0:T(8,128)} %bitcast.44), slice={[0:64], [0:131328]} | slice | bytes 67239936 | tf_op jit(solution)/shard_map/slice | solution.py:44
  58.8 73.5 %reshape.82 = f32[64,256,513]{2,1,0:T(8,128)} reshape(f32[64,131328]{1,0:T(8,128)} %slice.18) | data formatting | bytes 67239936 | tf_op jit(solution)/shard_map/reshape | solution.py:45
  132.3 11.5 %slice.19 = f32[64,256,256]{2,1,0:T(8,128)} slice(f32[64,256,513]{2,1,0:T(8,128)} %reshape.82), slice={[0:64], [0:256], [0:256]} | slice | bytes 33554432 | tf_op jit(solution)/shard_map/slice | solution.py:45
  143.9 3.0 fusion.14
  147.2 3.0 fusion.16
  150.4 682.5 %while.16 = (s32[]{:T(128)}, f32[256]{0:T(256)S(1)}, f32[4,32]{1,0:T(4,128)}, s32[4]{0:T(128)S(1)}, s32[4]{0:T(128)S(1)}, /*index=5*/s32[1]{0:T(128)}, f32[64,51...) while((s32[]{:T(128)}, f32[256]{0:T(256)S(1)}, ...), condition=%wide.region_8.9_spmd.clone, body=%wide.region_0.8_spmd.clone.sunk | while | flops 1613388672 | bytes 28792072 | solution.py:107
  152.1 0.7 dynamic_slice.54
  153.5 0.7 broadcast_select_fusion.2
  155.0 63.4 %all-reduce.2 = (f32[64,32]{1,0:T(8,128)S(1)}, f32[64,32]{1,0:T(8,128)S(1)}) all-reduce(f32[64,32]{1,0:T(8,128)S(1)} %get-tuple-element.353, f32[64,32]{1,0:T(8,128)S(1)} %get-tuple-element.354), channel_id=1, replica_groups=mesh['grp'=2,'col'=16] {'col'}, use_global_device_ids=true, to_apply=%region_3.3 | all-reduce | flops 4096 | bytes 32768 | tf_op jit(solution)/shard_map/while/body/eval_jaxpr/psum | solution.py:21
  218.4 28.7 %all-reduce.5.cloned.1.call-done = f32[64,287]{0,1:T(8,128)} async-done(((f32[64,287]{0,1:T(8,128)}), f32[64,287]{0,1:T(8,128)}) %all-reduce.5.cloned.1.call-update) | async-done | bytes 73488 | tf_op jit(solution)/shard_map/while/body/eval_jaxpr/psum | solution.py:21
  247.1 28.6 %gather_fusion = f32[8192,64]{1,0:T(8,128)} fusion(f32[64,287]{0,1:T(8,128)} %all-reduce.5.cloned.1.call-done, s32[8192]{0:T(1024)S(1)} %broadcast_clamp_fusion.2), kind=kCustom, calls=%fused_computation.clone.clone.1 | custom fusion | bytes 4227072 | tf_op jit(solution)/shard_map/while/body/eval_jaxpr/gather | solution.py:51
  275.7 3.4 copy.46
  279.1 13.1 %multiply_reduce_fusion.2 = f32[32,256]{1,0:T(8,128)S(1)} fusion(f32[64,256,256]{2,1,0:T(8,128)} %get-tuple-element.400, f32[32,256,64]{1,0,2:T(8,128)S(1)} %copy.46, f32[64,256]{1,0:T(8,128)S(1)} %get-tuple-element.402, f32[64,32]{1,0:T(8,128)S(1)} %get-tuple-element.355, f32[64,256]{1,0:T(8,128)S(1)} %get-tuple-element.401, ...), kind=kOutput, calls=%fused_computation.4.clone.1 | convolution fusion | flops 1613225984 | bytes 19054592 | tf_op jit(solution)/shard_map/while/body/eval_jaxpr/cqk,ckj->cqj/dot_general | solution.py:52
  292.2 0.8 fusion.30
  293.1 32.4 %pmin.13 = f32[1,32]{1,0:T(1,128)S(1)} all-reduce(f32[1,32]{1,0:T(1,128)S(1)} %bitcast.51), channel_id=1, replica_groups=mesh['grp'=2,'col'=16] {'col'}, use_global_device_ids=true, to_apply=%region_7.7 | all-reduce | flops 32 | bytes 256 | tf_op jit(solution)/shard_map/while/body/eval_jaxpr/pmin | solution.py:102
  325.4 1.3 dynamic_update_slice.9
  329.6 0.7 broadcast_select_fusion.2
  331.1 57.8 %all-reduce.2 = (f32[64,32]{1,0:T(8,128)S(1)}, f32[64,32]{1,0:T(8,128)S(1)}) all-reduce(f32[64,32]{1,0:T(8,128)S(1)} %get-tuple-element.353, f32[64,32]{1,0:T(8,128)S(1)} %get-tuple-element.354), channel_id=1, replica_groups=mesh['grp'=2,'col'=16] {'col'}, use_global_device_ids=true, to_apply=%region_3.3 | all-reduce | flops 4096 | bytes 32768 | tf_op jit(solution)/shard_map/while/body/eval_jaxpr/psum | solution.py:21
  388.9 27.2 %all-reduce.5.cloned.1.call-done = f32[64,287]{0,1:T(8,128)} async-done(((f32[64,287]{0,1:T(8,128)}), f32[64,287]{0,1:T(8,128)}) %all-reduce.5.cloned.1.call-update) | async-done | bytes 73488 | tf_op jit(solution)/shard_map/while/body/eval_jaxpr/psum | solution.py:21
  416.0 28.6 %gather_fusion = f32[8192,64]{1,0:T(8,128)} fusion(f32[64,287]{0,1:T(8,128)} %all-reduce.5.cloned.1.call-done, s32[8192]{0:T(1024)S(1)} %broadcast_clamp_fusion.2), kind=kCustom, calls=%fused_computation.clone.clone.1 | custom fusion | bytes 4227072 | tf_op jit(solution)/shard_map/while/body/eval_jaxpr/gather | solution.py:51
  444.6 3.4 copy.46
  448.0 13.1 %multiply_reduce_fusion.2 = f32[32,256]{1,0:T(8,128)S(1)} fusion(f32[64,256,256]{2,1,0:T(8,128)} %get-tuple-element.400, f32[32,256,64]{1,0,2:T(8,128)S(1)} %copy.46, f32[64,256]{1,0:T(8,128)S(1)} %get-tuple-element.402, f32[64,32]{1,0:T(8,128)S(1)} %get-tuple-element.355, f32[64,256]{1,0:T(8,128)S(1)} %get-tuple-element.401, ...), kind=kOutput, calls=%fused_computation.4.clone.1 | convolution fusion | flops 1613225984 | bytes 19054592 | tf_op jit(solution)/shard_map/while/body/eval_jaxpr/cqk,ckj->cqj/dot_general | solution.py:52
  461.1 0.8 fusion.30
  462.0 32.4 %pmin.13 = f32[1,32]{1,0:T(1,128)S(1)} all-reduce(f32[1,32]{1,0:T(1,128)S(1)} %bitcast.51), channel_id=1, replica_groups=mesh['grp'=2,'col'=16] {'col'}, use_global_device_ids=true, to_apply=%region_7.7 | all-reduce | flops 32 | bytes 256 | tf_op jit(solution)/shard_map/while/body/eval_jaxpr/pmin | solution.py:102
  494.3 1.3 dynamic_update_slice.9
  498.5 0.7 broadcast_select_fusion.2
  500.0 57.7 %all-reduce.2 = (f32[64,32]{1,0:T(8,128)S(1)}, f32[64,32]{1,0:T(8,128)S(1)}) all-reduce(f32[64,32]{1,0:T(8,128)S(1)} %get-tuple-element.353, f32[64,32]{1,0:T(8,128)S(1)} %get-tuple-element.354), channel_id=1, replica_groups=mesh['grp'=2,'col'=16] {'col'}, use_global_device_ids=true, to_apply=%region_3.3 | all-reduce | flops 4096 | bytes 32768 | tf_op jit(solution)/shard_map/while/body/eval_jaxpr/psum | solution.py:21
  557.8 27.1 %all-reduce.5.cloned.1.call-done = f32[64,287]{0,1:T(8,128)} async-done(((f32[64,287]{0,1:T(8,128)}), f32[64,287]{0,1:T(8,128)}) %all-reduce.5.cloned.1.call-update) | async-done | bytes 73488 | tf_op jit(solution)/shard_map/while/body/eval_jaxpr/psum | solution.py:21
  584.8 28.6 %gather_fusion = f32[8192,64]{1,0:T(8,128)} fusion(f32[64,287]{0,1:T(8,128)} %all-reduce.5.cloned.1.call-done, s32[8192]{0:T(1024)S(1)} %broadcast_clamp_fusion.2), kind=kCustom, calls=%fused_computation.clone.clone.1 | custom fusion | bytes 4227072 | tf_op jit(solution)/shard_map/while/body/eval_jaxpr/gather | solution.py:51
  613.4 3.4 copy.46
  616.8 13.1 %multiply_reduce_fusion.2 = f32[32,256]{1,0:T(8,128)S(1)} fusion(f32[64,256,256]{2,1,0:T(8,128)} %get-tuple-element.400, f32[32,256,64]{1,0,2:T(8,128)S(1)} %copy.46, f32[64,256]{1,0:T(8,128)S(1)} %get-tuple-element.402, f32[64,32]{1,0:T(8,128)S(1)} %get-tuple-element.355, f32[64,256]{1,0:T(8,128)S(1)} %get-tuple-element.401, ...), kind=kOutput, calls=%fused_computation.4.clone.1 | convolution fusion | flops 1613225984 | bytes 19054592 | tf_op jit(solution)/shard_map/while/body/eval_jaxpr/cqk,ckj->cqj/dot_general | solution.py:52
  629.9 0.8 fusion.30
  630.8 32.4 %pmin.13 = f32[1,32]{1,0:T(1,128)S(1)} all-reduce(f32[1,32]{1,0:T(1,128)S(1)} %bitcast.51), channel_id=1, replica_groups=mesh['grp'=2,'col'=16] {'col'}, use_global_device_ids=true, to_apply=%region_7.7 | all-reduce | flops 32 | bytes 256 | tf_op jit(solution)/shard_map/while/body/eval_jaxpr/pmin | solution.py:102
  663.2 1.3 dynamic_update_slice.9
  667.3 0.7 broadcast_select_fusion.2
  668.8 57.7 %all-reduce.2 = (f32[64,32]{1,0:T(8,128)S(1)}, f32[64,32]{1,0:T(8,128)S(1)}) all-reduce(f32[64,32]{1,0:T(8,128)S(1)} %get-tuple-element.353, f32[64,32]{1,0:T(8,128)S(1)} %get-tuple-element.354), channel_id=1, replica_groups=mesh['grp'=2,'col'=16] {'col'}, use_global_device_ids=true, to_apply=%region_3.3 | all-reduce | flops 4096 | bytes 32768 | tf_op jit(solution)/shard_map/while/body/eval_jaxpr/psum | solution.py:21
  726.6 26.8 %all-reduce.5.cloned.1.call-done = f32[64,287]{0,1:T(8,128)} async-done(((f32[64,287]{0,1:T(8,128)}), f32[64,287]{0,1:T(8,128)}) %all-reduce.5.cloned.1.call-update) | async-done | bytes 73488 | tf_op jit(solution)/shard_map/while/body/eval_jaxpr/psum | solution.py:21
  753.4 28.6 %gather_fusion = f32[8192,64]{1,0:T(8,128)} fusion(f32[64,287]{0,1:T(8,128)} %all-reduce.5.cloned.1.call-done, s32[8192]{0:T(1024)S(1)} %broadcast_clamp_fusion.2), kind=kCustom, calls=%fused_computation.clone.clone.1 | custom fusion | bytes 4227072 | tf_op jit(solution)/shard_map/while/body/eval_jaxpr/gather | solution.py:51
  782.0 3.4 copy.46
  785.3 13.1 %multiply_reduce_fusion.2 = f32[32,256]{1,0:T(8,128)S(1)} fusion(f32[64,256,256]{2,1,0:T(8,128)} %get-tuple-element.400, f32[32,256,64]{1,0,2:T(8,128)S(1)} %copy.46, f32[64,256]{1,0:T(8,128)S(1)} %get-tuple-element.402, f32[64,32]{1,0:T(8,128)S(1)} %get-tuple-element.355, f32[64,256]{1,0:T(8,128)S(1)} %get-tuple-element.401, ...), kind=kOutput, calls=%fused_computation.4.clone.1 | convolution fusion | flops 1613225984 | bytes 19054592 | tf_op jit(solution)/shard_map/while/body/eval_jaxpr/cqk,ckj->cqj/dot_general | solution.py:52
  798.5 0.8 fusion.30
  799.3 32.4 %pmin.13 = f32[1,32]{1,0:T(1,128)S(1)} all-reduce(f32[1,32]{1,0:T(1,128)S(1)} %bitcast.51), channel_id=1, replica_groups=mesh['grp'=2,'col'=16] {'col'}, use_global_device_ids=true, to_apply=%region_7.7 | all-reduce | flops 32 | bytes 256 | tf_op jit(solution)/shard_map/while/body/eval_jaxpr/pmin | solution.py:102
  831.7 1.3 dynamic_update_slice.9
  (77 shorter events, 7.0 us)
Async XLA Ops:
  7.2 3.4 collective-permute-start
  132.3 11.5 %copy-start = (f32[64,256]{1,0:T(8,128)S(1)}, f32[64,256]{1,0:T(8,128)}, u32[]{:S(2)}) copy-start(f32[64,256]{1,0:T(8,128)} %param.7) | copy-start | bytes 196612
  147.2 3.2 copy-start.1
  147.2 3.2 copy-start.2
  147.2 3.2 copy-start.3
  150.6 96.5 %all-reduce.5.cloned.1.call-start = ((), (), s32[]{:S(2)}) async-start(), calls=%async_computation | async-start | bytes 294912 | tf_op jit(solution)/shard_map/while/body/eval_jaxpr/psum | solution.py:21
  326.7 89.3 %all-reduce.5.cloned.1.call-start = ((), (), s32[]{:S(2)}) async-start(), calls=%async_computation | async-start | bytes 294912 | tf_op jit(solution)/shard_map/while/body/eval_jaxpr/psum | solution.py:21
  495.6 89.2 %all-reduce.5.cloned.1.call-start = ((), (), s32[]{:S(2)}) async-start(), calls=%async_computation | async-start | bytes 294912 | tf_op jit(solution)/shard_map/while/body/eval_jaxpr/psum | solution.py:21
  664.4 88.9 %all-reduce.5.cloned.1.call-start = ((), (), s32[]{:S(2)}) async-start(), calls=%async_computation | async-start | bytes 294912 | tf_op jit(solution)/shard_map/while/body/eval_jaxpr/psum | solution.py:21
Sparse Core Ops, SparseCore 0:
  154.9 92.1 all-reduce.4
  331.0 84.9 all-reduce.4
  499.9 84.9 all-reduce.4
  668.4 84.9 all-reduce.4
where the time goes:
time: 841 us; the launch traced here: 840 us
  blocking collectives  366 us (44%)
  local copies, waits for them, and re-layouts  273 us (32%)
  waiting for transfers between devices  111 us (13%)
  matrix products  58.4 us (7%)
  between operations  13.8 us (2%)
  loops' own time  8.79 us (1%)
    psum x4, blocking collectives, spread_2(): return lax.psum(block, axis)  237 us
    pmin x4, blocking collectives, step(): best = lax.pmin(best, 'col')  130 us
    gather x8, local copies, waits for them, and re-layouts, turn_profile(): windows = samples[:, offsets]  128 us
    psum x4, waiting for transfers between devices, spread_2(): return lax.psum(block, axis)  110 us
    reshape x1, local copies, waits for them, and re-layouts, column_windows(): return repeated.reshape(channels, M, width + 1)[:, :, :count]  73.5 us
    dot_general x4, matrix products, turn_profile(): jnp.einsum('cqk,ckj->cqj', windows, hankel, precision=highest, preferred_...  52.4 us
    unnamed x10, local copies, waits for them, and re-layouts  22.4 us
    slice x1, local copies, waits for them, and re-layouts, column_windows(): repeated = jnp.tile(extended, (1, M + 1))[:, :M * (width + 1)]  22.3 us
  transfers between devices with their start and end apart: 5, of which 5 were waited for; matrix products, arithmetic and copies ran while one was open for 0% of the time, Pallas kernels for 0%

commit v1 on v0

v1 whole, which is shorter than its diff:
```python
import functools

import jax
import jax.numpy as jnp
from jax import lax
from jax.experimental import pallas as pl
from jax.experimental.pallas import tpu as pltpu
from jax.sharding import PartitionSpec as P

M = 256
QB = 32
GROUP = 4
LANES = 128

f32 = jnp.float32
bf16 = jnp.bfloat16


def exchanged(block, mask):
    devices = range(lax.axis_size("col"))
    return lax.ppermute(block, "col", [(i, i ^ mask) for i in devices])


def rounds_beyond_group(devices):
    rounds, base, left = [], GROUP, devices // GROUP
    while left > 1:
        radix = 4 if left % 4 == 0 else 2
        rounds.append([base * i for i in range(1, radix)])
        base, left = base * radix, left // radix
    return rounds


def split3(value):
    high = value.astype(bf16)
    rest = value - high.astype(f32)
    mid = rest.astype(bf16)
    low = (rest - mid.astype(f32)).astype(bf16)
    return high, mid, low


def contributions_kernel(owners, blocks, x_ref, v_ref, *outs):
    turns = owners.shape[0]
    quarter = x_ref.shape[0] // GROUP
    width = x_ref.shape[1]
    here = lax.axis_index("col")
    member = lax.rem(here, GROUP)
    row = lax.broadcasted_iota(jnp.int32, (width, width), 0)
    col = lax.broadcasted_iota(jnp.int32, (width, width), 1)
    flip = (row + col == width - 1).astype(bf16)
    lane = lax.broadcasted_iota(jnp.int32, (quarter, width), 1)
    lane_128 = lax.broadcasted_iota(jnp.int32, (quarter, LANES), 1)
    per_tile = LANES // QB
    for mask, out in enumerate(outs):
        rows = pl.ds(pl.multiple_of((member ^ mask) * quarter, quarter), quarter)
        pieces = split3(x_ref[rows, :])
        turned = sum(jnp.dot(p, flip, preferred_element_type=f32) for p in reversed(pieces))
        flags = v_ref[rows, :].astype(f32)
        for tile in range(turns // per_tile):
            tails = jnp.zeros((quarter, LANES), f32)
            valids = jnp.zeros((quarter, LANES), f32)
            for i in range(per_tile):
                turn = tile * per_tile + i
                shift = blocks[turn] * QB
                mine = owners[turn] == here
                after = owners[turn] + 1 == here
                rolled = pltpu.roll(turned, lax.rem(shift + QB, width), 1)
                split = shift + QB
                keep = jnp.where(lane >= split, mine.astype(jnp.int32), after.astype(jnp.int32)) == 1
                out[:, turn * M : (turn + 1) * M] = jnp.where(keep, rolled, 0.0)
                there = (lane_128 >= i * QB) & (lane_128 < (i + 1) * QB) & (mine.astype(jnp.int32) == 1)
                tail = rolled[:, :LANES]
                flag = pltpu.roll(flags, lax.rem(width - shift, width), 1)[:, :LANES]
                if i:
                    tail = pltpu.roll(tail, i * QB, 1)
                    flag = pltpu.roll(flag, i * QB, 1)
                tails = jnp.where(there, tail, tails)
                valids = jnp.where(there, flag, valids)
            at = turns * M + tile * LANES
            out[:, at : at + LANES] = tails
            at = turns * (M + QB) + tile * LANES
            out[:, at : at + LANES] = valids


def query_kernel(turns, band_ref, *refs):
    parts, out = refs[:-1], refs[-1]
    total = parts[0][...]
    for part in parts[1:]:
        total = total + part[...]
    samples = turns * (M + QB)
    per_tile = LANES // QB
    main, tail = [], []
    for tile in range(turns // per_tile):
        at = turns * M + tile * LANES
        tail_tile = total[:, at : at + LANES]
        lane = lax.broadcasted_iota(jnp.int32, tail_tile.shape, 1)
        centre = jnp.zeros_like(tail_tile)
        for i in range(per_tile):
            turn = tile * per_tile + i
            block = total[:, turn * M : (turn + 1) * M]
            mean = jnp.sum(block, axis=1, keepdims=True) * (1.0 / M)
            main.append(block - mean)
            centre = jnp.where((lane >= i * QB) & (lane < (i + 1) * QB), mean, centre)
        tail.append(tail_tile - centre)
    for tile in range(turns // per_tile):
        rows = main[tile * per_tile : (tile + 1) * per_tile] + [tail[tile]]
        shifted = jnp.concatenate(rows, axis=1)
        quarter = shifted.shape[0]
        stack = jnp.concatenate([*split3(shifted), *split3(shifted * shifted)], axis=0)
        sums = jnp.dot(stack, band_ref[...], preferred_element_type=f32)
        first = sums[2 * quarter : 3 * quarter] + sums[quarter : 2 * quarter] + sums[:quarter]
        second = sums[5 * quarter : 6 * quarter] + sums[4 * quarter : 5 * quarter] + sums[3 * quarter : 4 * quarter]
        mean = first * (1.0 / M)
        spread = second * (1.0 / M) - mean * mean
        at = samples + tile * LANES
        scale = total[:, at : at + LANES] / jnp.sqrt(spread + 1e-05)
        out[:, at : at + LANES] = scale
        out[:, at + turns * QB : at + turns * QB + LANES] = mean * scale
    for turn in range(turns):
        out[:, turn * M : (turn + 1) * M] = main[turn]
    for tile in range(turns // per_tile):
        at = turns * M + tile * LANES
        out[:, at : at + LANES] = tail[tile]


def band_matrix():
    per_tile = LANES // QB
    query = jnp.arange(LANES)
    lane = jnp.arange(per_tile * (M + QB))
    in_main = lane < per_tile * M
    turn = jnp.where(in_main, lane // M, (lane - per_tile * M) // QB)
    place = jnp.where(in_main, lane % M, M + (lane - per_tile * M) % QB)
    q = query % QB
    inside = (place[:, None] >= QB - q[None, :]) & (place[:, None] <= M + QB - 1 - q[None, :])
    return ((turn[:, None] == query[None, :] // QB) & inside).astype(bf16)


def columns_kernel(first_mask, x_ref, h_ref, v_ref, hankel, scale_ref, offset_ref):
    quarter = x_ref.shape[0] // GROUP
    width = x_ref.shape[1]
    member = lax.rem(lax.axis_index("col"), GROUP)
    for piece in range(2):
        rows = pl.ds(pl.multiple_of((member ^ (first_mask + piece)) * quarter, quarter), quarter)
        own = x_ref[rows, :]
        centre = jnp.sum(own, axis=1, keepdims=True) * (1.0 / width)
        extended = jnp.concatenate([own - centre, h_ref[rows, :] - centre], axis=1)
        length = extended.shape[1]
        first, second = extended, extended * extended
        step = 1
        while step < M:
            first = first + pltpu.roll(first, length - step, 1)
            second = second + pltpu.roll(second, length - step, 1)
            step *= 2
        mean = first[:, :width] * (1.0 / M)
        spread = second[:, :width] * (1.0 / M) - mean * mean
        scale = v_ref[rows, :].astype(f32) / jnp.sqrt(jnp.maximum(spread, 0.0) + 1e-05)
        into = slice(piece * quarter, (piece + 1) * quarter)
        scale_ref[into, :] = scale
        offset_ref[into, :] = mean * scale
        for c in range(quarter):
            base = jnp.broadcast_to(extended[c : c + 1, :], (16, length))
            base = pltpu.roll(base, length - 15, 1, stride=1, stride_axis=0).astype(bf16)
            for b in range(M // 16):
                shift = M - 16 - 16 * b
                block = pltpu.roll(base, length - shift, 1) if shift else base
                hankel[piece * quarter + c, 16 * b : 16 * (b + 1), :] = block[:, :width]


def partial_sum(turns, pieces, hankel, scale_ref, offset_ref, acc):
    queries = turns * QB
    samples = turns * (M + QB)
    per_tile = LANES // QB
    quarter = pieces[0].shape[0]
    for index, piece in enumerate(pieces):
        by_query = jnp.transpose(piece[:, samples : samples + queries])
        offsets = jnp.transpose(piece[:, samples + queries : samples + 2 * queries])
        lines = []
        for turn in range(turns):
            at = turns * M + (turn // per_tile) * LANES
            tail = piece[:, at : at + LANES]
            if turn % per_tile:
                tail = pltpu.roll(tail, LANES - (turn % per_tile) * QB, 1)
            lines.append(jnp.concatenate([piece[:, turn * M : (turn + 1) * M], tail], axis=1))
        length = M + LANES
        for c in range(quarter):
            windows = []
            for turn in range(turns):
                row = jnp.broadcast_to(lines[turn][c : c + 1, :], (QB, length))
                row = pltpu.roll(row, length - QB, 1, stride=1, stride_axis=0)
                windows.append(row[:, :M].astype(bf16))
            at = index * quarter + c
            products = jnp.dot(jnp.concatenate(windows, axis=0), hankel[at], preferred_element_type=f32)
            acc = acc + products * by_query[:, c : c + 1] * scale_ref[at : at + 1, :]
        rows = slice(index * quarter, (index + 1) * quarter)
        means = jnp.dot(offsets, offset_ref[rows, :], preferred_element_type=f32, precision=lax.Precision.HIGHEST)
        acc = acc - M * means
    return acc


def first_half_kernel(turns, ya, yb, hankel, scale_ref, offset_ref, out):
    zero = jnp.zeros(out.shape, f32)
    out[...] = partial_sum(turns, (ya, yb), hankel, scale_ref, offset_ref, zero)


def second_half_kernel(
    turns, channels, limit, owners, blocks, excl, ya, yb, hankel, scale_ref, offset_ref, so_far, row_out, col_out
):
    summed = partial_sum(turns, (ya, yb), hankel, scale_ref, offset_ref, so_far[...])
    distance = 1.0 - summed * (1.0 / (M * channels))
    width = distance.shape[1]
    columns = lax.axis_index("col") * width + lax.broadcasted_iota(jnp.int32, (QB, width), 1)
    within = lax.broadcasted_iota(jnp.int32, (QB, width), 0)
    beyond = columns > limit
    column_min = jnp.full((1, width), 4.0, f32)
    rows = []
    for turn in range(turns):
        query = owners[turn] * width + blocks[turn] * QB + within
        banned = (jnp.abs(query - columns) < excl[0]) | beyond
        block = jnp.where(banned, 4.0, distance[turn * QB : (turn + 1) * QB, :])
        column_min = jnp.minimum(column_min, jnp.min(block, axis=0, keepdims=True))
        rows.append(jnp.min(block, axis=1, keepdims=True))
    col_out[...] = jnp.where(beyond[:1, :], 0.0, column_min)
    stacked = jnp.concatenate(rows, axis=0)
    flat = jnp.transpose(jnp.broadcast_to(stacked, (turns * QB, LANES)))[:1, :]
    for turn in range(turns):
        row_out[turn : turn + 1, :] = flat[:, turn * QB : (turn + 1) * QB]


VMEM = pl.BlockSpec(memory_space=pltpu.VMEM)
SMEM = pl.BlockSpec(memory_space=pltpu.SMEM)
PARAMS = pltpu.CompilerParams(vmem_limit_bytes=40 * 2**20)


def shards(series, valid, owners, blocks, excl):
    channels, seg_len = series.shape
    devices_col = lax.axis_size("col")
    turns = owners.shape[0]
    quarter = channels // GROUP
    queries = turns * QB
    limit = seg_len * devices_col - M

    following = lax.ppermute(series, "col", [(i, i - 1) for i in range(1, devices_col)])

    share = jax.ShapeDtypeStruct((quarter, turns * (M + 2 * QB)), f32)
    shares = pl.pallas_call(
        contributions_kernel,
        out_shape=[share] * GROUP,
        in_specs=[SMEM, SMEM, VMEM, VMEM],
        out_specs=[VMEM] * GROUP,
        compiler_params=PARAMS,
        name="contributions",
    )(owners, blocks, series, valid)
    arrived = [exchanged(shares[mask], mask) for mask in (3, 2, 1)]
    total = shares[0] + arrived[0] + arrived[1] + arrived[2]

    rounds = rounds_beyond_group(devices_col)
    for masks in rounds[:-1]:
        total = sum([exchanged(total, mask) for mask in masks], total)
    order = (0, 2, 1) if len(rounds[-1]) == 3 else (0,)
    parts = [total] + [exchanged(total, rounds[-1][i]) for i in order]
    query = jax.ShapeDtypeStruct((quarter, turns * (M + 3 * QB)), f32)
    mine = pl.pallas_call(
        functools.partial(query_kernel, turns),
        out_shape=query,
        in_specs=[VMEM] * (1 + len(parts)),
        out_specs=VMEM,
        compiler_params=PARAMS,
        name="query_stats",
    )(band_matrix(), *parts)

    def column_side(first_mask):
        return pl.pallas_call(
            functools.partial(columns_kernel, first_mask),
            out_shape=[
                jax.ShapeDtypeStruct((2 * quarter, M, seg_len), bf16),
                jax.ShapeDtypeStruct((2 * quarter, seg_len), f32),
                jax.ShapeDtypeStruct((2 * quarter, seg_len), f32),
            ],
            in_specs=[VMEM] * 3,
            out_specs=[VMEM] * 3,
            compiler_params=PARAMS,
            cost_estimate=pl.CostEstimate(flops=10**8, bytes_accessed=8 * 2**20, transcendentals=0),
            name="columns",
        )(series, following, valid)

    sides = column_side(0), column_side(2)
    others = {mask: exchanged(mine, mask) for mask in (3, 2, 1)}

    half = pl.pallas_call(
        functools.partial(first_half_kernel, turns),
        out_shape=jax.ShapeDtypeStruct((queries, seg_len), f32),
        in_specs=[VMEM] * 5,
        out_specs=VMEM,
        compiler_params=PARAMS,
        cost_estimate=pl.CostEstimate(flops=5 * 10**8, bytes_accessed=4 * 2**20, transcendentals=0),
        name="first_half",
    )(mine, others[1], *sides[0])
    rows, column = pl.pallas_call(
        functools.partial(second_half_kernel, turns, channels, limit),
        out_shape=[jax.ShapeDtypeStruct((turns, QB), f32), jax.ShapeDtypeStruct((1, seg_len), f32)],
        in_specs=[SMEM] * 3 + [VMEM] * 6,
        out_specs=[VMEM] * 2,
        compiler_params=PARAMS,
        name="second_half",
    )(owners, blocks, excl, others[2], others[3], *sides[1], half)

    for masks in [[1, 2, 3], *rounds]:
        rows = functools.reduce(jnp.minimum, [exchanged(rows, mask) for mask in masks], rows)
    return (rows, column.reshape(seg_len))


def solution(mesh):
    return jax.shard_map(
        shards,
        mesh=mesh,
        in_specs=(P(None, ("grp", "col")), P(None, ("grp", "col")), P("grp"), P("grp"), P("grp")),
        out_specs=(P("grp", None), P(("grp", "col"))),
        check_vma=False,
    )
```

time: 841 us -> 61.2 us (0.07)
  blocking collectives: 366 us -> 0 us
  local copies, waits for them, and re-layouts: 273 us -> 6.34 us
  waiting for transfers between devices: 111 us -> 16.8 us
  matrix products: 58.4 us -> 0 us
  starting transfers between devices: 1.38 us -> 20.5 us
  Pallas kernels: 0 us -> 14.3 us
  between operations: 13.8 us -> 1.46 us
  loops' own time: 8.79 us -> 0 us
    psum x4 -> x0, blocking collectives: 237 us -> none  [spread_2(): return lax.psum(block, axis)]
    pmin x4 -> x0, blocking collectives: 130 us -> none  [step(): best = lax.pmin(best, 'col')]
    gather x8 -> x0, local copies, waits for them, and re-layouts: 128 us -> none  [turn_profile(): windows = samples[:, offsets]]
    psum x4 -> x0, waiting for transfers between devices: 110 us -> none  [spread_2(): return lax.psum(block, axis)]
    reshape x1 -> x0, local copies, waits for them, and re-layouts: 73.5 us -> none  [column_windows(): return repeated.reshape(channels, M, width + 1)[:, :, :count]]
    dot_general x4 -> x0, matrix products: 52.4 us -> none  [turn_profile(): jnp.einsum('cqk,ckj->cqj', windows, hankel, precision=highest, preferred_...]
    slice x2 -> x0, local copies, waits for them, and re-layouts: 33.8 us -> none  [the longest x1 22.3 us: column_windows(): repeated = jnp.tile(extended, (1, M + 1))[:, :M * (width + 1)]]
    ppermute x1 -> x16, starting transfers between devices: 1.29 us -> 20.5 us  [the longest x15 19.2 us: exchanged(): return lax.ppermute(block, 'col', [(i, i ^ mask) for i in devices])]
  transfers between devices with their start and end apart: 5 -> 16, of which waited for: 5 -> 8; matrix products, arithmetic and copies ran while one was open for 0% -> 1% of each run, Pallas kernels for 0% -> 16%
where the time goes in v1:
time: 61.2 us; the launch traced here: 60.8 us
  starting transfers between devices  20.5 us (33%)
  waiting for transfers between devices  16.8 us (27%)
  Pallas kernels  14.3 us (23%)
  local copies, waits for them, and re-layouts  6.34 us (10%)
  between operations  1.46 us (2%)
  other arithmetic  1.38 us (2%)
    ppermute x15, starting transfers between devices, exchanged(): return lax.ppermute(block, 'col', [(i, i ^ mask) for i in devices])  19.2 us
    ppermute x15, waiting for transfers between devices, exchanged(): return lax.ppermute(block, 'col', [(i, i ^ mask) for i in devices])  16.8 us
    pallas_call x2, Pallas kernels, column_side(): pl.pallas_call(functools.partial(columns_kernel, first_mask), out_shape=[...  7.49 us
    unnamed x20, local copies, waits for them, and re-layouts  6.34 us
    pallas_call x1, Pallas kernels, shards(): pl.pallas_call(functools.partial(second_half_kernel, turns, channels, lim...  3.28 us
    pallas_call x1, Pallas kernels, shards(): pl.pallas_call(functools.partial(first_half_kernel, turns), out_shape=jax...  2.2 us
    ppermute x1, starting transfers between devices, shards(): lax.ppermute(series, 'col', [(i, i - 1) for i in range(1, devices_col)])  1.29 us
  transfers between devices with their start and end apart: 16, of which 8 were waited for; matrix products, arithmetic and copies ran while one was open for 1% of the time, Pallas kernels for 16%

profile of v1, /device:TPU:0, one launch (start us, length us, event | category | flops | bytes accessed | tf_op | source)
XLA Modules:
  0.0 60.8 jit_solution(647661100145144242)
XLA Ops:
  0.6 0.0 copy-start
  0.6 0.8 %copy-done = f32[64,256]{1,0:T(8,128)S(1)} copy-done((f32[64,256]{1,0:T(8,128)S(1)}, f32[64,256]{1,0:T(8,128)}, u32[]{:S(2)}) %copy-start) | copy-done | bytes 65560
  1.5 0.8 %copy-done.3 = s32[64,256]{1,0:T(8,128)S(1)} copy-done((s32[64,256]{1,0:T(8,128)S(1)}, s32[64,256]{1,0:T(8,128)}, u32[]{:S(2)}) %copy-start.3) | copy-done | bytes 65560
  2.3 0.7 %copy-done.6 = s32[4]{0:T(128)S(1)} copy-done((s32[4]{0:T(128)S(1)}, s32[4]{0:T(128)}, u32[]{:S(2)}) %copy-start.6) | copy-done | bytes 40
  3.0 0.7 %copy-done.8 = s32[4]{0:T(128)S(1)} copy-done((s32[4]{0:T(128)S(1)}, s32[4]{0:T(128)}, u32[]{:S(2)}) %copy-start.8) | copy-done | bytes 40
  3.6 1.0 %contributions.1 = (f32[16,1280]{1,0:T(8,128)S(1)}, f32[16,1280]{1,0:T(8,128)S(1)}, f32[16,1280]{1,0:T(8,128)S(1)}, f32[16,1280]{1,0:T(8,128)S(1)}) custom-call(s32[4]{0:T(128)S(1)} %copy-done.6, s32[4]{0:T(128)S(1)} %copy-done.8, f32[64,256]{1,0:T(8,128)S(1)} %copy-done, s32[64,256]{1,0:T(8,128)S(1)} %copy-done.3), custom_call_target="tpu_custom_call" | custom-call | tf_op jit(solution)/shard_map/contributions/pallas_call | solution.py:244
  4.7 2.5 %collective-permute-start = (f32[16,1280]{1,0:T(8,128)S(1)}, f32[16,1280]{1,0:T(8,128)S(1)}, u32[]{:S(2)}, u32[]{:S(2)}) collective-permute-start(f32[16,1280]{1,0:T(8,128)S(1)} %get-tuple-element.15), channel_id=1, source_target_pairs={{0,3},{1,2},{2,1},{3,0},{4,7},{5,6},{6,5},{7,4},{8,11},{9,10},{10,... | collective-permute-start | bytes 245768 | tf_op jit(solution)/shard_map/ppermute | solution.py:21
  7.1 0.6 %collective-permute-start.1 = (f32[16,1280]{1,0:T(8,128)S(1)}, f32[16,1280]{1,0:T(8,128)S(1)}, u32[]{:S(2)}, u32[]{:S(2)}) collective-permute-start(f32[16,1280]{1,0:T(8,128)S(1)} %get-tuple-element.16), channel_id=1, source_target_pairs={{0,2},{1,3},{2,0},{3,1},{4,6},{5,7},{6,4},{7,5},{8,10},{9,11},{10,... | collective-permute-start | bytes 245768 | tf_op jit(solution)/shard_map/ppermute | solution.py:21
  7.8 0.0 collective-permute-start.2
  7.8 2.1 %collective-permute-done = f32[16,1280]{1,0:T(8,128)S(1)} collective-permute-done((f32[16,1280]{1,0:T(8,128)S(1)}, f32[16,1280]{1,0:T(8,128)S(1)}, u32[]{:S(2)}, u32[]{:S(2)}) %collective-permute-start) | collective-permute-done | bytes 81952 | tf_op jit(solution)/shard_map/ppermute | solution.py:21
  10.0 2.2 %collective-permute-done.1 = f32[16,1280]{1,0:T(8,128)S(1)} collective-permute-done((f32[16,1280]{1,0:T(8,128)S(1)}, f32[16,1280]{1,0:T(8,128)S(1)}, u32[]{:S(2)}, u32[]{:S(2)}) %collective-permute-start.1) | collective-permute-done | bytes 81952 | tf_op jit(solution)/shard_map/ppermute | solution.py:21
  12.2 0.0 collective-permute-done.2
  12.2 2.2 %collective-permute-start.3 = (f32[16,1280]{1,0:T(8,128)S(1)}, f32[16,1280]{1,0:T(8,128)S(1)}, u32[]{:S(2)}, u32[]{:S(2)}) collective-permute-start(f32[16,1280]{1,0:T(8,128)S(1)} %add_add_fusion.refs_0_), channel_id=1, source_target_pairs={{0,4},{1,5},{2,6},{3,7},{4,0},{5,1},{6,2},{7,3},{8,12},{9,13},{10,... | collective-permute-start | bytes 245768 | tf_op jit(solution)/shard_map/ppermute | solution.py:21
  14.3 2.5 %collective-permute-start.4 = (f32[16,1280]{1,0:T(8,128)S(1)}, f32[16,1280]{1,0:T(8,128)S(1)}, u32[]{:S(2)}, u32[]{:S(2)}) collective-permute-start(f32[16,1280]{1,0:T(8,128)S(1)} %add_add_fusion.refs_0_), channel_id=1, source_target_pairs={{0,12},{1,13},{2,14},{3,15},{4,8},{5,9},{6,10},{7,11},{8,4},{9,5},... | collective-permute-start | bytes 245768 | tf_op jit(solution)/shard_map/ppermute | solution.py:21
  16.8 0.1 collective-permute-start.5
  16.9 0.8 %and_convert_fusion.band_ref = bf16[1152,128]{1,0:T(8,128)(2,1)S(1)} fusion(s32[128]{0:T(128)S(1)} %get-tuple-element.29, s32[128]{0:T(128)S(1)} %broadcast_subtract_fusion.1, s32[128]{0:T(128)S(1)} %get-tuple-element.28, s32[1152]{0:T(1024)S(1)} %get-tuple-element.27, s32[1152]{0:T(1024)S(1)} %get-tuple-element.26), kind=kLoop, calls=%fused_computation | loop fusion | flops 884736 | bytes 305664 | tf_op jit(solution)/shard_map/convert_element_type | solution.py:134
  17.7 0.0 collective-permute-done.3.refs_1_
  17.7 4.1 %collective-permute-done.4.refs_2_ = f32[16,1280]{1,0:T(8,128)S(1)} collective-permute-done((f32[16,1280]{1,0:T(8,128)S(1)}, f32[16,1280]{1,0:T(8,128)S(1)}, u32[]{:S(2)}, u32[]{:S(2)}) %collective-permute-start.4) | collective-permute-done | bytes 81952 | tf_op jit(solution)/shard_map/ppermute | solution.py:21
  21.8 2.8 %collective-permute-done.5.refs_3_ = f32[16,1280]{1,0:T(8,128)S(1)} collective-permute-done((f32[16,1280]{1,0:T(8,128)S(1)}, f32[16,1280]{1,0:T(8,128)S(1)}, u32[]{:S(2)}, u32[]{:S(2)}) %collective-permute-start.5) | collective-permute-done | bytes 81952 | tf_op jit(solution)/shard_map/ppermute | solution.py:21
  24.6 0.3 query_stats.1.ya
  24.9 0.1 collective-permute-start.9
  25.0 1.3 %collective-permute-start.8 = (f32[64,256]{1,0:T(8,128)}, f32[64,256]{1,0:T(8,128)S(1)}, u32[]{:S(2)}, u32[]{:S(2)}) collective-permute-start(f32[64,256]{1,0:T(8,128)} %x_ref.5), channel_id=1, source_target_pairs={{1,0},{2,1},{3,2},{4,3},{5,4},{6,5},{7,6},{8,7},{9,8},{10,9},{11,1... | collective-permute-start | bytes 196616 | tf_op jit(solution)/shard_map/ppermute | solution.py:241
  26.3 2.8 %collective-permute-start.6 = (f32[16,1408]{1,0:T(8,128)S(1)}, f32[16,1408]{1,0:T(8,128)S(1)}, u32[]{:S(2)}, u32[]{:S(2)}) collective-permute-start(f32[16,1408]{1,0:T(8,128)S(1)} %query_stats.1.ya), channel_id=1, source_target_pairs={{0,2},{1,3},{2,0},{3,1},{4,6},{5,7},{6,4},{7,5},{8,10},{9,11},{10,... | collective-permute-start | bytes 270344 | tf_op jit(solution)/shard_map/ppermute | solution.py:21
  29.1 0.0 collective-permute-start.7
  29.8 0.0 collective-permute-done.8.h_ref
  29.8 0.0 copy-start.1
  29.8 0.8 %copy-done.1 = f32[64,256]{1,0:T(8,128)S(1)} copy-done((f32[64,256]{1,0:T(8,128)S(1)}, f32[64,256]{1,0:T(8,128)}, u32[]{:S(2)}) %copy-start.1) | copy-done | bytes 65560
  30.6 0.8 %copy-done.4 = s32[64,256]{1,0:T(8,128)S(1)} copy-done((s32[64,256]{1,0:T(8,128)S(1)}, s32[64,256]{1,0:T(8,128)}, u32[]{:S(2)}) %copy-start.4) | copy-done | bytes 65560
  31.4 3.7 %columns.3 = (bf16[32,256,256]{2,1,0:T(8,128)(2,1)S(1)}, f32[32,256]{1,0:T(8,128)S(1)}, f32[32,256]{1,0:T(8,128)S(1)}) custom-call(f32[64,256]{1,0:T(8,128)S(1)} %copy-done.1, f32[64,256]{1,0:T(8,128)S(1)} %collective-permute-done.8.h_ref, s32[64,256]{1,0:T(8,128)S(1)} %copy-done.4), custom_call_target="tpu_custom_call" | custom-call | flops 100000000 | bytes 8388608 | tf_op jit(solution)/shard_map/columns/pallas_call | solution.py:271
  35.2 0.0 copy-start.2
  35.2 0.8 %copy-done.2 = f32[64,256]{1,0:T(8,128)S(1)} copy-done((f32[64,256]{1,0:T(8,128)S(1)}, f32[64,256]{1,0:T(8,128)}, u32[]{:S(2)}) %copy-start.2) | copy-done | bytes 65560
  36.0 0.8 %copy-done.5 = s32[64,256]{1,0:T(8,128)S(1)} copy-done((s32[64,256]{1,0:T(8,128)S(1)}, s32[64,256]{1,0:T(8,128)}, u32[]{:S(2)}) %copy-start.5) | copy-done | bytes 65560
  36.9 3.7 %columns.2 = (bf16[32,256,256]{2,1,0:T(8,128)(2,1)S(1)}, f32[32,256]{1,0:T(8,128)S(1)}, f32[32,256]{1,0:T(8,128)S(1)}) custom-call(f32[64,256]{1,0:T(8,128)S(1)} %copy-done.2, f32[64,256]{1,0:T(8,128)S(1)} %collective-permute-done.8.h_ref, s32[64,256]{1,0:T(8,128)S(1)} %copy-done.5), custom_call_target="tpu_custom_call" | custom-call | flops 100000000 | bytes 8388608 | tf_op jit(solution)/shard_map/columns/pallas_call | solution.py:271
  40.6 0.0 collective-permute-done.9.yb
  40.6 2.2 %first_half.1.so_far = f32[128,256]{1,0:T(8,128)S(1)} custom-call(f32[16,1408]{1,0:T(8,128)S(1)} %query_stats.1.ya, f32[16,1408]{1,0:T(8,128)S(1)} %collective-permute-done.9.yb, bf16[32,256,256]{2,1,0:T(8,128)(2,1)S(1)} %get-tuple-element.21.hankel, f32[32,256]{1,0:T(8,128)S(1)} %get-tuple-element.22.scale_ref, f32[32,256]{1,0:T(8,128)S(1)} %get-tuple-element.23.offset_ref), custom_call_target="tpu_custom_call" | custom-call | flops 500000000 | bytes 4194304 | tf_op jit(solution)/shard_map/first_half/pallas_call | solution.py:288
  42.9 0.0 collective-permute-done.7.yb
  42.9 3.3 %second_half.1 = (f32[4,32]{1,0:T(4,128)S(1)}, f32[1,256]{1,0:T(1,128)}) custom-call(s32[4]{0:T(128)S(1)} %copy-done.7, s32[4]{0:T(128)S(1)} %copy-done.9, s32[1]{0:T(128)S(6)} %copy.7.excl, f32[16,1408]{1,0:T(8,128)S(1)} %collective-permute-done.6.ya, f32[16,1408]{1,0:T(8,128)S(1)} %collective-permute-done.7.yb, ...), custom_call_target="tpu_custom_call" | custom-call | tf_op jit(solution)/shard_map/second_half/pallas_call | solution.py:297
  46.2 1.8 %collective-permute-start.10 = (f32[4,32]{1,0:T(4,128)S(1)}, f32[4,32]{1,0:T(4,128)S(1)}, u32[]{:S(2)}, u32[]{:S(2)}) collective-permute-start(f32[4,32]{1,0:T(4,128)S(1)} %get-tuple-element.24), channel_id=1, source_target_pairs={{0,1},{1,0},{2,3},{3,2},{4,5},{5,4},{6,7},{7,6},{8,9},{9,8},{10,11... | collective-permute-start | bytes 1544 | tf_op jit(solution)/shard_map/ppermute | solution.py:21
  48.0 2.2 %collective-permute-start.11 = (f32[4,32]{1,0:T(4,128)S(1)}, f32[4,32]{1,0:T(4,128)S(1)}, u32[]{:S(2)}, u32[]{:S(2)}) collective-permute-start(f32[4,32]{1,0:T(4,128)S(1)} %get-tuple-element.24), channel_id=1, source_target_pairs={{0,2},{1,3},{2,0},{3,1},{4,6},{5,7},{6,4},{7,5},{8,10},{9,11},{10,... | collective-permute-start | bytes 1544 | tf_op jit(solution)/shard_map/ppermute | solution.py:21
  50.2 0.0 collective-permute-start.12
  50.2 0.0 collective-permute-done.10
  50.2 1.6 %collective-permute-done.11 = f32[4,32]{1,0:T(4,128)S(1)} collective-permute-done((f32[4,32]{1,0:T(4,128)S(1)}, f32[4,32]{1,0:T(4,128)S(1)}, u32[]{:S(2)}, u32[]{:S(2)}) %collective-permute-start.11) | collective-permute-done | bytes 544 | tf_op jit(solution)/shard_map/ppermute | solution.py:21
  51.8 1.4 %collective-permute-done.12 = f32[4,32]{1,0:T(4,128)S(1)} collective-permute-done((f32[4,32]{1,0:T(4,128)S(1)}, f32[4,32]{1,0:T(4,128)S(1)}, u32[]{:S(2)}, u32[]{:S(2)}) %collective-permute-start.12) | collective-permute-done | bytes 544 | tf_op jit(solution)/shard_map/ppermute | solution.py:21
  53.2 1.6 %collective-permute-start.14 = (f32[4,32]{1,0:T(4,128)S(1)}, f32[4,32]{1,0:T(4,128)S(1)}, u32[]{:S(2)}, u32[]{:S(2)}) collective-permute-start(f32[4,32]{1,0:T(4,128)S(1)} %minimum_minimum_fusion.1), channel_id=1, source_target_pairs={{0,8},{1,9},{2,10},{3,11},{4,12},{5,13},{6,14},{7,15},{8,0},{9,1},... | collective-permute-start | bytes 1544 | tf_op jit(solution)/shard_map/ppermute | solution.py:21
  54.8 2.8 %collective-permute-start.15 = (f32[4,32]{1,0:T(4,128)S(1)}, f32[4,32]{1,0:T(4,128)S(1)}, u32[]{:S(2)}, u32[]{:S(2)}) collective-permute-start(f32[4,32]{1,0:T(4,128)S(1)} %minimum_minimum_fusion.1), channel_id=1, source_target_pairs={{0,12},{1,13},{2,14},{3,15},{4,8},{5,9},{6,10},{7,11},{8,4},{9,5},... | collective-permute-start | bytes 1544 | tf_op jit(solution)/shard_map/ppermute | solution.py:21
  57.6 0.2 collective-permute-done.14
  57.8 2.4 %collective-permute-done.15 = f32[4,32]{1,0:T(4,128)S(1)} collective-permute-done((f32[4,32]{1,0:T(4,128)S(1)}, f32[4,32]{1,0:T(4,128)S(1)}, u32[]{:S(2)}, u32[]{:S(2)}) %collective-permute-start.15) | collective-permute-done | bytes 544 | tf_op jit(solution)/shard_map/ppermute | solution.py:21
  60.2 0.6 minimum_minimum_fusion
  (17 shorter events, 0.1 us)
Async XLA Ops:
  0.6 0.8 %copy-start = (f32[64,256]{1,0:T(8,128)S(1)}, f32[64,256]{1,0:T(8,128)}, u32[]{:S(2)}) copy-start(f32[64,256]{1,0:T(8,128)} %x_ref.5) | copy-start | bytes 196612
  1.5 0.8 %copy-start.3 = (s32[64,256]{1,0:T(8,128)S(1)}, s32[64,256]{1,0:T(8,128)}, u32[]{:S(2)}) copy-start(s32[64,256]{1,0:T(8,128)} %v_ref.5) | copy-start | bytes 196612
  2.3 0.7 %copy-start.6 = (s32[4]{0:T(128)S(1)}, s32[4]{0:T(128)}, u32[]{:S(2)}) copy-start(s32[4]{0:T(128)} %owners.3) | copy-start | bytes 52
  3.0 0.7 %copy-start.8 = (s32[4]{0:T(128)S(1)}, s32[4]{0:T(128)}, u32[]{:S(2)}) copy-start(s32[4]{0:T(128)} %blocks.3) | copy-start | bytes 52
  3.6 39.3 %copy-start.7 = (s32[4]{0:T(128)S(1)}, s32[4]{0:T(128)}, u32[]{:S(2)}) copy-start(s32[4]{0:T(128)} %owners.3) | copy-start | bytes 52
  3.6 39.3 %copy-start.9 = (s32[4]{0:T(128)S(1)}, s32[4]{0:T(128)}, u32[]{:S(2)}) copy-start(s32[4]{0:T(128)} %blocks.3) | copy-start | bytes 52
  4.7 5.3 %collective-permute-start = (f32[16,1280]{1,0:T(8,128)S(1)}, f32[16,1280]{1,0:T(8,128)S(1)}, u32[]{:S(2)}, u32[]{:S(2)}) collective-permute-start(f32[16,1280]{1,0:T(8,128)S(1)} %get-tuple-element.15), channel_id=1, source_target_pairs={{0,3},{1,2},{2,1},{3,0},{4,7},{5,6},{6,5},{7,4},{8,11},{9,10},{10,... | collective-permute-start | bytes 245768 | tf_op jit(solution)/shard_map/ppermute | solution.py:21
  7.1 5.0 %collective-permute-start.1 = (f32[16,1280]{1,0:T(8,128)S(1)}, f32[16,1280]{1,0:T(8,128)S(1)}, u32[]{:S(2)}, u32[]{:S(2)}) collective-permute-start(f32[16,1280]{1,0:T(8,128)S(1)} %get-tuple-element.16), channel_id=1, source_target_pairs={{0,2},{1,3},{2,0},{3,1},{4,6},{5,7},{6,4},{7,5},{8,10},{9,11},{10,... | collective-permute-start | bytes 245768 | tf_op jit(solution)/shard_map/ppermute | solution.py:21
  7.8 4.4 %collective-permute-start.2 = (f32[16,1280]{1,0:T(8,128)S(1)}, f32[16,1280]{1,0:T(8,128)S(1)}, u32[]{:S(2)}, u32[]{:S(2)}) collective-permute-start(f32[16,1280]{1,0:T(8,128)S(1)} %get-tuple-element.17), channel_id=1, source_target_pairs={{0,1},{1,0},{2,3},{3,2},{4,5},{5,4},{6,7},{7,6},{8,9},{9,8},{10,11... | collective-permute-start | bytes 245768 | tf_op jit(solution)/shard_map/ppermute | solution.py:21
  12.2 5.5 %collective-permute-start.3 = (f32[16,1280]{1,0:T(8,128)S(1)}, f32[16,1280]{1,0:T(8,128)S(1)}, u32[]{:S(2)}, u32[]{:S(2)}) collective-permute-start(f32[16,1280]{1,0:T(8,128)S(1)} %add_add_fusion.refs_0_), channel_id=1, source_target_pairs={{0,4},{1,5},{2,6},{3,7},{4,0},{5,1},{6,2},{7,3},{8,12},{9,13},{10,... | collective-permute-start | bytes 245768 | tf_op jit(solution)/shard_map/ppermute | solution.py:21
  14.3 7.5 %collective-permute-start.4 = (f32[16,1280]{1,0:T(8,128)S(1)}, f32[16,1280]{1,0:T(8,128)S(1)}, u32[]{:S(2)}, u32[]{:S(2)}) collective-permute-start(f32[16,1280]{1,0:T(8,128)S(1)} %add_add_fusion.refs_0_), channel_id=1, source_target_pairs={{0,12},{1,13},{2,14},{3,15},{4,8},{5,9},{6,10},{7,11},{8,4},{9,5},... | collective-permute-start | bytes 245768 | tf_op jit(solution)/shard_map/ppermute | solution.py:21
  16.8 7.8 %collective-permute-start.5 = (f32[16,1280]{1,0:T(8,128)S(1)}, f32[16,1280]{1,0:T(8,128)S(1)}, u32[]{:S(2)}, u32[]{:S(2)}) collective-permute-start(f32[16,1280]{1,0:T(8,128)S(1)} %add_add_fusion.refs_0_), channel_id=1, source_target_pairs={{0,8},{1,9},{2,10},{3,11},{4,12},{5,13},{6,14},{7,15},{8,0},{9,1},... | collective-permute-start | bytes 245768 | tf_op jit(solution)/shard_map/ppermute | solution.py:21
  24.9 15.7 %collective-permute-start.9 = (f32[16,1408]{1,0:T(8,128)S(1)}, f32[16,1408]{1,0:T(8,128)S(1)}, u32[]{:S(2)}, u32[]{:S(2)}) collective-permute-start(f32[16,1408]{1,0:T(8,128)S(1)} %query_stats.1.ya), channel_id=1, source_target_pairs={{0,1},{1,0},{2,3},{3,2},{4,5},{5,4},{6,7},{7,6},{8,9},{9,8},{10,11... | collective-permute-start | bytes 270344 | tf_op jit(solution)/shard_map/ppermute | solution.py:21
  25.0 4.8 %collective-permute-start.8 = (f32[64,256]{1,0:T(8,128)}, f32[64,256]{1,0:T(8,128)S(1)}, u32[]{:S(2)}, u32[]{:S(2)}) collective-permute-start(f32[64,256]{1,0:T(8,128)} %x_ref.5), channel_id=1, source_target_pairs={{1,0},{2,1},{3,2},{4,3},{5,4},{6,5},{7,6},{8,7},{9,8},{10,9},{11,1... | collective-permute-start | bytes 196616 | tf_op jit(solution)/shard_map/ppermute | solution.py:241
  26.3 16.6 %collective-permute-start.6 = (f32[16,1408]{1,0:T(8,128)S(1)}, f32[16,1408]{1,0:T(8,128)S(1)}, u32[]{:S(2)}, u32[]{:S(2)}) collective-permute-start(f32[16,1408]{1,0:T(8,128)S(1)} %query_stats.1.ya), channel_id=1, source_target_pairs={{0,2},{1,3},{2,0},{3,1},{4,6},{5,7},{6,4},{7,5},{8,10},{9,11},{10,... | collective-permute-start | bytes 270344 | tf_op jit(solution)/shard_map/ppermute | solution.py:21
  29.1 13.8 %collective-permute-start.7 = (f32[16,1408]{1,0:T(8,128)S(1)}, f32[16,1408]{1,0:T(8,128)S(1)}, u32[]{:S(2)}, u32[]{:S(2)}) collective-permute-start(f32[16,1408]{1,0:T(8,128)S(1)} %query_stats.1.ya), channel_id=1, source_target_pairs={{0,3},{1,2},{2,1},{3,0},{4,7},{5,6},{6,5},{7,4},{8,11},{9,10},{10,... | collective-permute-start | bytes 270344 | tf_op jit(solution)/shard_map/ppermute | solution.py:21
  29.8 0.8 %copy-start.1 = (f32[64,256]{1,0:T(8,128)S(1)}, f32[64,256]{1,0:T(8,128)}, u32[]{:S(2)}) copy-start(f32[64,256]{1,0:T(8,128)} %x_ref.5) | copy-start | bytes 196612
  30.6 0.8 %copy-start.4 = (s32[64,256]{1,0:T(8,128)S(1)}, s32[64,256]{1,0:T(8,128)}, u32[]{:S(2)}) copy-start(s32[64,256]{1,0:T(8,128)} %v_ref.5) | copy-start | bytes 196612
  35.2 0.8 %copy-start.2 = (f32[64,256]{1,0:T(8,128)S(1)}, f32[64,256]{1,0:T(8,128)}, u32[]{:S(2)}) copy-start(f32[64,256]{1,0:T(8,128)} %x_ref.5) | copy-start | bytes 196612
  36.0 0.8 %copy-start.5 = (s32[64,256]{1,0:T(8,128)S(1)}, s32[64,256]{1,0:T(8,128)}, u32[]{:S(2)}) copy-start(s32[64,256]{1,0:T(8,128)} %v_ref.5) | copy-start | bytes 196612
  46.2 4.1 %collective-permute-start.10 = (f32[4,32]{1,0:T(4,128)S(1)}, f32[4,32]{1,0:T(4,128)S(1)}, u32[]{:S(2)}, u32[]{:S(2)}) collective-permute-start(f32[4,32]{1,0:T(4,128)S(1)} %get-tuple-element.24), channel_id=1, source_target_pairs={{0,1},{1,0},{2,3},{3,2},{4,5},{5,4},{6,7},{7,6},{8,9},{9,8},{10,11... | collective-permute-start | bytes 1544 | tf_op jit(solution)/shard_map/ppermute | solution.py:21
  48.0 3.8 %collective-permute-start.11 = (f32[4,32]{1,0:T(4,128)S(1)}, f32[4,32]{1,0:T(4,128)S(1)}, u32[]{:S(2)}, u32[]{:S(2)}) collective-permute-start(f32[4,32]{1,0:T(4,128)S(1)} %get-tuple-element.24), channel_id=1, source_target_pairs={{0,2},{1,3},{2,0},{3,1},{4,6},{5,7},{6,4},{7,5},{8,10},{9,11},{10,... | collective-permute-start | bytes 1544 | tf_op jit(solution)/shard_map/ppermute | solution.py:21
  50.2 3.0 %collective-permute-start.12 = (f32[4,32]{1,0:T(4,128)S(1)}, f32[4,32]{1,0:T(4,128)S(1)}, u32[]{:S(2)}, u32[]{:S(2)}) collective-permute-start(f32[4,32]{1,0:T(4,128)S(1)} %get-tuple-element.24), channel_id=1, source_target_pairs={{0,3},{1,2},{2,1},{3,0},{4,7},{5,6},{6,5},{7,4},{8,11},{9,10},{10,... | collective-permute-start | bytes 1544 | tf_op jit(solution)/shard_map/ppermute | solution.py:21
  53.2 4.4 %collective-permute-start.13 = (f32[4,32]{1,0:T(4,128)S(1)}, f32[4,32]{1,0:T(4,128)S(1)}, u32[]{:S(2)}, u32[]{:S(2)}) collective-permute-start(f32[4,32]{1,0:T(4,128)S(1)} %minimum_minimum_fusion.1), channel_id=1, source_target_pairs={{0,4},{1,5},{2,6},{3,7},{4,0},{5,1},{6,2},{7,3},{8,12},{9,13},{10,... | collective-permute-start | bytes 1544 | tf_op jit(solution)/shard_map/ppermute | solution.py:21
  53.2 4.5 %collective-permute-start.14 = (f32[4,32]{1,0:T(4,128)S(1)}, f32[4,32]{1,0:T(4,128)S(1)}, u32[]{:S(2)}, u32[]{:S(2)}) collective-permute-start(f32[4,32]{1,0:T(4,128)S(1)} %minimum_minimum_fusion.1), channel_id=1, source_target_pairs={{0,8},{1,9},{2,10},{3,11},{4,12},{5,13},{6,14},{7,15},{8,0},{9,1},... | collective-permute-start | bytes 1544 | tf_op jit(solution)/shard_map/ppermute | solution.py:21
  54.8 5.4 %collective-permute-start.15 = (f32[4,32]{1,0:T(4,128)S(1)}, f32[4,32]{1,0:T(4,128)S(1)}, u32[]{:S(2)}, u32[]{:S(2)}) collective-permute-start(f32[4,32]{1,0:T(4,128)S(1)} %minimum_minimum_fusion.1), channel_id=1, source_target_pairs={{0,12},{1,13},{2,14},{3,15},{4,8},{5,9},{6,10},{7,11},{8,4},{9,5},... | collective-permute-start | bytes 1544 | tf_op jit(solution)/shard_map/ppermute | solution.py:21

commit v2 on v1

--- a/solution.py
+++ b/solution.py
@@ -38,50 +38,68 @@
     return high, mid, low
 
 
-def contributions_kernel(owners, blocks, x_ref, v_ref, *outs):
+def share_kernel(packed, samples, flags, *outs):
+    width = samples.shape[1]
+    quarter = packed.shape[0] // GROUP
+    member = lax.rem(lax.axis_index("col"), GROUP)
+    samples[...] = packed[:, :width]
+    flags[...] = packed[:, width:]
+    for mask, out in enumerate(outs):
+        out[...] = packed[pl.ds(pl.multiple_of((member ^ mask) * quarter, quarter), quarter), :]
+
+
+def windows_kernel(owners, blocks, after, *refs):
+    parts, out = refs[:GROUP], refs[GROUP]
     turns = owners.shape[0]
-    quarter = x_ref.shape[0] // GROUP
-    width = x_ref.shape[1]
+    quarter, width = parts[0].shape[0], parts[0].shape[1] // 2
     here = lax.axis_index("col")
-    member = lax.rem(here, GROUP)
     row = lax.broadcasted_iota(jnp.int32, (width, width), 0)
     col = lax.broadcasted_iota(jnp.int32, (width, width), 1)
     flip = (row + col == width - 1).astype(bf16)
+    stack = jnp.concatenate([piece for part in parts for piece in split3(part[:, :width])], axis=0)
+    turned = jnp.dot(stack, flip, preferred_element_type=f32)
+    lines = []
+    for i in range(GROUP):
+        high, mid, low = (turned[(3 * i + j) * quarter : (3 * i + j + 1) * quarter] for j in range(3))
+        lines.append(low + mid + high)
     lane = lax.broadcasted_iota(jnp.int32, (quarter, width), 1)
     lane_128 = lax.broadcasted_iota(jnp.int32, (quarter, LANES), 1)
     per_tile = LANES // QB
-    for mask, out in enumerate(outs):
-        rows = pl.ds(pl.multiple_of((member ^ mask) * quarter, quarter), quarter)
-        pieces = split3(x_ref[rows, :])
-        turned = sum(jnp.dot(p, flip, preferred_element_type=f32) for p in reversed(pieces))
-        flags = v_ref[rows, :].astype(f32)
-        for tile in range(turns // per_tile):
-            tails = jnp.zeros((quarter, LANES), f32)
-            valids = jnp.zeros((quarter, LANES), f32)
-            for i in range(per_tile):
-                turn = tile * per_tile + i
-                shift = blocks[turn] * QB
-                mine = owners[turn] == here
-                after = owners[turn] + 1 == here
-                rolled = pltpu.roll(turned, lax.rem(shift + QB, width), 1)
-                split = shift + QB
-                keep = jnp.where(lane >= split, mine.astype(jnp.int32), after.astype(jnp.int32)) == 1
-                out[:, turn * M : (turn + 1) * M] = jnp.where(keep, rolled, 0.0)
-                there = (lane_128 >= i * QB) & (lane_128 < (i + 1) * QB) & (mine.astype(jnp.int32) == 1)
-                tail = rolled[:, :LANES]
-                flag = pltpu.roll(flags, lax.rem(width - shift, width), 1)[:, :LANES]
-                if i:
-                    tail = pltpu.roll(tail, i * QB, 1)
-                    flag = pltpu.roll(flag, i * QB, 1)
-                tails = jnp.where(there, tail, tails)
-                valids = jnp.where(there, flag, valids)
-            at = turns * M + tile * LANES
-            out[:, at : at + LANES] = tails
-            at = turns * (M + QB) + tile * LANES
-            out[:, at : at + LANES] = valids
-
-
-def query_kernel(turns, band_ref, *refs):
+    for tile in range(turns // per_tile):
+        tails = jnp.zeros((quarter, LANES), f32)
+        valids = jnp.zeros((quarter, LANES), f32)
+        for i in range(per_tile):
+            turn = tile * per_tile + i
+            shift = blocks[turn] * QB
+            split = shift + QB
+            first = jnp.zeros((quarter, width), f32)
+            second = jnp.zeros((quarter, width), f32)
+            flags = jnp.zeros((quarter, width), f32)
+            for mask, part in enumerate(parts):
+                mine = (owners[turn] == here ^ mask).astype(f32)
+                after_mine = (owners[turn] + 1 == here ^ mask).astype(f32)
+                first = first + mine * lines[mask]
+                second = second + after_mine * lines[mask]
+                flags = flags + mine * part[:, width:]
+            amount = lax.rem(split, width)
+            first = pltpu.roll(first, amount, 1)
+            second = pltpu.roll(second, amount, 1)
+            flags = pltpu.roll(flags, lax.rem(width - shift, width), 1)
+            out[:, turn * M : (turn + 1) * M] = jnp.where(lane >= split, first, second)
+            tail, flag = first[:, :LANES], flags[:, :LANES]
+            if i:
+                tail = pltpu.roll(tail, i * QB, 1)
+                flag = pltpu.roll(flag, i * QB, 1)
+            there = (lane_128 >= i * QB) & (lane_128 < (i + 1) * QB)
+            tails = jnp.where(there, tail, tails)
+            valids = jnp.where(there, flag, valids)
+        at = turns * M + tile * LANES
+        out[:, at : at + LANES] = tails
+        at = turns * (M + QB) + tile * LANES
+        out[:, at : at + LANES] = valids
+
+
+def query_kernel(turns, after, band_ref, *refs):
     parts, out = refs[:-1], refs[-1]
     total = parts[0][...]
     for part in parts[1:]:
@@ -122,22 +140,24 @@
         out[:, at : at + LANES] = tail[tile]
 
 
-def band_matrix():
+def band_matrix(shape):
+    lane = lax.broadcasted_iota(jnp.int32, shape, 0)
+    query = lax.broadcasted_iota(jnp.int32, shape, 1)
     per_tile = LANES // QB
-    query = jnp.arange(LANES)
-    lane = jnp.arange(per_tile * (M + QB))
-    in_main = lane < per_tile * M
-    turn = jnp.where(in_main, lane // M, (lane - per_tile * M) // QB)
-    place = jnp.where(in_main, lane % M, M + (lane - per_tile * M) % QB)
+    beyond = lane - per_tile * M
+    turn = jnp.where(beyond < 0, lane // M, beyond // QB)
+    place = jnp.where(beyond < 0, lane % M, M + beyond % QB)
     q = query % QB
-    inside = (place[:, None] >= QB - q[None, :]) & (place[:, None] <= M + QB - 1 - q[None, :])
-    return ((turn[:, None] == query[None, :] // QB) & inside).astype(bf16)
-
-
-def columns_kernel(first_mask, x_ref, h_ref, v_ref, hankel, scale_ref, offset_ref):
+    inside = (turn == query // QB) & (place >= QB - q) & (place <= M + QB - 1 - q)
+    return jnp.where(inside, 1.0, 0.0).astype(bf16)
+
+
+def columns_kernel(first_mask, x_ref, h_ref, v_ref, hankel, scale_ref, offset_ref, *band_ref):
     quarter = x_ref.shape[0] // GROUP
     width = x_ref.shape[1]
     member = lax.rem(lax.axis_index("col"), GROUP)
+    for ref in band_ref:
+        ref[...] = band_matrix(ref.shape)
     for piece in range(2):
         rows = pl.ds(pl.multiple_of((member ^ (first_mask + piece)) * quarter, quarter), quarter)
         own = x_ref[rows, :]
@@ -152,7 +172,7 @@
             step *= 2
         mean = first[:, :width] * (1.0 / M)
         spread = second[:, :width] * (1.0 / M) - mean * mean
-        scale = v_ref[rows, :].astype(f32) / jnp.sqrt(jnp.maximum(spread, 0.0) + 1e-05)
+        scale = v_ref[rows, :] / jnp.sqrt(jnp.maximum(spread, 0.0) + 1e-05)
         into = slice(piece * quarter, (piece + 1) * quarter)
         scale_ref[into, :] = scale
         offset_ref[into, :] = mean * scale
@@ -165,12 +185,12 @@
                 hankel[piece * quarter + c, 16 * b : 16 * (b + 1), :] = block[:, :width]
 
 
-def partial_sum(turns, pieces, hankel, scale_ref, offset_ref, acc):
+def partial_sum(turns, pieces, held_at, hankel, scale_ref, offset_ref, acc):
     queries = turns * QB
     samples = turns * (M + QB)
     per_tile = LANES // QB
     quarter = pieces[0].shape[0]
-    for index, piece in enumerate(pieces):
+    for index, piece in enumerate(pieces, held_at):
         by_query = jnp.transpose(piece[:, samples : samples + queries])
         offsets = jnp.transpose(piece[:, samples + queries : samples + 2 * queries])
         lines = []
@@ -196,15 +216,19 @@
     return acc
 
 
-def first_half_kernel(turns, ya, yb, hankel, scale_ref, offset_ref, out):
+def first_kernel(turns, ya, yb, hankel, scale_ref, offset_ref, out):
     zero = jnp.zeros(out.shape, f32)
-    out[...] = partial_sum(turns, (ya, yb), hankel, scale_ref, offset_ref, zero)
-
-
-def second_half_kernel(
-    turns, channels, limit, owners, blocks, excl, ya, yb, hankel, scale_ref, offset_ref, so_far, row_out, col_out
+    out[...] = partial_sum(turns, (ya, yb), 0, hankel, scale_ref, offset_ref, zero)
+
+
+def next_kernel(turns, y, hankel, scale_ref, offset_ref, so_far, out):
+    out[...] = partial_sum(turns, (y,), 0, hankel, scale_ref, offset_ref, so_far[...])
+
+
+def last_kernel(
+    turns, channels, limit, owners, blocks, excl, y, hankel, scale_ref, offset_ref, so_far, row_out, col_out
 ):
-    summed = partial_sum(turns, (ya, yb), hankel, scale_ref, offset_ref, so_far[...])
+    summed = partial_sum(turns, (y,), 1, hankel, scale_ref, offset_ref, so_far[...])
     distance = 1.0 - summed * (1.0 / (M * channels))
     width = distance.shape[1]
     columns = lax.axis_index("col") * width + lax.broadcasted_iota(jnp.int32, (QB, width), 1)
@@ -227,6 +251,7 @@
 
 VMEM = pl.BlockSpec(memory_space=pltpu.VMEM)
 SMEM = pl.BlockSpec(memory_space=pltpu.SMEM)
+ANY = pl.BlockSpec(memory_space=pl.ANY)
 PARAMS = pltpu.CompilerParams(vmem_limit_bytes=40 * 2**20)
 
 
@@ -238,72 +263,92 @@
     queries = turns * QB
     limit = seg_len * devices_col - M
 
-    following = lax.ppermute(series, "col", [(i, i - 1) for i in range(1, devices_col)])
-
-    share = jax.ShapeDtypeStruct((quarter, turns * (M + 2 * QB)), f32)
-    shares = pl.pallas_call(
-        contributions_kernel,
-        out_shape=[share] * GROUP,
-        in_specs=[SMEM, SMEM, VMEM, VMEM],
-        out_specs=[VMEM] * GROUP,
-        compiler_params=PARAMS,
-        name="contributions",
-    )(owners, blocks, series, valid)
-    arrived = [exchanged(shares[mask], mask) for mask in (3, 2, 1)]
-    total = shares[0] + arrived[0] + arrived[1] + arrived[2]
-
-    rounds = rounds_beyond_group(devices_col)
-    for masks in rounds[:-1]:
-        total = sum([exchanged(total, mask) for mask in masks], total)
-    order = (0, 2, 1) if len(rounds[-1]) == 3 else (0,)
-    parts = [total] + [exchanged(total, rounds[-1][i]) for i in order]
-    query = jax.ShapeDtypeStruct((quarter, turns * (M + 3 * QB)), f32)
-    mine = pl.pallas_call(
-        functools.partial(query_kernel, turns),
-        out_shape=query,
-        in_specs=[VMEM] * (1 + len(parts)),
-        out_specs=VMEM,
-        compiler_params=PARAMS,
-        name="query_stats",
-    )(band_matrix(), *parts)
-
-    def column_side(first_mask):
+    packed = jnp.concatenate([series, valid.astype(f32)], axis=1)
+    segment = jax.ShapeDtypeStruct(series.shape, f32)
+    part = jax.ShapeDtypeStruct((quarter, 2 * seg_len), f32)
+    samples, flags, *shares = pl.pallas_call(
+        share_kernel,
+        out_shape=[segment] * 2 + [part] * GROUP,
+        in_specs=[VMEM],
+        out_specs=[VMEM] * (2 + GROUP),
+        compiler_params=PARAMS,
+        name="share",
+    )(packed)
+    arrived = {mask: exchanged(shares[mask], mask) for mask in (3, 2, 1)}
+    following = lax.ppermute(samples, "col", [(i, i - 1) for i in range(1, devices_col)])
+
+    def column_side(first_mask, *band):
         return pl.pallas_call(
             functools.partial(columns_kernel, first_mask),
             out_shape=[
                 jax.ShapeDtypeStruct((2 * quarter, M, seg_len), bf16),
                 jax.ShapeDtypeStruct((2 * quarter, seg_len), f32),
                 jax.ShapeDtypeStruct((2 * quarter, seg_len), f32),
+                *band,
             ],
             in_specs=[VMEM] * 3,
-            out_specs=[VMEM] * 3,
+            out_specs=[VMEM] * (3 + len(band)),
             compiler_params=PARAMS,
             cost_estimate=pl.CostEstimate(flops=10**8, bytes_accessed=8 * 2**20, transcendentals=0),
             name="columns",
-        )(series, following, valid)
-
-    sides = column_side(0), column_side(2)
+        )(samples, following, flags)
+
+    *near, band = column_side(0, jax.ShapeDtypeStruct((LANES // QB * (M + QB), LANES), bf16))
+    total = pl.pallas_call(
+        windows_kernel,
+        out_shape=jax.ShapeDtypeStruct((quarter, turns * (M + 2 * QB)), f32),
+        in_specs=[SMEM] * 2 + [ANY] + [VMEM] * GROUP,
+        out_specs=VMEM,
+        compiler_params=PARAMS,
+        name="windows",
+    )(owners, blocks, near[1], shares[0], arrived[1], arrived[2], arrived[3])
+
+    rounds = rounds_beyond_group(devices_col)
+    for masks in rounds[:-1]:
+        total = sum([exchanged(total, mask) for mask in masks], total)
+    order = (0, 2, 1) if len(rounds[-1]) == 3 else (0,)
+    parts = [total] + [exchanged(total, rounds[-1][i]) for i in order]
+    far = column_side(2)
+    mine = pl.pallas_call(
+        functools.partial(query_kernel, turns),
+        out_shape=jax.ShapeDtypeStruct((quarter, turns * (M + 3 * QB)), f32),
+        in_specs=[ANY] + [VMEM] * (1 + len(parts)),
+        out_specs=VMEM,
+        compiler_params=PARAMS,
+        name="query_stats",
+    )(far[1], band, *parts)
     others = {mask: exchanged(mine, mask) for mask in (3, 2, 1)}
 
-    half = pl.pallas_call(
-        functools.partial(first_half_kernel, turns),
-        out_shape=jax.ShapeDtypeStruct((queries, seg_len), f32),
+    partial = jax.ShapeDtypeStruct((queries, seg_len), f32)
+    summed = pl.pallas_call(
+        functools.partial(first_kernel, turns),
+        out_shape=partial,
         in_specs=[VMEM] * 5,
         out_specs=VMEM,
         compiler_params=PARAMS,
         cost_estimate=pl.CostEstimate(flops=5 * 10**8, bytes_accessed=4 * 2**20, transcendentals=0),
-        name="first_half",
-    )(mine, others[1], *sides[0])
+        name="first_two",
+    )(mine, others[1], *near)
+    summed = pl.pallas_call(
+        functools.partial(next_kernel, turns),
+        out_shape=partial,
+        in_specs=[VMEM] * 5,
+        out_specs=VMEM,
+        compiler_params=PARAMS,
+        cost_estimate=pl.CostEstimate(flops=2 * 10**8, bytes_accessed=2 * 2**20, transcendentals=0),
+        name="third",
+    )(others[2], *far, summed)
     rows, column = pl.pallas_call(
-        functools.partial(second_half_kernel, turns, channels, limit),
+        functools.partial(last_kernel, turns, channels, limit),
         out_shape=[jax.ShapeDtypeStruct((turns, QB), f32), jax.ShapeDtypeStruct((1, seg_len), f32)],
-        in_specs=[SMEM] * 3 + [VMEM] * 6,
+        in_specs=[SMEM] * 3 + [VMEM] * 5,
         out_specs=[VMEM] * 2,
         compiler_params=PARAMS,
-        name="second_half",
-    )(owners, blocks, excl, others[2], others[3], *sides[1], half)
-
-    for masks in [[1, 2, 3], *rounds]:
+        name="fourth",
+    )(owners, blocks, excl, others[3], *far, summed)
+
+    small = [[masks[0] + 1, *(m + 1 for m in reversed(masks[1:]))] for masks in rounds]
+    for masks in [[1, 2, 3], *small]:
         rows = functools.reduce(jnp.minimum, [exchanged(rows, mask) for mask in masks], rows)
     return (rows, column.reshape(seg_len))
 

time: 61.2 us -> 47.4 us (0.77)
  the two profiles are of different devices: /device:TPU:0 before, /device:TPU:1 now
where the time goes in v2:
time: 47.4 us; the launch traced here: 47.1 us
  starting transfers between devices  17.4 us (37%)
  Pallas kernels  14.5 us (31%)
  waiting for transfers between devices  10.2 us (22%)
  other arithmetic  2.28 us (5%)
  between operations  1.43 us (3%)
  local copies, waits for them, and re-layouts  1.32 us (3%)
    ppermute x15, starting transfers between devices, exchanged(): return lax.ppermute(block, 'col', [(i, i ^ mask) for i in devices])  15.4 us
    ppermute x15, waiting for transfers between devices, exchanged(): return lax.ppermute(block, 'col', [(i, i ^ mask) for i in devices])  8.54 us
    pallas_call x2, Pallas kernels, column_side(): pl.pallas_call(functools.partial(columns_kernel, first_mask), out_shape=[...  7.58 us
    pallas_call x1, Pallas kernels, shards(): pl.pallas_call(functools.partial(first_kernel, turns), out_shape=partial,...  2.28 us
    pallas_call x1, Pallas kernels, shards(): pl.pallas_call(functools.partial(last_kernel, turns, channels, limit), ou...  2.26 us
    ppermute x1, starting transfers between devices, shards(): lax.ppermute(samples, 'col', [(i, i - 1) for i in range(1, devices_col)])  1.97 us
    ppermute x1, waiting for transfers between devices, shards(): lax.ppermute(samples, 'col', [(i, i - 1) for i in range(1, devices_col)])  1.66 us
    unnamed x8, local copies, waits for them, and re-layouts  1.32 us
  transfers between devices with their start and end apart: 16, of which 8 were waited for; matrix products, arithmetic and copies ran while one was open for 0% of the time, Pallas kernels for 23%

profile of v2, /device:TPU:1, one launch (start us, length us, event | category | flops | bytes accessed | tf_op | source)
XLA Modules:
  0.0 47.1 jit_solution(18065965048126389953)
XLA Ops:
  0.6 0.8 %convert_element_type.3 = f32[64,256]{1,0:T(8,128)S(1)} convert(s32[64,256]{1,0:T(8,128)} %param.6) | non-fusion elementwise | flops 16384 | bytes 131072 | tf_op jit(solution)/shard_map/convert_element_type | solution.py:266
  1.5 0.8 %pad_maximum_fusion.packed = f32[64,512]{1,0:T(8,128)S(1)} fusion(f32[64,256]{1,0:T(8,128)S(1)} %convert_element_type.3, f32[64,256]{1,0:T(8,128)} %param.5), kind=kLoop, calls=%fused_computation | loop fusion | flops 32768 | bytes 262144 | tf_op jit(solution)/shard_map/concatenate | solution.py:266
  2.4 2.0 %collective-permute-start = (f32[64,256]{1,0:T(8,128)S(1)}, f32[64,256]{1,0:T(8,128)S(1)}, u32[]{:S(2)}, u32[]{:S(2)}) collective-permute-start(f32[64,256]{1,0:T(8,128)S(1)} %get-tuple-element.17.x_ref), channel_id=1, source_target_pairs={{1,0},{2,1},{3,2},{4,3},{5,4},{6,5},{7,6},{8,7},{9,8},{10,9},{11,1... | collective-permute-start | bytes 196616 | tf_op jit(solution)/shard_map/ppermute | solution.py:278
  4.3 0.1 collective-permute-start.1
  4.4 2.8 %collective-permute-start.2 = (f32[16,512]{1,0:T(8,128)S(1)}, f32[16,512]{1,0:T(8,128)S(1)}, u32[]{:S(2)}, u32[]{:S(2)}) collective-permute-start(f32[16,512]{1,0:T(8,128)S(1)} %get-tuple-element.24), channel_id=1, source_target_pairs={{0,2},{1,3},{2,0},{3,1},{4,6},{5,7},{6,4},{7,5},{8,10},{9,11},{10,... | collective-permute-start | bytes 98312 | tf_op jit(solution)/shard_map/ppermute | solution.py:21
  7.2 0.3 collective-permute-start.3
  7.5 1.7 %collective-permute-done.h_ref = f32[64,256]{1,0:T(8,128)S(1)} collective-permute-done((f32[64,256]{1,0:T(8,128)S(1)}, f32[64,256]{1,0:T(8,128)S(1)}, u32[]{:S(2)}, u32[]{:S(2)}) %collective-permute-start) | collective-permute-done | bytes 65568 | tf_op jit(solution)/shard_map/ppermute | solution.py:278
  9.2 3.8 %columns.3 = (bf16[32,256,256]{2,1,0:T(8,128)(2,1)S(1)}, f32[32,256]{1,0:T(8,128)S(1)}, f32[32,256]{1,0:T(8,128)S(1)}, bf16[1152,128]{1,0:T(8,128)(2,1)S(1)}) custom-call(f32[64,256]{1,0:T(8,128)S(1)} %get-tuple-element.17.x_ref, f32[64,256]{1,0:T(8,128)S(1)} %collective-permute-done.h_ref, f32[64,256]{1,0:T(8,128)S(1)} %get-tuple-element.18.v_ref), custom_call_target="tpu_custom_call" | custom-call | flops 100000000 | bytes 8388608 | tf_op jit(solution)/shard_map/columns/pallas_call | solution.py:281
  13.0 0.0 collective-permute-done.1.refs_1_
  13.0 0.0 collective-permute-done.2.refs_2_
  13.0 0.0 collective-permute-done.3.refs_3_
  13.0 0.0 copy-start
  13.1 0.6 %copy-done = s32[4]{0:T(128)S(1)} copy-done((s32[4]{0:T(128)S(1)}, s32[4]{0:T(128)}, u32[]{:S(2)}) %copy-start) | copy-done | bytes 40
  13.7 0.7 %copy-done.2 = s32[4]{0:T(128)S(1)} copy-done((s32[4]{0:T(128)S(1)}, s32[4]{0:T(128)}, u32[]{:S(2)}) %copy-start.2) | copy-done | bytes 40
  14.4 0.9 %windows.1.refs_0_ = f32[16,1280]{1,0:T(8,128)S(1)} custom-call(s32[4]{0:T(128)S(1)} %copy-done, s32[4]{0:T(128)S(1)} %copy-done.2, f32[32,256]{1,0:T(8,128)S(1)} %get-tuple-element.21.after.scale_ref, f32[16,512]{1,0:T(8,128)S(1)} %get-tuple-element.22.refs_0_, f32[16,512]{1,0:T(8,128)S(1)} %collective-permute-done.1.refs_1_, ...), custom_call_target="tpu_custom_call" | custom-call | tf_op jit(solution)/shard_map/windows/pallas_call | solution.py:297
  15.2 2.0 %collective-permute-start.6 = (f32[16,1280]{1,0:T(8,128)S(1)}, f32[16,1280]{1,0:T(8,128)S(1)}, u32[]{:S(2)}, u32[]{:S(2)}) collective-permute-start(f32[16,1280]{1,0:T(8,128)S(1)} %windows.1.refs_0_), channel_id=1, source_target_pairs={{0,8},{1,9},{2,10},{3,11},{4,12},{5,13},{6,14},{7,15},{8,0},{9,1},... | collective-permute-start | bytes 245768 | tf_op jit(solution)/shard_map/ppermute | solution.py:21
  17.3 1.1 %collective-permute-start.5 = (f32[16,1280]{1,0:T(8,128)S(1)}, f32[16,1280]{1,0:T(8,128)S(1)}, u32[]{:S(2)}, u32[]{:S(2)}) collective-permute-start(f32[16,1280]{1,0:T(8,128)S(1)} %windows.1.refs_0_), channel_id=1, source_target_pairs={{0,12},{1,13},{2,14},{3,15},{4,8},{5,9},{6,10},{7,11},{8,4},{9,5},... | collective-permute-start | bytes 245768 | tf_op jit(solution)/shard_map/ppermute | solution.py:21
  18.4 0.2 collective-permute-start.4
  18.6 3.7 %columns.2 = (bf16[32,256,256]{2,1,0:T(8,128)(2,1)S(1)}, f32[32,256]{1,0:T(8,128)S(1)}, f32[32,256]{1,0:T(8,128)S(1)}) custom-call(f32[64,256]{1,0:T(8,128)S(1)} %get-tuple-element.17.x_ref, f32[64,256]{1,0:T(8,128)S(1)} %collective-permute-done.h_ref, f32[64,256]{1,0:T(8,128)S(1)} %get-tuple-element.18.v_ref), custom_call_target="tpu_custom_call" | custom-call | flops 100000000 | bytes 8388608 | tf_op jit(solution)/shard_map/columns/pallas_call | solution.py:281
  22.3 1.6 %collective-permute-done.6.refs_3_ = f32[16,1280]{1,0:T(8,128)S(1)} collective-permute-done((f32[16,1280]{1,0:T(8,128)S(1)}, f32[16,1280]{1,0:T(8,128)S(1)}, u32[]{:S(2)}, u32[]{:S(2)}) %collective-permute-start.6) | collective-permute-done | bytes 81952 | tf_op jit(solution)/shard_map/ppermute | solution.py:21
  23.9 0.0 collective-permute-done.5.refs_2_
  23.9 0.7 %collective-permute-done.4.refs_1_ = f32[16,1280]{1,0:T(8,128)S(1)} collective-permute-done((f32[16,1280]{1,0:T(8,128)S(1)}, f32[16,1280]{1,0:T(8,128)S(1)}, u32[]{:S(2)}, u32[]{:S(2)}) %collective-permute-start.4) | collective-permute-done | bytes 81952 | tf_op jit(solution)/shard_map/ppermute | solution.py:21
  24.6 0.3 query_stats.1.ya
  24.9 0.9 %collective-permute-start.9 = (f32[16,1408]{1,0:T(8,128)S(1)}, f32[16,1408]{1,0:T(8,128)S(1)}, u32[]{:S(2)}, u32[]{:S(2)}) collective-permute-start(f32[16,1408]{1,0:T(8,128)S(1)} %query_stats.1.ya), channel_id=1, source_target_pairs={{0,1},{1,0},{2,3},{3,2},{4,5},{5,4},{6,7},{7,6},{8,9},{9,8},{10,11... | collective-permute-start | bytes 270344 | tf_op jit(solution)/shard_map/ppermute | solution.py:21
  25.9 0.4 collective-permute-start.8
  26.2 1.3 %collective-permute-start.7 = (f32[16,1408]{1,0:T(8,128)S(1)}, f32[16,1408]{1,0:T(8,128)S(1)}, u32[]{:S(2)}, u32[]{:S(2)}) collective-permute-start(f32[16,1408]{1,0:T(8,128)S(1)} %query_stats.1.ya), channel_id=1, source_target_pairs={{0,3},{1,2},{2,1},{3,0},{4,7},{5,6},{6,5},{7,4},{8,11},{9,10},{10,... | collective-permute-start | bytes 270344 | tf_op jit(solution)/shard_map/ppermute | solution.py:21
  28.2 0.0 collective-permute-done.9.yb
  28.2 0.0 copy-start.1
  28.2 0.0 copy-start.3
  28.3 2.3 %first_two.1.so_far = f32[128,256]{1,0:T(8,128)S(1)} custom-call(f32[16,1408]{1,0:T(8,128)S(1)} %query_stats.1.ya, f32[16,1408]{1,0:T(8,128)S(1)} %collective-permute-done.9.yb, bf16[32,256,256]{2,1,0:T(8,128)(2,1)S(1)} %get-tuple-element.28.hankel, f32[32,256]{1,0:T(8,128)S(1)} %get-tuple-element.21.after.scale_ref, f32[32,256]{1,0:T(8,128)S(1)} %get-tuple-element.29.offset_ref), custom_call_target="tpu_custom_call" | custom-call | flops 500000000 | bytes 4194304 | tf_op jit(solution)/shard_map/first_two/pallas_call | solution.py:323
  30.5 0.0 collective-permute-done.8.y
  30.6 1.2 %third.1.so_far = f32[128,256]{1,0:T(8,128)S(1)} custom-call(f32[16,1408]{1,0:T(8,128)S(1)} %collective-permute-done.8.y, bf16[32,256,256]{2,1,0:T(8,128)(2,1)S(1)} %get-tuple-element.26.hankel, f32[32,256]{1,0:T(8,128)S(1)} %get-tuple-element.19.after.scale_ref, f32[32,256]{1,0:T(8,128)S(1)} %get-tuple-element.27.offset_ref, f32[128,256]{1,0:T(8,128)S(1)} %first_two.1.so_far), custom_call_target="tpu_custom_call" | custom-call | flops 200000000 | bytes 2097152 | tf_op jit(solution)/shard_map/third/pallas_call | solution.py:332
  31.7 0.4 collective-permute-done.7.y
  32.1 0.0 copy-done.1
  32.2 2.3 %fourth.1 = (f32[4,32]{1,0:T(4,128)S(1)}, f32[1,256]{1,0:T(1,128)}) custom-call(s32[4]{0:T(128)S(1)} %copy-done.1, s32[4]{0:T(128)S(1)} %copy-done.3, s32[1]{0:T(128)S(6)} %copy.7.excl, f32[16,1408]{1,0:T(8,128)S(1)} %collective-permute-done.7.y, bf16[32,256,256]{2,1,0:T(8,128)(2,1)S(1)} %get-tuple-element.26.hankel, ...), custom_call_target="tpu_custom_call" | custom-call | tf_op jit(solution)/shard_map/fourth/pallas_call | solution.py:341
  34.4 0.8 %collective-permute-start.12 = (f32[4,32]{1,0:T(4,128)S(1)}, f32[4,32]{1,0:T(4,128)S(1)}, u32[]{:S(2)}, u32[]{:S(2)}) collective-permute-start(f32[4,32]{1,0:T(4,128)S(1)} %get-tuple-element.30), channel_id=1, source_target_pairs={{0,3},{1,2},{2,1},{3,0},{4,7},{5,6},{6,5},{7,4},{8,11},{9,10},{10,... | collective-permute-start | bytes 1544 | tf_op jit(solution)/shard_map/ppermute | solution.py:21
  35.3 0.9 %collective-permute-start.11 = (f32[4,32]{1,0:T(4,128)S(1)}, f32[4,32]{1,0:T(4,128)S(1)}, u32[]{:S(2)}, u32[]{:S(2)}) collective-permute-start(f32[4,32]{1,0:T(4,128)S(1)} %get-tuple-element.30), channel_id=1, source_target_pairs={{0,2},{1,3},{2,0},{3,1},{4,6},{5,7},{6,4},{7,5},{8,10},{9,11},{10,... | collective-permute-start | bytes 1544 | tf_op jit(solution)/shard_map/ppermute | solution.py:21
  36.2 0.4 collective-permute-start.10
  36.6 0.9 %collective-permute-done.12 = f32[4,32]{1,0:T(4,128)S(1)} collective-permute-done((f32[4,32]{1,0:T(4,128)S(1)}, f32[4,32]{1,0:T(4,128)S(1)}, u32[]{:S(2)}, u32[]{:S(2)}) %collective-permute-start.12) | collective-permute-done | bytes 544 | tf_op jit(solution)/shard_map/ppermute | solution.py:21
  37.4 0.3 collective-permute-done.11
  37.7 0.0 collective-permute-done.10
  37.7 4.0 %collective-permute-start.15 = (f32[4,32]{1,0:T(4,128)S(1)}, f32[4,32]{1,0:T(4,128)S(1)}, u32[]{:S(2)}, u32[]{:S(2)}) collective-permute-start(f32[4,32]{1,0:T(4,128)S(1)} %minimum_minimum_fusion.1), channel_id=1, source_target_pairs={{0,9},{1,8},{2,11},{3,10},{4,13},{5,12},{6,15},{7,14},{8,1},{9,0},... | collective-permute-start | bytes 1544 | tf_op jit(solution)/shard_map/ppermute | solution.py:21
  41.7 0.1 collective-permute-start.14
  41.9 0.0 collective-permute-start.13
  41.9 1.1 %collective-permute-done.15 = f32[4,32]{1,0:T(4,128)S(1)} collective-permute-done((f32[4,32]{1,0:T(4,128)S(1)}, f32[4,32]{1,0:T(4,128)S(1)}, u32[]{:S(2)}, u32[]{:S(2)}) %collective-permute-start.15) | collective-permute-done | bytes 544 | tf_op jit(solution)/shard_map/ppermute | solution.py:21
  43.0 3.5 %collective-permute-done.14 = f32[4,32]{1,0:T(4,128)S(1)} collective-permute-done((f32[4,32]{1,0:T(4,128)S(1)}, f32[4,32]{1,0:T(4,128)S(1)}, u32[]{:S(2)}, u32[]{:S(2)}) %collective-permute-start.14) | collective-permute-done | bytes 544 | tf_op jit(solution)/shard_map/ppermute | solution.py:21
  46.5 0.0 collective-permute-done.13
  46.5 0.6 %minimum_minimum_fusion = f32[4,32]{1,0:T(4,128)} fusion(f32[4,32]{1,0:T(4,128)S(1)} %collective-permute-done.15, f32[4,32]{1,0:T(4,128)S(1)} %collective-permute-done.14, f32[4,32]{1,0:T(4,128)S(1)} %minimum_minimum_fusion.1, f32[4,32]{1,0:T(4,128)S(1)} %collective-permute-done.13), kind=kLoop, calls=%fused_computation.1 | loop fusion | flops 384 | bytes 2560 | tf_op jit(solution)/shard_map/min | solution.py:352
  (4 shorter events, 0.0 us)
Async XLA Ops:
  2.4 6.8 %collective-permute-start = (f32[64,256]{1,0:T(8,128)S(1)}, f32[64,256]{1,0:T(8,128)S(1)}, u32[]{:S(2)}, u32[]{:S(2)}) collective-permute-start(f32[64,256]{1,0:T(8,128)S(1)} %get-tuple-element.17.x_ref), channel_id=1, source_target_pairs={{1,0},{2,1},{3,2},{4,3},{5,4},{6,5},{7,6},{8,7},{9,8},{10,9},{11,1... | collective-permute-start | bytes 196616 | tf_op jit(solution)/shard_map/ppermute | solution.py:278
  4.3 8.7 %collective-permute-start.1 = (f32[16,512]{1,0:T(8,128)S(1)}, f32[16,512]{1,0:T(8,128)S(1)}, u32[]{:S(2)}, u32[]{:S(2)}) collective-permute-start(f32[16,512]{1,0:T(8,128)S(1)} %get-tuple-element.23), channel_id=1, source_target_pairs={{0,1},{1,0},{2,3},{3,2},{4,5},{5,4},{6,7},{7,6},{8,9},{9,8},{10,11... | collective-permute-start | bytes 98312 | tf_op jit(solution)/shard_map/ppermute | solution.py:21
  4.4 8.6 %collective-permute-start.2 = (f32[16,512]{1,0:T(8,128)S(1)}, f32[16,512]{1,0:T(8,128)S(1)}, u32[]{:S(2)}, u32[]{:S(2)}) collective-permute-start(f32[16,512]{1,0:T(8,128)S(1)} %get-tuple-element.24), channel_id=1, source_target_pairs={{0,2},{1,3},{2,0},{3,1},{4,6},{5,7},{6,4},{7,5},{8,10},{9,11},{10,... | collective-permute-start | bytes 98312 | tf_op jit(solution)/shard_map/ppermute | solution.py:21
  7.2 5.9 %collective-permute-start.3 = (f32[16,512]{1,0:T(8,128)S(1)}, f32[16,512]{1,0:T(8,128)S(1)}, u32[]{:S(2)}, u32[]{:S(2)}) collective-permute-start(f32[16,512]{1,0:T(8,128)S(1)} %get-tuple-element.25), channel_id=1, source_target_pairs={{0,3},{1,2},{2,1},{3,0},{4,7},{5,6},{6,5},{7,4},{8,11},{9,10},{10,... | collective-permute-start | bytes 98312 | tf_op jit(solution)/shard_map/ppermute | solution.py:21
  13.0 0.7 %copy-start = (s32[4]{0:T(128)S(1)}, s32[4]{0:T(128)}, u32[]{:S(2)}) copy-start(s32[4]{0:T(128)} %owners.3) | copy-start | bytes 52
  13.7 0.7 %copy-start.2 = (s32[4]{0:T(128)S(1)}, s32[4]{0:T(128)}, u32[]{:S(2)}) copy-start(s32[4]{0:T(128)} %blocks.3) | copy-start | bytes 52
  15.2 8.7 %collective-permute-start.6 = (f32[16,1280]{1,0:T(8,128)S(1)}, f32[16,1280]{1,0:T(8,128)S(1)}, u32[]{:S(2)}, u32[]{:S(2)}) collective-permute-start(f32[16,1280]{1,0:T(8,128)S(1)} %windows.1.refs_0_), channel_id=1, source_target_pairs={{0,8},{1,9},{2,10},{3,11},{4,12},{5,13},{6,14},{7,15},{8,0},{9,1},... | collective-permute-start | bytes 245768 | tf_op jit(solution)/shard_map/ppermute | solution.py:21
  17.3 6.7 %collective-permute-start.5 = (f32[16,1280]{1,0:T(8,128)S(1)}, f32[16,1280]{1,0:T(8,128)S(1)}, u32[]{:S(2)}, u32[]{:S(2)}) collective-permute-start(f32[16,1280]{1,0:T(8,128)S(1)} %windows.1.refs_0_), channel_id=1, source_target_pairs={{0,12},{1,13},{2,14},{3,15},{4,8},{5,9},{6,10},{7,11},{8,4},{9,5},... | collective-permute-start | bytes 245768 | tf_op jit(solution)/shard_map/ppermute | solution.py:21
  18.4 6.3 %collective-permute-start.4 = (f32[16,1280]{1,0:T(8,128)S(1)}, f32[16,1280]{1,0:T(8,128)S(1)}, u32[]{:S(2)}, u32[]{:S(2)}) collective-permute-start(f32[16,1280]{1,0:T(8,128)S(1)} %windows.1.refs_0_), channel_id=1, source_target_pairs={{0,4},{1,5},{2,6},{3,7},{4,0},{5,1},{6,2},{7,3},{8,12},{9,13},{10,... | collective-permute-start | bytes 245768 | tf_op jit(solution)/shard_map/ppermute | solution.py:21
  24.9 3.3 %collective-permute-start.9 = (f32[16,1408]{1,0:T(8,128)S(1)}, f32[16,1408]{1,0:T(8,128)S(1)}, u32[]{:S(2)}, u32[]{:S(2)}) collective-permute-start(f32[16,1408]{1,0:T(8,128)S(1)} %query_stats.1.ya), channel_id=1, source_target_pairs={{0,1},{1,0},{2,3},{3,2},{4,5},{5,4},{6,7},{7,6},{8,9},{9,8},{10,11... | collective-permute-start | bytes 270344 | tf_op jit(solution)/shard_map/ppermute | solution.py:21
  25.9 4.7 %collective-permute-start.8 = (f32[16,1408]{1,0:T(8,128)S(1)}, f32[16,1408]{1,0:T(8,128)S(1)}, u32[]{:S(2)}, u32[]{:S(2)}) collective-permute-start(f32[16,1408]{1,0:T(8,128)S(1)} %query_stats.1.ya), channel_id=1, source_target_pairs={{0,2},{1,3},{2,0},{3,1},{4,6},{5,7},{6,4},{7,5},{8,10},{9,11},{10,... | collective-permute-start | bytes 270344 | tf_op jit(solution)/shard_map/ppermute | solution.py:21
  26.2 5.9 %collective-permute-start.7 = (f32[16,1408]{1,0:T(8,128)S(1)}, f32[16,1408]{1,0:T(8,128)S(1)}, u32[]{:S(2)}, u32[]{:S(2)}) collective-permute-start(f32[16,1408]{1,0:T(8,128)S(1)} %query_stats.1.ya), channel_id=1, source_target_pairs={{0,3},{1,2},{2,1},{3,0},{4,7},{5,6},{6,5},{7,4},{8,11},{9,10},{10,... | collective-permute-start | bytes 270344 | tf_op jit(solution)/shard_map/ppermute | solution.py:21
  28.2 3.9 %copy-start.1 = (s32[4]{0:T(128)S(1)}, s32[4]{0:T(128)}, u32[]{:S(2)}) copy-start(s32[4]{0:T(128)} %owners.3) | copy-start | bytes 52
  28.2 3.9 %copy-start.3 = (s32[4]{0:T(128)S(1)}, s32[4]{0:T(128)}, u32[]{:S(2)}) copy-start(s32[4]{0:T(128)} %blocks.3) | copy-start | bytes 52
  34.4 3.0 %collective-permute-start.12 = (f32[4,32]{1,0:T(4,128)S(1)}, f32[4,32]{1,0:T(4,128)S(1)}, u32[]{:S(2)}, u32[]{:S(2)}) collective-permute-start(f32[4,32]{1,0:T(4,128)S(1)} %get-tuple-element.30), channel_id=1, source_target_pairs={{0,3},{1,2},{2,1},{3,0},{4,7},{5,6},{6,5},{7,4},{8,11},{9,10},{10,... | collective-permute-start | bytes 1544 | tf_op jit(solution)/shard_map/ppermute | solution.py:21
  35.3 2.4 %collective-permute-start.11 = (f32[4,32]{1,0:T(4,128)S(1)}, f32[4,32]{1,0:T(4,128)S(1)}, u32[]{:S(2)}, u32[]{:S(2)}) collective-permute-start(f32[4,32]{1,0:T(4,128)S(1)} %get-tuple-element.30), channel_id=1, source_target_pairs={{0,2},{1,3},{2,0},{3,1},{4,6},{5,7},{6,4},{7,5},{8,10},{9,11},{10,... | collective-permute-start | bytes 1544 | tf_op jit(solution)/shard_map/ppermute | solution.py:21
  36.2 1.5 %collective-permute-start.10 = (f32[4,32]{1,0:T(4,128)S(1)}, f32[4,32]{1,0:T(4,128)S(1)}, u32[]{:S(2)}, u32[]{:S(2)}) collective-permute-start(f32[4,32]{1,0:T(4,128)S(1)} %get-tuple-element.30), channel_id=1, source_target_pairs={{0,1},{1,0},{2,3},{3,2},{4,5},{5,4},{6,7},{7,6},{8,9},{9,8},{10,11... | collective-permute-start | bytes 1544 | tf_op jit(solution)/shard_map/ppermute | solution.py:21
  37.7 5.3 %collective-permute-start.15 = (f32[4,32]{1,0:T(4,128)S(1)}, f32[4,32]{1,0:T(4,128)S(1)}, u32[]{:S(2)}, u32[]{:S(2)}) collective-permute-start(f32[4,32]{1,0:T(4,128)S(1)} %minimum_minimum_fusion.1), channel_id=1, source_target_pairs={{0,9},{1,8},{2,11},{3,10},{4,13},{5,12},{6,15},{7,14},{8,1},{9,0},... | collective-permute-start | bytes 1544 | tf_op jit(solution)/shard_map/ppermute | solution.py:21
  41.7 4.8 %collective-permute-start.14 = (f32[4,32]{1,0:T(4,128)S(1)}, f32[4,32]{1,0:T(4,128)S(1)}, u32[]{:S(2)}, u32[]{:S(2)}) collective-permute-start(f32[4,32]{1,0:T(4,128)S(1)} %minimum_minimum_fusion.1), channel_id=1, source_target_pairs={{0,13},{1,12},{2,15},{3,14},{4,9},{5,8},{6,11},{7,10},{8,5},{9,4},... | collective-permute-start | bytes 1544 | tf_op jit(solution)/shard_map/ppermute | solution.py:21
  41.9 4.7 %collective-permute-start.13 = (f32[4,32]{1,0:T(4,128)S(1)}, f32[4,32]{1,0:T(4,128)S(1)}, u32[]{:S(2)}, u32[]{:S(2)}) collective-permute-start(f32[4,32]{1,0:T(4,128)S(1)} %minimum_minimum_fusion.1), channel_id=1, source_target_pairs={{0,5},{1,4},{2,7},{3,6},{4,1},{5,0},{6,3},{7,2},{8,13},{9,12},{10,... | collective-permute-start | bytes 1544 | tf_op jit(solution)/shard_map/ppermute | solution.py:21

commit v3 on v0

v3 whole, which is shorter than its diff:
```python
import functools

import jax
import jax.numpy as jnp
from jax import lax
from jax.experimental import pallas as pl
from jax.experimental.pallas import tpu as pltpu
from jax.sharding import PartitionSpec as P

M = 256
QB = 32
CORES = 2
BASE = 4
LANES = 128

f32 = jnp.float32
bf16 = jnp.bfloat16


def exchanged(block, mask):
    devices = range(lax.axis_size("col"))
    return lax.ppermute(block, "col", [(i, i ^ mask) for i in devices])


def rounds_from(base, devices):
    rounds = []
    while base < devices:
        radix = 4 if (devices // base) % 4 == 0 else 2
        rounds.append([base * i for i in range(1, radix)])
        base *= radix
    return rounds


def split3(value):
    high = value.astype(bf16)
    rest = value - high.astype(f32)
    mid = rest.astype(bf16)
    low = (rest - mid.astype(f32)).astype(bf16)
    return high, mid, low


def half_rows(ref, which):
    half = ref.shape[0] // CORES
    return pl.ds(pl.multiple_of(which * half, half), half)


def share_kernel(packed, keep, send):
    core = lax.rem(lax.axis_index("col"), CORES)
    keep[...] = packed[half_rows(packed, core), :]
    send[...] = packed[half_rows(packed, 1 - core), :]


def chip_kernel(starts, own, other, out, both, starts_out):
    turns = starts.shape[0]
    half, width = own.shape[0], own.shape[1] // 2
    here = lax.axis_index("col")
    core = lax.rem(here, CORES)
    row = lax.broadcasted_iota(jnp.int32, (width, width), 0)
    col = lax.broadcasted_iota(jnp.int32, (width, width), 1)
    flip = (row + col == width - 1).astype(bf16)
    stack = jnp.concatenate(split3(own[:, :width]) + split3(other[:, :width]), axis=0)
    turned = jnp.dot(stack, flip, preferred_element_type=f32)
    for i in range(CORES):
        high, mid, low = (turned[(3 * i + j) * half : (3 * i + j + 1) * half] for j in range(3))
        out[:, i * width : (i + 1) * width] = low + mid + high
    for turn in range(turns):
        starts_out[turn : turn + 1, :] = jnp.full((1, LANES), starts[turn].astype(f32))
    both[core] = own[...]
    both[1 - core] = other[...]
    lane = lax.broadcasted_iota(jnp.int32, (half, LANES), 1)
    per_tile = LANES // QB
    for tile in range(turns // per_tile):
        valids = jnp.zeros((half, LANES), f32)
        for i in range(per_tile):
            start = starts[tile * per_tile + i]
            owner, shift = start // width, lax.rem(start, width)
            mine = (owner == here).astype(f32)
            others = (owner == here ^ 1).astype(f32)
            flags = mine * own[:, width:] + others * other[:, width:]
            flags = pltpu.roll(flags, lax.rem(width - shift, width), 1)[:, :LANES]
            if i:
                flags = pltpu.roll(flags, i * QB, 1)
            valids = jnp.where((lane >= i * QB) & (lane < (i + 1) * QB), flags, valids)
        at = 2 * width + tile * LANES
        out[:, at : at + LANES] = valids


def windows_kernel(masks, starts_ref, after, after_too, *refs):
    parts, out, lines = refs[: len(masks)], refs[len(masks)], refs[len(masks) + 1]
    turns = starts_ref.shape[0]
    starts = [jnp.max(starts_ref[turn : turn + 1, :]).astype(jnp.int32) for turn in range(turns)]
    half, width = out.shape[0], lines.shape[1]
    here = lax.axis_index("col")
    for i, part in enumerate(parts):
        for j in range(CORES):
            at = (CORES * i + j) * half
            lines[at : at + half, :] = part[:, j * width : (j + 1) * width]
    none = CORES * len(masks)
    lines[none * half :, :] = jnp.zeros((half, width), f32)
    held = sum(masks[i] for i in range(1, len(masks)) if masks[i] & (masks[i] - 1) == 0) + CORES - 1

    def segment(device):
        relative = device ^ here
        slot = CORES * ((relative & (held - CORES + 1)) // BASE) + (relative & (CORES - 1))
        slot = jnp.where((relative & held) == relative, slot, none)
        return lines[pl.ds(pl.multiple_of(slot * half, half), half), :]

    lane = lax.broadcasted_iota(jnp.int32, (half, width), 1)
    lane_128 = lax.broadcasted_iota(jnp.int32, (half, LANES), 1)
    per_tile = LANES // QB
    for tile in range(turns // per_tile):
        tails = jnp.zeros((half, LANES), f32)
        for i in range(per_tile):
            turn = tile * per_tile + i
            owner, split = starts[turn] // width, lax.rem(starts[turn], width) + QB
            amount = lax.rem(split, width)
            first = pltpu.roll(segment(owner), amount, 1)
            second = pltpu.roll(segment(owner + 1), amount, 1)
            out[:, turn * M : (turn + 1) * M] = jnp.where(lane >= split, first, second)
            tail = first[:, :LANES]
            if i:
                tail = pltpu.roll(tail, i * QB, 1)
            tails = jnp.where((lane_128 >= i * QB) & (lane_128 < (i + 1) * QB), tail, tails)
        at = turns * M + tile * LANES
        out[:, at : at + LANES] = tails
        at = turns * (M + QB) + tile * LANES
        flags = slice(2 * width + tile * LANES, 2 * width + (tile + 1) * LANES)
        out[:, at : at + LANES] = sum([part[:, flags] for part in parts[1:]], parts[0][:, flags])


def query_kernel(turns, after, band_ref, *refs):
    parts, out = refs[:-1], refs[-1]
    total = parts[0][...]
    for part in parts[1:]:
        total = total + part[...]
    samples = turns * (M + QB)
    per_tile = LANES // QB
    main, tail = [], []
    for tile in range(turns // per_tile):
        at = turns * M + tile * LANES
        tail_tile = total[:, at : at + LANES]
        lane = lax.broadcasted_iota(jnp.int32, tail_tile.shape, 1)
        centre = jnp.zeros_like(tail_tile)
        for i in range(per_tile):
            turn = tile * per_tile + i
            block = total[:, turn * M : (turn + 1) * M]
            mean = jnp.sum(block, axis=1, keepdims=True) * (1.0 / M)
            main.append(block - mean)
            centre = jnp.where((lane >= i * QB) & (lane < (i + 1) * QB), mean, centre)
        tail.append(tail_tile - centre)
    for tile in range(turns // per_tile):
        rows = main[tile * per_tile : (tile + 1) * per_tile] + [tail[tile]]
        shifted = jnp.concatenate(rows, axis=1)
        half = shifted.shape[0]
        stack = jnp.concatenate([*split3(shifted), *split3(shifted * shifted)], axis=0)
        sums = jnp.dot(stack, band_ref[...], preferred_element_type=f32)
        first = sums[2 * half : 3 * half] + sums[half : 2 * half] + sums[:half]
        second = sums[5 * half : 6 * half] + sums[4 * half : 5 * half] + sums[3 * half : 4 * half]
        mean = first * (1.0 / M)
        spread = second * (1.0 / M) - mean * mean
        at = samples + tile * LANES
        scale = total[:, at : at + LANES] / jnp.sqrt(spread + 1e-05)
        out[:, at : at + LANES] = scale
        out[:, at + turns * QB : at + turns * QB + LANES] = mean * scale
    for turn in range(turns):
        out[:, turn * M : (turn + 1) * M] = main[turn]
    for tile in range(turns // per_tile):
        at = turns * M + tile * LANES
        out[:, at : at + LANES] = tail[tile]


def band_matrix(shape):
    lane = lax.broadcasted_iota(jnp.int32, shape, 0)
    query = lax.broadcasted_iota(jnp.int32, shape, 1)
    per_tile = LANES // QB
    beyond = lane - per_tile * M
    turn = jnp.where(beyond < 0, lane // M, beyond // QB)
    place = jnp.where(beyond < 0, lane % M, M + beyond % QB)
    q = query % QB
    inside = (turn == query // QB) & (place >= QB - q) & (place <= M + QB - 1 - q)
    return jnp.where(inside, 1.0, 0.0).astype(bf16)


def segment_columns(own, following, hankel, scale_ref, offset_ref):
    width = scale_ref.shape[1]
    samples = own[:, :width]
    centre = jnp.sum(samples, axis=1, keepdims=True) * (1.0 / width)
    extended = jnp.concatenate([samples - centre, following[:, :width] - centre], axis=1)
    length = extended.shape[1]
    first, second = extended, extended * extended
    step = 1
    while step < M:
        first = first + pltpu.roll(first, length - step, 1)
        second = second + pltpu.roll(second, length - step, 1)
        step *= 2
    mean = first[:, :width] * (1.0 / M)
    spread = second[:, :width] * (1.0 / M) - mean * mean
    scale = own[:, width:] / jnp.sqrt(jnp.maximum(spread, 0.0) + 1e-05)
    scale_ref[...] = scale
    offset_ref[...] = mean * scale
    for c in range(extended.shape[0]):
        base = jnp.broadcast_to(extended[c : c + 1, :], (16, length))
        base = pltpu.roll(base, length - 15, 1, stride=1, stride_axis=0).astype(bf16)
        for b in range(M // 16):
            shift = M - 16 - 16 * b
            block = pltpu.roll(base, length - shift, 1) if shift else base
            hankel[c, 16 * b : 16 * (b + 1), :] = block[:, :width]


def first_columns_kernel(both, hankel, scale_ref, offset_ref, band_ref):
    band_ref[...] = band_matrix(band_ref.shape)
    segment_columns(both.at[0], both.at[1], hankel.at[0], scale_ref.at[0], offset_ref.at[0])


def second_columns_kernel(
    limit, starts, excl, both, following, hankel_in, scale_in, offset_in, hankel, scale_ref, offset_ref, banned, beyond
):
    width = banned.shape[1]
    columns = lax.axis_index("col") * width + lax.broadcasted_iota(jnp.int32, (QB, width), 1)
    apart = lax.broadcasted_iota(jnp.int32, (QB, width), 0) - columns
    last = jnp.where(columns > limit, 1.0, 0.0)
    for turn in range(starts.shape[0]):
        near = jnp.where(jnp.abs(apart + starts[turn]) < excl[0], 1.0, last)
        banned[turn * QB : (turn + 1) * QB, :] = near
    beyond[...] = last[:8]
    segment_columns(both.at[1], following, hankel.at[1], scale_ref.at[1], offset_ref.at[1])


def other_core_kernel(turns, y, hankel, scale_ref, offset_ref, out, windows_ref):
    queries = turns * QB
    samples = turns * (M + QB)
    per_tile = LANES // QB
    which = 1 - lax.rem(lax.axis_index("col"), CORES)
    by_query = jnp.transpose(y[:, samples : samples + queries])
    offsets = jnp.transpose(y[:, samples + queries : samples + 2 * queries])
    lines = []
    for turn in range(turns):
        at = turns * M + (turn // per_tile) * LANES
        tail = y[:, at : at + LANES]
        if turn % per_tile:
            tail = pltpu.roll(tail, LANES - (turn % per_tile) * QB, 1)
        lines.append(jnp.concatenate([y[:, turn * M : (turn + 1) * M], tail], axis=1))
    length = M + LANES
    acc = -M * jnp.dot(offsets, offset_ref[which], preferred_element_type=f32, precision=lax.Precision.HIGHEST)
    for c in range(y.shape[0]):
        scale = by_query[:, c : c + 1]
        windows = []
        for turn in range(turns):
            row = jnp.broadcast_to(lines[turn][c : c + 1, :], (QB, length))
            row = pltpu.roll(row, length - QB, 1, stride=1, stride_axis=0)
            windows.append((row[:, :M] * scale[turn * QB : (turn + 1) * QB]).astype(bf16))
        windows = jnp.concatenate(windows, axis=0)
        windows_ref[c] = windows
        products = jnp.dot(windows, hankel[which, c], preferred_element_type=f32)
        acc = acc + products * scale_ref[which, c : c + 1, :]
    out[...] = acc


def own_core_kernel(turns, y, windows_ref, hankel, scale_ref, offset_ref, out):
    queries = turns * QB
    at = turns * (M + QB) + queries
    which = lax.rem(lax.axis_index("col"), CORES)
    offsets = jnp.transpose(y[:, at : at + queries])
    acc = -M * jnp.dot(offsets, offset_ref[which], preferred_element_type=f32, precision=lax.Precision.HIGHEST)
    for c in range(y.shape[0]):
        products = jnp.dot(windows_ref[c], hankel[which, c], preferred_element_type=f32)
        acc = acc + products * scale_ref[which, c : c + 1, :]
    out[...] = acc


def minima_kernel(turns, channels, own, other, banned, beyond, row_out, col_out):
    distance = 1.0 - (own[...] + other[...]) * (1.0 / (M * channels))
    distance = jnp.where(banned[...] > 0.0, 4.0, distance)
    width = distance.shape[1]
    column_min = jnp.min(distance, axis=0, keepdims=True)
    col_out[...] = jnp.where(beyond[:1, :] > 0.0, 0.0, column_min)
    narrow = distance[:, :LANES]
    for at in range(LANES, width, LANES):
        narrow = jnp.minimum(narrow, distance[:, at : at + LANES])
    flat = jnp.min(jnp.transpose(narrow), axis=0, keepdims=True)
    for turn in range(turns):
        row_out[turn : turn + 1, :] = flat[:, turn * QB : (turn + 1) * QB]


SPECS = dict(
    v=pl.BlockSpec(memory_space=pltpu.VMEM), s=pl.BlockSpec(memory_space=pltpu.SMEM), a=pl.BlockSpec(memory_space=pl.ANY)
)


def call(kernel, name, out_shape, spaces, *operands, flops=10**6, **options):
    many = isinstance(out_shape, list)
    return pl.pallas_call(
        kernel,
        out_shape=out_shape,
        in_specs=[SPECS[space] for space in spaces],
        out_specs=[SPECS["v"]] * len(out_shape) if many else SPECS["v"],
        compiler_params=pltpu.CompilerParams(vmem_limit_bytes=40 * 2**20),
        cost_estimate=pl.CostEstimate(flops=flops, bytes_accessed=2**20, transcendentals=0),
        name=name,
        **options,
    )(*operands)


def shards(series, valid, owners, blocks, excl):
    channels, seg_len = series.shape
    devices_col = lax.axis_size("col")
    turns = owners.shape[0]
    half = channels // CORES
    queries = turns * QB
    limit = seg_len * devices_col - M
    starts = owners * seg_len + blocks * QB

    packed = jnp.concatenate([series, valid.astype(f32)], axis=1)
    part = jax.ShapeDtypeStruct((half, 2 * seg_len), f32)
    keep, send = call(share_kernel, "share", [part] * 2, "v", packed)
    chip, both, starts_vector = call(
        chip_kernel,
        "chip",
        [
            jax.ShapeDtypeStruct((half, 2 * seg_len + queries), f32),
            jax.ShapeDtypeStruct((CORES, half, 2 * seg_len), f32),
            jax.ShapeDtypeStruct((turns, LANES), f32),
        ],
        "svv",
        starts,
        keep,
        exchanged(send, 1),
    )
    back = [(i, (i - CORES) % devices_col) for i in range(devices_col)]
    following = lax.ppermute(both[0, :, :seg_len], "col", back)

    side = [
        jax.ShapeDtypeStruct((CORES, half, M, seg_len), bf16),
        jax.ShapeDtypeStruct((CORES, half, seg_len), f32),
        jax.ShapeDtypeStruct((CORES, half, seg_len), f32),
    ]
    band = jax.ShapeDtypeStruct((LANES // QB * (M + QB), LANES), bf16)
    *columns, band = call(first_columns_kernel, "columns", [*side, band], "v", both, flops=10**8)

    rounds = rounds_from(BASE, devices_col)
    masks = [0, *rounds[0]]
    total = call(
        functools.partial(windows_kernel, masks),
        "windows",
        jax.ShapeDtypeStruct((half, turns * (M + 2 * QB)), f32),
        "vaa" + "v" * len(masks),
        starts_vector,
        columns[1],
        following,
        chip,
        *[exchanged(chip, mask) for mask in rounds[0]],
        scratch_shapes=[pltpu.VMEM(((CORES * len(masks) + 1) * half, seg_len), f32)],
    )
    for others in rounds[1:]:
        total = sum([exchanged(total, mask) for mask in others], total)
    *columns, banned, beyond = call(
        functools.partial(second_columns_kernel, limit),
        "columns",
        [*side, jax.ShapeDtypeStruct((queries, seg_len), f32), jax.ShapeDtypeStruct((8, seg_len), f32)],
        "ssvvaaa",
        starts,
        excl,
        both,
        following,
        *columns,
        input_output_aliases={4: 0, 5: 1, 6: 2},
        flops=10**8,
    )
    queried = call(
        functools.partial(query_kernel, turns),
        "query_stats",
        jax.ShapeDtypeStruct((half, turns * (M + 3 * QB)), f32),
        "avvv",
        columns[1],
        band,
        total,
        exchanged(total, CORES),
    )
    partial = jax.ShapeDtypeStruct((queries, seg_len), f32)
    theirs, windows = call(
        functools.partial(other_core_kernel, turns),
        "other_core",
        [partial, jax.ShapeDtypeStruct((half, queries, M), bf16)],
        "vvvv",
        queried,
        *columns,
    )
    mine = call(
        functools.partial(own_core_kernel, turns),
        "own_core",
        partial,
        "vvvvv",
        queried,
        windows,
        *columns,
        flops=5 * 10**8,
    )
    rows, column = call(
        functools.partial(minima_kernel, turns, channels),
        "minima",
        [jax.ShapeDtypeStruct((turns, QB), f32), jax.ShapeDtypeStruct((1, seg_len), f32)],
        "vvvv",
        mine,
        exchanged(theirs, 1),
        banned,
        beyond,
    )
    crossed = [[others[0] + 1, *(mask + 1 for mask in reversed(others[1:]))] for others in rounds]
    for others in [[1, 2, 3], *crossed]:
        rows = functools.reduce(jnp.minimum, [exchanged(rows, mask) for mask in others], rows)
    return (rows, column.reshape(seg_len))


def solution(mesh):
    return jax.shard_map(
        shards,
        mesh=mesh,
        in_specs=(P(None, ("grp", "col")), P(None, ("grp", "col")), P("grp"), P("grp"), P("grp")),
        out_specs=(P("grp", None), P(("grp", "col"))),
        check_vma=False,
    )
```

time: 841 us -> 39.7 us (0.05)
  blocking collectives: 366 us -> 0 us
  local copies, waits for them, and re-layouts: 273 us -> 0.01 us
  waiting for transfers between devices: 111 us -> 6.53 us
  matrix products: 58.4 us -> 0 us
  starting transfers between devices: 1.38 us -> 15.5 us
  Pallas kernels: 0 us -> 13 us
  between operations: 13.8 us -> 1.4 us
  loops' own time: 8.79 us -> 0 us
    psum x4 -> x0, blocking collectives: 237 us -> none  [spread_2(): return lax.psum(block, axis)]
    pmin x4 -> x0, blocking collectives: 130 us -> none  [step(): best = lax.pmin(best, 'col')]
    gather x8 -> x0, local copies, waits for them, and re-layouts: 128 us -> none  [turn_profile(): windows = samples[:, offsets]]
    psum x4 -> x0, waiting for transfers between devices: 110 us -> none  [spread_2(): return lax.psum(block, axis)]
    reshape x1 -> x0, local copies, waits for them, and re-layouts: 73.5 us -> none  [column_windows(): return repeated.reshape(channels, M, width + 1)[:, :, :count]]
    dot_general x4 -> x0, matrix products: 52.4 us -> none  [turn_profile(): jnp.einsum('cqk,ckj->cqj', windows, hankel, precision=highest, preferred_...]
    slice x2 -> x0, local copies, waits for them, and re-layouts: 33.8 us -> none  [the longest x1 22.3 us: column_windows(): repeated = jnp.tile(extended, (1, M + 1))[:, :M * (width + 1)]]
    unnamed x10 -> x0, local copies, waits for them, and re-layouts: 22.4 us -> none
  transfers between devices with their start and end apart: 5 -> 13, of which waited for: 5 -> 7; matrix products, arithmetic and copies ran while one was open for 0% -> 2% of each run, Pallas kernels for 0% -> 21%
where the time goes in v3:
time: 39.7 us; the launch traced here: 39.4 us
  starting transfers between devices  15.5 us (39%)
  Pallas kernels  13 us (33%)
  waiting for transfers between devices  6.53 us (16%)
  other arithmetic  2.96 us (7%)
  between operations  1.4 us (4%)
    pallas_call x9, Pallas kernels, call(): pl.pallas_call(kernel, out_shape=out_shape, in_specs=[SPECS[space] for sp...  13 us
    ppermute x12, starting transfers between devices, exchanged(): return lax.ppermute(block, 'col', [(i, i ^ mask) for i in devices])  10.8 us
    ppermute x12, waiting for transfers between devices, exchanged(): return lax.ppermute(block, 'col', [(i, i ^ mask) for i in devices])  6.53 us
    ppermute x1, starting transfers between devices, shards(): following = lax.ppermute(both[0, :, :seg_len], 'col', back)  4.7 us
    concatenate x1, other arithmetic, shards(): packed = jnp.concatenate([series, valid.astype(f32)], axis=1)  0.85 us
    convert_element_type x1, other arithmetic, shards(): packed = jnp.concatenate([series, valid.astype(f32)], axis=1)  0.85 us
  transfers between devices with their start and end apart: 13, of which 7 were waited for; matrix products, arithmetic and copies ran while one was open for 2% of the time, Pallas kernels for 21%

profile of v3, /device:TPU:0, one launch (start us, length us, event | category | flops | bytes accessed | tf_op | source)
XLA Modules:
  0.0 39.4 jit_solution(15963106980008436162)
XLA Ops:
  0.6 0.8 %convert_element_type.3 = f32[64,256]{1,0:T(8,128)S(1)} convert(s32[64,256]{1,0:T(8,128)} %param.6) | non-fusion elementwise | flops 16384 | bytes 131072 | tf_op jit(solution)/shard_map/convert_element_type | solution.py:313
  1.5 0.8 %pad_maximum_fusion.packed = f32[64,512]{1,0:T(8,128)S(1)} fusion(f32[64,256]{1,0:T(8,128)S(1)} %convert_element_type.3, f32[64,256]{1,0:T(8,128)} %param.5), kind=kLoop, calls=%fused_computation | loop fusion | flops 32768 | bytes 262144 | tf_op jit(solution)/shard_map/concatenate | solution.py:313
  2.4 0.5 %collective-permute-start = (f32[32,512]{1,0:T(8,128)S(1)}, f32[32,512]{1,0:T(8,128)S(1)}, u32[]{:S(2)}, u32[]{:S(2)}) collective-permute-start(f32[32,512]{1,0:T(8,128)S(1)} %get-tuple-element.21), channel_id=1, source_target_pairs={{0,1},{1,0},{2,3},{3,2},{4,5},{5,4},{6,7},{7,6},{8,9},{9,8},{10,11... | collective-permute-start | bytes 196616 | tf_op jit(solution)/shard_map/ppermute | solution.py:22
  2.9 0.7 %multiply_add_fusion.starts = s32[4]{0:T(128)S(1)} fusion(s32[4]{0:T(128)} %param.8, s32[4]{0:T(128)} %param.7), kind=kLoop, calls=%fused_computation.4 | loop fusion | flops 12 | bytes 48 | tf_op jit(solution)/shard_map/add | solution.py:311
  3.6 0.2 collective-permute-done.other
  3.8 0.7 %chip.1 = (f32[32,640]{1,0:T(8,128)S(1)}, f32[2,32,512]{2,1,0:T(8,128)S(1)}, f32[4,128]{1,0:T(4,128)S(1)}) custom-call(s32[4]{0:T(128)S(1)} %multiply_add_fusion.starts, f32[32,512]{1,0:T(8,128)S(1)} %get-tuple-element.20.own, f32[32,512]{1,0:T(8,128)S(1)} %collective-permute-done.other), custom_call_target="tpu_custom_call" | custom-call | flops 1000000 | bytes 1048576 | tf_op jit(solution)/shard_map/chip/pallas_call | solution.py:292
  4.5 5.0 %collective-permute-start.4 = (f32[32,640]{1,0:T(8,128)S(1)}, f32[32,640]{1,0:T(8,128)S(1)}, u32[]{:S(2)}, u32[]{:S(2)}) collective-permute-start(f32[32,640]{1,0:T(8,128)S(1)} %get-tuple-element.29.refs_0_), channel_id=1, source_target_pairs={{0,12},{1,13},{2,14},{3,15},{4,8},{5,9},{6,10},{7,11},{8,4},{9,5},... | collective-permute-start | bytes 245768 | tf_op jit(solution)/shard_map/ppermute | solution.py:22
  9.5 0.0 collective-permute-start.3
  9.5 0.6 %collective-permute-start.2 = (f32[32,640]{1,0:T(8,128)S(1)}, f32[32,640]{1,0:T(8,128)S(1)}, u32[]{:S(2)}, u32[]{:S(2)}) collective-permute-start(f32[32,640]{1,0:T(8,128)S(1)} %get-tuple-element.29.refs_0_), channel_id=1, source_target_pairs={{0,4},{1,5},{2,6},{3,7},{4,0},{5,1},{6,2},{7,3},{8,12},{9,13},{10,... | collective-permute-start | bytes 245768 | tf_op jit(solution)/shard_map/ppermute | solution.py:22
  10.2 4.7 %collective-permute-start.1 = (f32[32,256]{1,0:T(8,128)S(1)}, f32[32,256]{1,0:T(8,128)S(1)}, u32[]{:S(2)}, u32[]{:S(2)}) collective-permute-start(f32[32,256]{1,0:T(8,128)S(1)} %slice_bitcast_fusion), channel_id=1, source_target_pairs={{0,14},{1,15},{2,0},{3,1},{4,2},{5,3},{6,4},{7,5},{8,6},{9,7},{10,... | collective-permute-start | bytes 98312 | tf_op jit(solution)/shard_map/ppermute | solution.py:330
  14.9 3.5 %columns.2 = (bf16[2,32,256,256]{3,2,1,0:T(8,128)(2,1)S(1)}, f32[2,32,256]{2,1,0:T(8,128)S(1)}, f32[2,32,256]{2,1,0:T(8,128)S(1)}, bf16[1152,128]{1,0:T(8,128)(2,1)S(1)}) custom-call(f32[2,32,512]{2,1,0:T(8,128)S(1)} %get-tuple-element.22.both), custom_call_target="tpu_custom_call" | custom-call | flops 100000000 | bytes 1048576 | tf_op jit(solution)/shard_map/columns/pallas_call | solution.py:292
  18.4 0.0 collective-permute-done.1.following.after_too
  18.4 0.0 collective-permute-done.4.refs_3_
  18.4 0.0 collective-permute-done.3.refs_2_
  18.4 0.0 collective-permute-done.2.refs_1_
  18.5 0.3 windows.1.refs_0_
  18.8 0.1 collective-permute-start.5
  19.5 4.0 %columns.3 = (bf16[2,32,256,256]{3,2,1,0:T(8,128)(2,1)S(1)}, f32[2,32,256]{2,1,0:T(8,128)S(1)}, f32[2,32,256]{2,1,0:T(8,128)S(1)}, f32[128,256]{1,0:T(8,128)S(1)}, f32[8,256]{1,0:T(8,128)S(1)}) custom-call(s32[4]{0:T(128)S(1)} %multiply_add_fusion.starts, s32[1]{0:T(128)S(6)} %copy.13.excl, ...), custom_call_target="tpu_custom_call", output_to_operand_aliasing={{0}: (4, {}), {1}: (5, {}), {2}: (6, {})} | custom-call | flops 100000000 | bytes 1048576 | tf_op jit(solution)/shard_map/columns/pallas_call | solution.py:292
  23.5 0.7 %collective-permute-done.5.refs_1_ = f32[32,1280]{1,0:T(8,128)S(1)} collective-permute-done((f32[32,1280]{1,0:T(8,128)S(1)}, f32[32,1280]{1,0:T(8,128)S(1)}, u32[]{:S(2)}, u32[]{:S(2)}) %collective-permute-start.5) | collective-permute-done | bytes 163872 | tf_op jit(solution)/shard_map/ppermute | solution.py:22
  24.2 0.4 query_stats.1.y
  24.5 2.6 %other_core.1 = (f32[128,256]{1,0:T(8,128)S(1)}, bf16[32,128,256]{2,1,0:T(8,128)(2,1)S(1)}) custom-call(f32[32,1408]{1,0:T(8,128)S(1)} %query_stats.1.y, bf16[2,32,256,256]{3,2,1,0:T(8,128)(2,1)S(1)} %get-tuple-element.30.hankel, f32[2,32,256]{2,1,0:T(8,128)S(1)} %get-tuple-element.26.after.scale_ref, f32[2,32,256]{2,1,0:T(8,128)S(1)} %get-tuple-element.31.offset_ref), custom_call_target="tpu_custom_call" | custom-call | flops 1000000 | bytes 1048576 | tf_op jit(solution)/shard_map/other_core/pallas_call | solution.py:292
  27.1 0.1 collective-permute-start.6
  27.2 0.9 %own_core.1.own = f32[128,256]{1,0:T(8,128)S(1)} custom-call(f32[32,1408]{1,0:T(8,128)S(1)} %query_stats.1.y, bf16[32,128,256]{2,1,0:T(8,128)(2,1)S(1)} %get-tuple-element.32.windows_ref, bf16[2,32,256,256]{3,2,1,0:T(8,128)(2,1)S(1)} %get-tuple-element.30.hankel, f32[2,32,256]{2,1,0:T(8,128)S(1)} %get-tuple-element.26.after.scale_ref, ...), custom_call_target="tpu_custom_call" | custom-call | flops 500000000 | bytes 1048576 | tf_op jit(solution)/shard_map/own_core/pallas_call | solution.py:292
  28.1 0.4 %collective-permute-done.6.other = f32[128,256]{1,0:T(8,128)S(1)} collective-permute-done((f32[128,256]{1,0:T(8,128)S(1)}, f32[128,256]{1,0:T(8,128)S(1)}, u32[]{:S(2)}, u32[]{:S(2)}) %collective-permute-start.6) | collective-permute-done | bytes 131104 | tf_op jit(solution)/shard_map/ppermute | solution.py:22
  28.6 0.6 %minima.1 = (f32[4,32]{1,0:T(4,128)S(1)}, f32[1,256]{1,0:T(1,128)}) custom-call(f32[128,256]{1,0:T(8,128)S(1)} %own_core.1.own, f32[128,256]{1,0:T(8,128)S(1)} %collective-permute-done.6.other, f32[128,256]{1,0:T(8,128)S(1)} %get-tuple-element.34.banned, f32[8,256]{1,0:T(8,128)S(1)} %get-tuple-element.35.beyond), custom_call_target="tpu_custom_call" | custom-call | flops 1000000 | bytes 1048576 | tf_op jit(solution)/shard_map/minima/pallas_call | solution.py:292
  29.2 1.1 %collective-permute-start.9 = (f32[4,32]{1,0:T(4,128)S(1)}, f32[4,32]{1,0:T(4,128)S(1)}, u32[]{:S(2)}, u32[]{:S(2)}) collective-permute-start(f32[4,32]{1,0:T(4,128)S(1)} %get-tuple-element.36), channel_id=1, source_target_pairs={{0,3},{1,2},{2,1},{3,0},{4,7},{5,6},{6,5},{7,4},{8,11},{9,10},{10,... | collective-permute-start | bytes 1544 | tf_op jit(solution)/shard_map/ppermute | solution.py:22
  30.2 0.7 %collective-permute-start.8 = (f32[4,32]{1,0:T(4,128)S(1)}, f32[4,32]{1,0:T(4,128)S(1)}, u32[]{:S(2)}, u32[]{:S(2)}) collective-permute-start(f32[4,32]{1,0:T(4,128)S(1)} %get-tuple-element.36), channel_id=1, source_target_pairs={{0,2},{1,3},{2,0},{3,1},{4,6},{5,7},{6,4},{7,5},{8,10},{9,11},{10,... | collective-permute-start | bytes 1544 | tf_op jit(solution)/shard_map/ppermute | solution.py:22
  30.9 0.1 collective-permute-start.7
  31.0 1.1 %collective-permute-done.9 = f32[4,32]{1,0:T(4,128)S(1)} collective-permute-done((f32[4,32]{1,0:T(4,128)S(1)}, f32[4,32]{1,0:T(4,128)S(1)}, u32[]{:S(2)}, u32[]{:S(2)}) %collective-permute-start.9) | collective-permute-done | bytes 544 | tf_op jit(solution)/shard_map/ppermute | solution.py:22
  32.2 1.7 %collective-permute-done.8 = f32[4,32]{1,0:T(4,128)S(1)} collective-permute-done((f32[4,32]{1,0:T(4,128)S(1)}, f32[4,32]{1,0:T(4,128)S(1)}, u32[]{:S(2)}, u32[]{:S(2)}) %collective-permute-start.8) | collective-permute-done | bytes 544 | tf_op jit(solution)/shard_map/ppermute | solution.py:22
  33.8 0.0 collective-permute-done.7
  33.9 0.1 collective-permute-start.12
  33.9 1.7 %collective-permute-start.11 = (f32[4,32]{1,0:T(4,128)S(1)}, f32[4,32]{1,0:T(4,128)S(1)}, u32[]{:S(2)}, u32[]{:S(2)}) collective-permute-start(f32[4,32]{1,0:T(4,128)S(1)} %minimum_minimum_fusion.1), channel_id=1, source_target_pairs={{0,13},{1,12},{2,15},{3,14},{4,9},{5,8},{6,11},{7,10},{8,5},{9,4},... | collective-permute-start | bytes 1544 | tf_op jit(solution)/shard_map/ppermute | solution.py:22
  35.7 0.8 %collective-permute-start.10 = (f32[4,32]{1,0:T(4,128)S(1)}, f32[4,32]{1,0:T(4,128)S(1)}, u32[]{:S(2)}, u32[]{:S(2)}) collective-permute-start(f32[4,32]{1,0:T(4,128)S(1)} %minimum_minimum_fusion.1), channel_id=1, source_target_pairs={{0,5},{1,4},{2,7},{3,6},{4,1},{5,0},{6,3},{7,2},{8,13},{9,12},{10,... | collective-permute-start | bytes 1544 | tf_op jit(solution)/shard_map/ppermute | solution.py:22
  36.5 1.4 %collective-permute-done.12 = f32[4,32]{1,0:T(4,128)S(1)} collective-permute-done((f32[4,32]{1,0:T(4,128)S(1)}, f32[4,32]{1,0:T(4,128)S(1)}, u32[]{:S(2)}, u32[]{:S(2)}) %collective-permute-start.12) | collective-permute-done | bytes 544 | tf_op jit(solution)/shard_map/ppermute | solution.py:22
  37.8 1.0 %collective-permute-done.11 = f32[4,32]{1,0:T(4,128)S(1)} collective-permute-done((f32[4,32]{1,0:T(4,128)S(1)}, f32[4,32]{1,0:T(4,128)S(1)}, u32[]{:S(2)}, u32[]{:S(2)}) %collective-permute-start.11) | collective-permute-done | bytes 544 | tf_op jit(solution)/shard_map/ppermute | solution.py:22
  38.8 0.0 collective-permute-done.10
  38.8 0.6 %minimum_minimum_fusion = f32[4,32]{1,0:T(4,128)} fusion(f32[4,32]{1,0:T(4,128)S(1)} %collective-permute-done.12, f32[4,32]{1,0:T(4,128)S(1)} %collective-permute-done.11, f32[4,32]{1,0:T(4,128)S(1)} %minimum_minimum_fusion.1, f32[4,32]{1,0:T(4,128)S(1)} %collective-permute-done.10), kind=kLoop, calls=%fused_computation.2 | loop fusion | flops 384 | bytes 2560 | tf_op jit(solution)/shard_map/min | solution.py:410
  (3 shorter events, 0.0 us)
Async XLA Ops:
  2.4 1.4 %collective-permute-start = (f32[32,512]{1,0:T(8,128)S(1)}, f32[32,512]{1,0:T(8,128)S(1)}, u32[]{:S(2)}, u32[]{:S(2)}) collective-permute-start(f32[32,512]{1,0:T(8,128)S(1)} %get-tuple-element.21), channel_id=1, source_target_pairs={{0,1},{1,0},{2,3},{3,2},{4,5},{5,4},{6,7},{7,6},{8,9},{9,8},{10,11... | collective-permute-start | bytes 196616 | tf_op jit(solution)/shard_map/ppermute | solution.py:22
  4.5 13.9 %collective-permute-start.4 = (f32[32,640]{1,0:T(8,128)S(1)}, f32[32,640]{1,0:T(8,128)S(1)}, u32[]{:S(2)}, u32[]{:S(2)}) collective-permute-start(f32[32,640]{1,0:T(8,128)S(1)} %get-tuple-element.29.refs_0_), channel_id=1, source_target_pairs={{0,12},{1,13},{2,14},{3,15},{4,8},{5,9},{6,10},{7,11},{8,4},{9,5},... | collective-permute-start | bytes 245768 | tf_op jit(solution)/shard_map/ppermute | solution.py:22
  9.5 8.9 %collective-permute-start.3 = (f32[32,640]{1,0:T(8,128)S(1)}, f32[32,640]{1,0:T(8,128)S(1)}, u32[]{:S(2)}, u32[]{:S(2)}) collective-permute-start(f32[32,640]{1,0:T(8,128)S(1)} %get-tuple-element.29.refs_0_), channel_id=1, source_target_pairs={{0,8},{1,9},{2,10},{3,11},{4,12},{5,13},{6,14},{7,15},{8,0},{9,1},... | collective-permute-start | bytes 245768 | tf_op jit(solution)/shard_map/ppermute | solution.py:22
  9.5 8.9 %collective-permute-start.2 = (f32[32,640]{1,0:T(8,128)S(1)}, f32[32,640]{1,0:T(8,128)S(1)}, u32[]{:S(2)}, u32[]{:S(2)}) collective-permute-start(f32[32,640]{1,0:T(8,128)S(1)} %get-tuple-element.29.refs_0_), channel_id=1, source_target_pairs={{0,4},{1,5},{2,6},{3,7},{4,0},{5,1},{6,2},{7,3},{8,12},{9,13},{10,... | collective-permute-start | bytes 245768 | tf_op jit(solution)/shard_map/ppermute | solution.py:22
  10.2 8.2 %collective-permute-start.1 = (f32[32,256]{1,0:T(8,128)S(1)}, f32[32,256]{1,0:T(8,128)S(1)}, u32[]{:S(2)}, u32[]{:S(2)}) collective-permute-start(f32[32,256]{1,0:T(8,128)S(1)} %slice_bitcast_fusion), channel_id=1, source_target_pairs={{0,14},{1,15},{2,0},{3,1},{4,2},{5,3},{6,4},{7,5},{8,6},{9,7},{10,... | collective-permute-start | bytes 98312 | tf_op jit(solution)/shard_map/ppermute | solution.py:330
  18.8 5.4 %collective-permute-start.5 = (f32[32,1280]{1,0:T(8,128)S(1)}, f32[32,1280]{1,0:T(8,128)S(1)}, u32[]{:S(2)}, u32[]{:S(2)}) collective-permute-start(f32[32,1280]{1,0:T(8,128)S(1)} %windows.1.refs_0_), channel_id=1, source_target_pairs={{0,2},{1,3},{2,0},{3,1},{4,6},{5,7},{6,4},{7,5},{8,10},{9,11},{10,... | collective-permute-start | bytes 491528 | tf_op jit(solution)/shard_map/ppermute | solution.py:22
  27.1 1.4 %collective-permute-start.6 = (f32[128,256]{1,0:T(8,128)S(1)}, f32[128,256]{1,0:T(8,128)S(1)}, u32[]{:S(2)}, u32[]{:S(2)}) collective-permute-start(f32[128,256]{1,0:T(8,128)S(1)} %get-tuple-element.33), channel_id=1, source_target_pairs={{0,1},{1,0},{2,3},{3,2},{4,5},{5,4},{6,7},{7,6},{8,9},{9,8},{10,11... | collective-permute-start | bytes 393224 | tf_op jit(solution)/shard_map/ppermute | solution.py:22
  29.2 3.0 %collective-permute-start.9 = (f32[4,32]{1,0:T(4,128)S(1)}, f32[4,32]{1,0:T(4,128)S(1)}, u32[]{:S(2)}, u32[]{:S(2)}) collective-permute-start(f32[4,32]{1,0:T(4,128)S(1)} %get-tuple-element.36), channel_id=1, source_target_pairs={{0,3},{1,2},{2,1},{3,0},{4,7},{5,6},{6,5},{7,4},{8,11},{9,10},{10,... | collective-permute-start | bytes 1544 | tf_op jit(solution)/shard_map/ppermute | solution.py:22
  30.2 3.6 %collective-permute-start.8 = (f32[4,32]{1,0:T(4,128)S(1)}, f32[4,32]{1,0:T(4,128)S(1)}, u32[]{:S(2)}, u32[]{:S(2)}) collective-permute-start(f32[4,32]{1,0:T(4,128)S(1)} %get-tuple-element.36), channel_id=1, source_target_pairs={{0,2},{1,3},{2,0},{3,1},{4,6},{5,7},{6,4},{7,5},{8,10},{9,11},{10,... | collective-permute-start | bytes 1544 | tf_op jit(solution)/shard_map/ppermute | solution.py:22
  30.9 2.9 %collective-permute-start.7 = (f32[4,32]{1,0:T(4,128)S(1)}, f32[4,32]{1,0:T(4,128)S(1)}, u32[]{:S(2)}, u32[]{:S(2)}) collective-permute-start(f32[4,32]{1,0:T(4,128)S(1)} %get-tuple-element.36), channel_id=1, source_target_pairs={{0,1},{1,0},{2,3},{3,2},{4,5},{5,4},{6,7},{7,6},{8,9},{9,8},{10,11... | collective-permute-start | bytes 1544 | tf_op jit(solution)/shard_map/ppermute | solution.py:22
  33.9 4.0 %collective-permute-start.12 = (f32[4,32]{1,0:T(4,128)S(1)}, f32[4,32]{1,0:T(4,128)S(1)}, u32[]{:S(2)}, u32[]{:S(2)}) collective-permute-start(f32[4,32]{1,0:T(4,128)S(1)} %minimum_minimum_fusion.1), channel_id=1, source_target_pairs={{0,9},{1,8},{2,11},{3,10},{4,13},{5,12},{6,15},{7,14},{8,1},{9,0},... | collective-permute-start | bytes 1544 | tf_op jit(solution)/shard_map/ppermute | solution.py:22
  33.9 4.9 %collective-permute-start.11 = (f32[4,32]{1,0:T(4,128)S(1)}, f32[4,32]{1,0:T(4,128)S(1)}, u32[]{:S(2)}, u32[]{:S(2)}) collective-permute-start(f32[4,32]{1,0:T(4,128)S(1)} %minimum_minimum_fusion.1), channel_id=1, source_target_pairs={{0,13},{1,12},{2,15},{3,14},{4,9},{5,8},{6,11},{7,10},{8,5},{9,4},... | collective-permute-start | bytes 1544 | tf_op jit(solution)/shard_map/ppermute | solution.py:22
  35.7 3.2 %collective-permute-start.10 = (f32[4,32]{1,0:T(4,128)S(1)}, f32[4,32]{1,0:T(4,128)S(1)}, u32[]{:S(2)}, u32[]{:S(2)}) collective-permute-start(f32[4,32]{1,0:T(4,128)S(1)} %minimum_minimum_fusion.1), channel_id=1, source_target_pairs={{0,5},{1,4},{2,7},{3,6},{4,1},{5,0},{6,3},{7,2},{8,13},{9,12},{10,... | collective-permute-start | bytes 1544 | tf_op jit(solution)/shard_map/ppermute | solution.py:22

commit v4 on v3

--- a/solution.py
+++ b/solution.py
@@ -40,18 +40,25 @@
 
 
 def half_rows(ref, which):
-    half = ref.shape[0] // CORES
+    half = ref.shape[0]
     return pl.ds(pl.multiple_of(which * half, half), half)
 
 
 def share_kernel(packed, keep, send):
     core = lax.rem(lax.axis_index("col"), CORES)
-    keep[...] = packed[half_rows(packed, core), :]
-    send[...] = packed[half_rows(packed, 1 - core), :]
-
-
-def chip_kernel(starts, own, other, out, both, starts_out):
-    turns = starts.shape[0]
+    width = packed.shape[2]
+    for which, out in ((core, keep), (1 - core, send)):
+        for i in range(packed.shape[0]):
+            out[:, i * width : (i + 1) * width] = packed[i, half_rows(out, which), :]
+
+
+def first_lane(ref):
+    return [jnp.max(ref[row : row + 1, :]).astype(jnp.int32) for row in range(ref.shape[0])]
+
+
+def chip_kernel(starts_ref, own, other, out, both):
+    turns = starts_ref.shape[0]
+    starts = first_lane(starts_ref)
     half, width = own.shape[0], own.shape[1] // 2
     here = lax.axis_index("col")
     core = lax.rem(here, CORES)
@@ -63,8 +70,6 @@
     for i in range(CORES):
         high, mid, low = (turned[(3 * i + j) * half : (3 * i + j + 1) * half] for j in range(3))
         out[:, i * width : (i + 1) * width] = low + mid + high
-    for turn in range(turns):
-        starts_out[turn : turn + 1, :] = jnp.full((1, LANES), starts[turn].astype(f32))
     both[core] = own[...]
     both[1 - core] = other[...]
     lane = lax.broadcasted_iota(jnp.int32, (half, LANES), 1)
@@ -88,7 +93,7 @@
 def windows_kernel(masks, starts_ref, after, after_too, *refs):
     parts, out, lines = refs[: len(masks)], refs[len(masks)], refs[len(masks) + 1]
     turns = starts_ref.shape[0]
-    starts = [jnp.max(starts_ref[turn : turn + 1, :]).astype(jnp.int32) for turn in range(turns)]
+    starts = first_lane(starts_ref)
     half, width = out.shape[0], lines.shape[1]
     here = lax.axis_index("col")
     for i, part in enumerate(parts):
@@ -181,39 +186,46 @@
     return jnp.where(inside, 1.0, 0.0).astype(bf16)
 
 
-def segment_columns(own, following, hankel, scale_ref, offset_ref):
+def column_band(shape):
+    row = lax.broadcasted_iota(jnp.int32, shape, 0)
+    col = lax.broadcasted_iota(jnp.int32, shape, 1)
+    return jnp.where((row >= col) & (row < col + M), 1.0, 0.0).astype(bf16)
+
+
+def segment_columns(own, following, band, hankel, scale_ref, offset_ref):
     width = scale_ref.shape[1]
     samples = own[:, :width]
     centre = jnp.sum(samples, axis=1, keepdims=True) * (1.0 / width)
     extended = jnp.concatenate([samples - centre, following[:, :width] - centre], axis=1)
     length = extended.shape[1]
-    first, second = extended, extended * extended
-    step = 1
-    while step < M:
-        first = first + pltpu.roll(first, length - step, 1)
-        second = second + pltpu.roll(second, length - step, 1)
-        step *= 2
-    mean = first[:, :width] * (1.0 / M)
-    spread = second[:, :width] * (1.0 / M) - mean * mean
+    channels = extended.shape[0]
+    stack = jnp.concatenate([*split3(extended), *split3(extended * extended)], axis=0)
+    sums = jnp.dot(stack, band[...], preferred_element_type=f32)
+    first, first_mid, first_low, second, second_mid, second_low = (
+        sums[i * channels : (i + 1) * channels] for i in range(6)
+    )
+    mean = (first_low + first_mid + first) * (1.0 / M)
+    spread = (second_low + second_mid + second) * (1.0 / M) - mean * mean
     scale = own[:, width:] / jnp.sqrt(jnp.maximum(spread, 0.0) + 1e-05)
     scale_ref[...] = scale
     offset_ref[...] = mean * scale
-    for c in range(extended.shape[0]):
-        base = jnp.broadcast_to(extended[c : c + 1, :], (16, length))
-        base = pltpu.roll(base, length - 15, 1, stride=1, stride_axis=0).astype(bf16)
-        for b in range(M // 16):
-            shift = M - 16 - 16 * b
-            block = pltpu.roll(base, length - shift, 1) if shift else base
-            hankel[c, 16 * b : 16 * (b + 1), :] = block[:, :width]
-
-
-def first_columns_kernel(both, hankel, scale_ref, offset_ref, band_ref):
+    for c in range(channels):
+        base = jnp.broadcast_to(extended[c : c + 1, :], (LANES, length))
+        base = pltpu.roll(base, length - LANES + 1, 1, stride=1, stride_axis=0).astype(bf16)
+        for high in range(M // LANES):
+            at = M - LANES - high * LANES
+            hankel[c, at : at + LANES, :] = base[:, high * LANES : high * LANES + width]
+
+
+def first_columns_kernel(both, hankel, scale_ref, offset_ref, band_ref, sums_ref, spread_ref):
+    spread_ref[...] = spread_matrix(spread_ref.shape)
     band_ref[...] = band_matrix(band_ref.shape)
-    segment_columns(both.at[0], both.at[1], hankel.at[0], scale_ref.at[0], offset_ref.at[0])
+    sums_ref[...] = column_band(sums_ref.shape)
+    segment_columns(both.at[0], both.at[1], sums_ref, hankel.at[0], scale_ref.at[0], offset_ref.at[0])
 
 
 def second_columns_kernel(
-    limit, starts, excl, both, following, hankel_in, scale_in, offset_in, hankel, scale_ref, offset_ref, banned, beyond
+    limit, starts, excl, both, following, sums_ref, hankel_in, scale_in, offset_in, hankel, scale_ref, offset_ref, banned, beyond
 ):
     width = banned.shape[1]
     columns = lax.axis_index("col") * width + lax.broadcasted_iota(jnp.int32, (QB, width), 1)
@@ -223,16 +235,33 @@
         near = jnp.where(jnp.abs(apart + starts[turn]) < excl[0], 1.0, last)
         banned[turn * QB : (turn + 1) * QB, :] = near
     beyond[...] = last[:8]
-    segment_columns(both.at[1], following, hankel.at[1], scale_ref.at[1], offset_ref.at[1])
-
-
-def other_core_kernel(turns, y, hankel, scale_ref, offset_ref, out, windows_ref):
+    segment_columns(both.at[1], following, sums_ref, hankel.at[1], scale_ref.at[1], offset_ref.at[1])
+
+
+def spread_matrix(shape):
+    row = lax.broadcasted_iota(jnp.int32, shape, 0)
+    tile = lax.broadcasted_iota(jnp.int32, shape, 1) // LANES
+    channels = shape[0] // 2
+    return jnp.where((row == tile) | (row == tile + channels), 1.0, 0.0).astype(bf16)
+
+
+def covariances(offsets, windows_ref, hankel, scale_ref, offset_ref, which):
+    acc = -M * jnp.dot(offsets, offset_ref[which], preferred_element_type=f32, precision=lax.Precision.HIGHEST)
+    for c in range(windows_ref.shape[0]):
+        products = jnp.dot(windows_ref[c], hankel[which, c], preferred_element_type=f32)
+        acc = acc + products * scale_ref[which, c : c + 1, :]
+    return acc
+
+
+def other_core_kernel(turns, y, spread_ref, hankel, scale_ref, offset_ref, out, windows_ref, scales):
     queries = turns * QB
     samples = turns * (M + QB)
     per_tile = LANES // QB
-    which = 1 - lax.rem(lax.axis_index("col"), CORES)
     by_query = jnp.transpose(y[:, samples : samples + queries])
     offsets = jnp.transpose(y[:, samples + queries : samples + 2 * queries])
+    high = by_query.astype(bf16)
+    low = (by_query - high.astype(f32)).astype(bf16)
+    scales[...] = jnp.dot(jnp.concatenate([high, low], axis=1), spread_ref[...], preferred_element_type=f32)
     lines = []
     for turn in range(turns):
         at = turns * M + (turn // per_tile) * LANES
@@ -240,15 +269,16 @@
         if turn % per_tile:
             tail = pltpu.roll(tail, LANES - (turn % per_tile) * QB, 1)
         lines.append(jnp.concatenate([y[:, turn * M : (turn + 1) * M], tail], axis=1))
-    length = M + LANES
+    which = 1 - lax.rem(lax.axis_index("col"), CORES)
     acc = -M * jnp.dot(offsets, offset_ref[which], preferred_element_type=f32, precision=lax.Precision.HIGHEST)
     for c in range(y.shape[0]):
-        scale = by_query[:, c : c + 1]
         windows = []
         for turn in range(turns):
-            row = jnp.broadcast_to(lines[turn][c : c + 1, :], (QB, length))
-            row = pltpu.roll(row, length - QB, 1, stride=1, stride_axis=0)
-            windows.append((row[:, :M] * scale[turn * QB : (turn + 1) * QB]).astype(bf16))
+            row = jnp.broadcast_to(lines[turn][c : c + 1, :], (QB, M + LANES))
+            row = pltpu.roll(row, M + LANES - QB, 1, stride=1, stride_axis=0)
+            scale = scales[turn * QB : (turn + 1) * QB, c * LANES : (c + 1) * LANES]
+            scaled = [row[:, k : k + LANES] * scale for k in range(0, M, LANES)]
+            windows.append(jnp.concatenate(scaled, axis=1).astype(bf16))
         windows = jnp.concatenate(windows, axis=0)
         windows_ref[c] = windows
         products = jnp.dot(windows, hankel[which, c], preferred_element_type=f32)
@@ -259,13 +289,9 @@
 def own_core_kernel(turns, y, windows_ref, hankel, scale_ref, offset_ref, out):
     queries = turns * QB
     at = turns * (M + QB) + queries
+    offsets = jnp.transpose(y[:, at : at + queries])
     which = lax.rem(lax.axis_index("col"), CORES)
-    offsets = jnp.transpose(y[:, at : at + queries])
-    acc = -M * jnp.dot(offsets, offset_ref[which], preferred_element_type=f32, precision=lax.Precision.HIGHEST)
-    for c in range(y.shape[0]):
-        products = jnp.dot(windows_ref[c], hankel[which, c], preferred_element_type=f32)
-        acc = acc + products * scale_ref[which, c : c + 1, :]
-    out[...] = acc
+    out[...] = covariances(offsets, windows_ref, hankel, scale_ref, offset_ref, which)
 
 
 def minima_kernel(turns, channels, own, other, banned, beyond, row_out, col_out):
@@ -309,20 +335,21 @@
     queries = turns * QB
     limit = seg_len * devices_col - M
     starts = owners * seg_len + blocks * QB
-
-    packed = jnp.concatenate([series, valid.astype(f32)], axis=1)
+    starts_vector = jnp.broadcast_to(starts.astype(f32)[:, None], (turns, LANES))
+
+    which = lax.broadcasted_iota(jnp.int32, (2, *series.shape), 0)
+    packed = jnp.where(which == 0, series[None], valid[None].astype(f32))
     part = jax.ShapeDtypeStruct((half, 2 * seg_len), f32)
     keep, send = call(share_kernel, "share", [part] * 2, "v", packed)
-    chip, both, starts_vector = call(
+    chip, both = call(
         chip_kernel,
         "chip",
         [
             jax.ShapeDtypeStruct((half, 2 * seg_len + queries), f32),
             jax.ShapeDtypeStruct((CORES, half, 2 * seg_len), f32),
-            jax.ShapeDtypeStruct((turns, LANES), f32),
         ],
-        "svv",
-        starts,
+        "vvv",
+        starts_vector,
         keep,
         exchanged(send, 1),
     )
@@ -335,7 +362,11 @@
         jax.ShapeDtypeStruct((CORES, half, seg_len), f32),
     ]
     band = jax.ShapeDtypeStruct((LANES // QB * (M + QB), LANES), bf16)
-    *columns, band = call(first_columns_kernel, "columns", [*side, band], "v", both, flops=10**8)
+    sums = jax.ShapeDtypeStruct((2 * seg_len, seg_len), bf16)
+    spread = jax.ShapeDtypeStruct((2 * half, half * LANES), bf16)
+    *columns, band, sums, spread = call(
+        first_columns_kernel, "columns", [*side, band, sums, spread], "v", both, flops=10**8
+    )
 
     rounds = rounds_from(BASE, devices_col)
     masks = [0, *rounds[0]]
@@ -357,13 +388,14 @@
         functools.partial(second_columns_kernel, limit),
         "columns",
         [*side, jax.ShapeDtypeStruct((queries, seg_len), f32), jax.ShapeDtypeStruct((8, seg_len), f32)],
-        "ssvvaaa",
+        "ssvvvaaa",
         starts,
         excl,
         both,
         following,
+        sums,
         *columns,
-        input_output_aliases={4: 0, 5: 1, 6: 2},
+        input_output_aliases={5: 0, 6: 1, 7: 2},
         flops=10**8,
     )
     queried = call(
@@ -381,9 +413,11 @@
         functools.partial(other_core_kernel, turns),
         "other_core",
         [partial, jax.ShapeDtypeStruct((half, queries, M), bf16)],
-        "vvvv",
+        "vvvvv",
         queried,
+        spread,
         *columns,
+        scratch_shapes=[pltpu.VMEM((queries, half * LANES), f32)],
     )
     mine = call(
         functools.partial(own_core_kernel, turns),

time: 39.7 us -> 38.9 us (0.980)
  Pallas kernels: 13 us -> 7.68 us
  starting transfers between devices: 15.5 us -> 18.1 us
  waiting for transfers between devices: 6.53 us -> 8.11 us
    pallas_call x9, Pallas kernels: 13 us -> 7.68 us  [call(): pl.pallas_call(kernel, out_shape=out_shape, in_specs=[SPECS[space] for sp...]
    ppermute x12, starting transfers between devices: 10.8 us -> 13.4 us  [exchanged(): return lax.ppermute(block, 'col', [(i, i ^ mask) for i in devices])]
    ppermute x12, waiting for transfers between devices: 6.53 us -> 7.91 us  [exchanged(): return lax.ppermute(block, 'col', [(i, i ^ mask) for i in devices])]
    select_n x0 -> x1, other arithmetic: none -> 0.92 us  [shards(): packed = jnp.where(which == 0, series[None], valid[None].astype(f32))]
    concatenate x1 -> x0, other arithmetic: 0.85 us -> none  [shards(): packed = jnp.concatenate([series, valid.astype(f32)], axis=1)]
    convert_element_type x1 -> x2, other arithmetic: 0.85 us -> 1.52 us  [the longest x1 0.85 us: shards(): packed = jnp.where(which == 0, series[None], valid[None].astype(f32))]
    add x1 -> x0, other arithmetic: 0.67 us -> none  [shards(): starts = owners * seg_len + blocks * QB]
  transfers between devices with their start and end apart: 13 -> 13, of which waited for: 7 -> 9; matrix products, arithmetic and copies ran while one was open for 2% -> 2% of each run, Pallas kernels for 21% -> 11%
where the time goes in v4:
time: 38.9 us; the launch traced here: 38.4 us
  starting transfers between devices  18.1 us (47%)
  waiting for transfers between devices  8.11 us (21%)
  Pallas kernels  7.68 us (20%)
  other arithmetic  3.04 us (8%)
  between operations  1.37 us (4%)
    ppermute x12, starting transfers between devices, exchanged(): return lax.ppermute(block, 'col', [(i, i ^ mask) for i in devices])  13.4 us
    ppermute x12, waiting for transfers between devices, exchanged(): return lax.ppermute(block, 'col', [(i, i ^ mask) for i in devices])  7.91 us
    pallas_call x9, Pallas kernels, call(): pl.pallas_call(kernel, out_shape=out_shape, in_specs=[SPECS[space] for sp...  7.68 us
    ppermute x1, starting transfers between devices, shards(): following = lax.ppermute(both[0, :, :seg_len], 'col', back)  4.7 us
    select_n x1, other arithmetic, shards(): packed = jnp.where(which == 0, series[None], valid[None].astype(f32))  0.92 us
    convert_element_type x1, other arithmetic, shards(): packed = jnp.where(which == 0, series[None], valid[None].astype(f32))  0.85 us
  transfers between devices with their start and end apart: 13, of which 9 were waited for; matrix products, arithmetic and copies ran while one was open for 2% of the time, Pallas kernels for 11%

profile of v4, /device:TPU:0, one launch (start us, length us, event | category | flops | bytes accessed | tf_op | source)
XLA Modules:
  0.0 38.4 jit_solution(1845882755551156436)
XLA Ops:
  0.6 0.8 %convert_element_type.8 = f32[64,256]{1,0:T(8,128)S(1)} convert(s32[64,256]{1,0:T(8,128)} %param.6) | non-fusion elementwise | flops 16384 | bytes 131072 | tf_op jit(solution)/shard_map/convert_element_type | solution.py:341
  1.5 0.9 %broadcast_select_fusion.packed = f32[2,64,256]{2,1,0:T(8,128)S(1)} fusion(f32[64,256]{1,0:T(8,128)S(1)} %convert_element_type.8, f32[64,256]{1,0:T(8,128)} %param.5, pred[2]{0:T(512)(128)(4,1)S(1)} %iota_compare_fusion), kind=kLoop, calls=%fused_computation | loop fusion | flops 32768 | bytes 262146 | tf_op jit(solution)/shard_map/jit(_where)/select_n | solution.py:341
  2.4 0.5 %collective-permute-start = (f32[32,512]{1,0:T(8,128)S(1)}, f32[32,512]{1,0:T(8,128)S(1)}, u32[]{:S(2)}, u32[]{:S(2)}) collective-permute-start(f32[32,512]{1,0:T(8,128)S(1)} %get-tuple-element.22), channel_id=1, source_target_pairs={{0,1},{1,0},{2,3},{3,2},{4,5},{5,4},{6,7},{7,6},{8,9},{9,8},{10,11... | collective-permute-start | bytes 196616 | tf_op jit(solution)/shard_map/ppermute | solution.py:22
  3.0 0.7 %fusion = (f32[4]{0:T(128)S(1)}, s32[4]{0:T(128)S(1)}) fusion(s32[4]{0:T(128)} %param.8, s32[4]{0:T(128)} %param.7), kind=kLoop, calls=%fused_computation.6 | loop fusion | flops 16 | bytes 64 | tf_op jit(solution)/shard_map/convert_element_type | solution.py:338
  3.6 0.2 collective-permute-done.other
  3.9 0.1 broadcast_in_dim.24.starts_ref
  3.9 0.3 chip.1
  4.2 5.0 %collective-permute-start.4 = (f32[32,640]{1,0:T(8,128)S(1)}, f32[32,640]{1,0:T(8,128)S(1)}, u32[]{:S(2)}, u32[]{:S(2)}) collective-permute-start(f32[32,640]{1,0:T(8,128)S(1)} %get-tuple-element.30.refs_0_), channel_id=1, source_target_pairs={{0,12},{1,13},{2,14},{3,15},{4,8},{5,9},{6,10},{7,11},{8,4},{9,5},... | collective-permute-start | bytes 245768 | tf_op jit(solution)/shard_map/ppermute | solution.py:22
  9.3 0.0 collective-permute-start.3
  9.3 0.6 %collective-permute-start.2 = (f32[32,640]{1,0:T(8,128)S(1)}, f32[32,640]{1,0:T(8,128)S(1)}, u32[]{:S(2)}, u32[]{:S(2)}) collective-permute-start(f32[32,640]{1,0:T(8,128)S(1)} %get-tuple-element.30.refs_0_), channel_id=1, source_target_pairs={{0,4},{1,5},{2,6},{3,7},{4,0},{5,1},{6,2},{7,3},{8,12},{9,13},{10,... | collective-permute-start | bytes 245768 | tf_op jit(solution)/shard_map/ppermute | solution.py:22
  9.9 4.7 %collective-permute-start.1 = (f32[32,256]{1,0:T(8,128)S(1)}, f32[32,256]{1,0:T(8,128)S(1)}, u32[]{:S(2)}, u32[]{:S(2)}) collective-permute-start(f32[32,256]{1,0:T(8,128)S(1)} %slice_bitcast_fusion), channel_id=1, source_target_pairs={{0,14},{1,15},{2,0},{3,1},{4,2},{5,3},{6,4},{7,5},{8,6},{9,7},{10,... | collective-permute-start | bytes 98312 | tf_op jit(solution)/shard_map/ppermute | solution.py:357
  14.6 1.4 %columns.2 = (bf16[2,32,256,256]{3,2,1,0:T(8,128)(2,1)S(1)}, f32[2,32,256]{2,1,0:T(8,128)S(1)}, f32[2,32,256]{2,1,0:T(8,128)S(1)}, bf16[1152,128]{1,0:T(8,128)(2...) custom-call(f32[2,32,512]{2,1,0:T(8,128)S(1)} %get-tuple-element.23.both), custom_call_target="tpu_custom_call" | custom-call | flops 100000000 | bytes 1048576 | tf_op jit(solution)/shard_map/columns/pallas_call | solution.py:318
  16.0 0.2 collective-permute-done.1.following.after_too
  16.2 0.0 collective-permute-done.4.refs_3_
  16.2 0.6 %collective-permute-done.3.refs_2_ = f32[32,640]{1,0:T(8,128)S(1)} collective-permute-done((f32[32,640]{1,0:T(8,128)S(1)}, f32[32,640]{1,0:T(8,128)S(1)}, u32[]{:S(2)}, u32[]{:S(2)}) %collective-permute-start.3) | collective-permute-done | bytes 81952 | tf_op jit(solution)/shard_map/ppermute | solution.py:22
  16.8 0.0 collective-permute-done.2.refs_1_
  16.8 0.3 windows.1.refs_0_
  17.1 1.2 %collective-permute-start.5 = (f32[32,1280]{1,0:T(8,128)S(1)}, f32[32,1280]{1,0:T(8,128)S(1)}, u32[]{:S(2)}, u32[]{:S(2)}) collective-permute-start(f32[32,1280]{1,0:T(8,128)S(1)} %windows.1.refs_0_), channel_id=1, source_target_pairs={{0,2},{1,3},{2,0},{3,1},{4,6},{5,7},{6,4},{7,5},{8,10},{9,11},{10,... | collective-permute-start | bytes 491528 | tf_op jit(solution)/shard_map/ppermute | solution.py:22
  19.0 1.8 %columns.3 = (bf16[2,32,256,256]{3,2,1,0:T(8,128)(2,1)S(1)}, f32[2,32,256]{2,1,0:T(8,128)S(1)}, f32[2,32,256]{2,1,0:T(8,128)S(1)}, f32[128,256]{1,0:T(8,128)S(1)}, f32[8,256]{1,0:T(8,128)S(1)}) custom-call(s32[4]{0:T(128)S(1)} %get-tuple-element.41.starts, s32[1]{0:T(128)S(6)} %copy.13.excl, ...), custom_call_target="tpu_custom_call", output_to_operand_aliasing={{0}: (5, {}), {1}: (6, {}), {2}: (7, {})} | custom-call | flops 100000000 | bytes 1048576 | tf_op jit(solution)/shard_map/columns/pallas_call | solution.py:318
  20.8 1.7 %collective-permute-done.5.refs_1_ = f32[32,1280]{1,0:T(8,128)S(1)} collective-permute-done((f32[32,1280]{1,0:T(8,128)S(1)}, f32[32,1280]{1,0:T(8,128)S(1)}, u32[]{:S(2)}, u32[]{:S(2)}) %collective-permute-start.5) | collective-permute-done | bytes 163872 | tf_op jit(solution)/shard_map/ppermute | solution.py:22
  22.5 0.4 query_stats.1.y
  22.9 2.0 %other_core.1 = (f32[128,256]{1,0:T(8,128)S(1)}, bf16[32,128,256]{2,1,0:T(8,128)(2,1)S(1)}) custom-call(f32[32,1408]{1,0:T(8,128)S(1)} %query_stats.1.y, bf16[64,4096]{1,0:T(8,128)(2,1)S(1)} %get-tuple-element.31.spread_ref, bf16[2,32,256,256]{3,2,1,0:T(8,128)(2,1)S(1)} %get-tuple-element.32.hankel, f32[2,32,256]{2,1,0:T(8,128)S(1)} %get-tuple-element.28.after.scale_ref, ...), custom_call_target="tpu_custom_call" | custom-call | flops 1000000 | bytes 1048576 | tf_op jit(solution)/shard_map/other_core/pallas_call | solution.py:318
  24.8 0.1 collective-permute-start.6
  24.9 0.9 %own_core.1.own = f32[128,256]{1,0:T(8,128)S(1)} custom-call(f32[32,1408]{1,0:T(8,128)S(1)} %query_stats.1.y, bf16[32,128,256]{2,1,0:T(8,128)(2,1)S(1)} %get-tuple-element.34.windows_ref, bf16[2,32,256,256]{3,2,1,0:T(8,128)(2,1)S(1)} %get-tuple-element.32.hankel, f32[2,32,256]{2,1,0:T(8,128)S(1)} %get-tuple-element.28.after.scale_ref, ...), custom_call_target="tpu_custom_call" | custom-call | flops 500000000 | bytes 1048576 | tf_op jit(solution)/shard_map/own_core/pallas_call | solution.py:318
  25.8 0.4 %collective-permute-done.6.other = f32[128,256]{1,0:T(8,128)S(1)} collective-permute-done((f32[128,256]{1,0:T(8,128)S(1)}, f32[128,256]{1,0:T(8,128)S(1)}, u32[]{:S(2)}, u32[]{:S(2)}) %collective-permute-start.6) | collective-permute-done | bytes 131104 | tf_op jit(solution)/shard_map/ppermute | solution.py:22
  26.3 0.6 %minima.1 = (f32[4,32]{1,0:T(4,128)S(1)}, f32[1,256]{1,0:T(1,128)}) custom-call(f32[128,256]{1,0:T(8,128)S(1)} %own_core.1.own, f32[128,256]{1,0:T(8,128)S(1)} %collective-permute-done.6.other, f32[128,256]{1,0:T(8,128)S(1)} %get-tuple-element.36.banned, f32[8,256]{1,0:T(8,128)S(1)} %get-tuple-element.37.beyond), custom_call_target="tpu_custom_call" | custom-call | flops 1000000 | bytes 1048576 | tf_op jit(solution)/shard_map/minima/pallas_call | solution.py:318
  26.9 1.0 %collective-permute-start.9 = (f32[4,32]{1,0:T(4,128)S(1)}, f32[4,32]{1,0:T(4,128)S(1)}, u32[]{:S(2)}, u32[]{:S(2)}) collective-permute-start(f32[4,32]{1,0:T(4,128)S(1)} %get-tuple-element.38), channel_id=1, source_target_pairs={{0,3},{1,2},{2,1},{3,0},{4,7},{5,6},{6,5},{7,4},{8,11},{9,10},{10,... | collective-permute-start | bytes 1544 | tf_op jit(solution)/shard_map/ppermute | solution.py:22
  27.9 0.8 %collective-permute-start.8 = (f32[4,32]{1,0:T(4,128)S(1)}, f32[4,32]{1,0:T(4,128)S(1)}, u32[]{:S(2)}, u32[]{:S(2)}) collective-permute-start(f32[4,32]{1,0:T(4,128)S(1)} %get-tuple-element.38), channel_id=1, source_target_pairs={{0,2},{1,3},{2,0},{3,1},{4,6},{5,7},{6,4},{7,5},{8,10},{9,11},{10,... | collective-permute-start | bytes 1544 | tf_op jit(solution)/shard_map/ppermute | solution.py:22
  28.7 0.1 collective-permute-start.7
  28.7 1.1 %collective-permute-done.9 = f32[4,32]{1,0:T(4,128)S(1)} collective-permute-done((f32[4,32]{1,0:T(4,128)S(1)}, f32[4,32]{1,0:T(4,128)S(1)}, u32[]{:S(2)}, u32[]{:S(2)}) %collective-permute-start.9) | collective-permute-done | bytes 544 | tf_op jit(solution)/shard_map/ppermute | solution.py:22
  29.9 1.6 %collective-permute-done.8 = f32[4,32]{1,0:T(4,128)S(1)} collective-permute-done((f32[4,32]{1,0:T(4,128)S(1)}, f32[4,32]{1,0:T(4,128)S(1)}, u32[]{:S(2)}, u32[]{:S(2)}) %collective-permute-start.8) | collective-permute-done | bytes 544 | tf_op jit(solution)/shard_map/ppermute | solution.py:22
  31.5 0.0 collective-permute-done.7
  31.5 0.1 collective-permute-start.12
  31.6 3.2 %collective-permute-start.11 = (f32[4,32]{1,0:T(4,128)S(1)}, f32[4,32]{1,0:T(4,128)S(1)}, u32[]{:S(2)}, u32[]{:S(2)}) collective-permute-start(f32[4,32]{1,0:T(4,128)S(1)} %minimum_minimum_fusion.1), channel_id=1, source_target_pairs={{0,13},{1,12},{2,15},{3,14},{4,9},{5,8},{6,11},{7,10},{8,5},{9,4},... | collective-permute-start | bytes 1544 | tf_op jit(solution)/shard_map/ppermute | solution.py:22
  34.8 0.8 %collective-permute-start.10 = (f32[4,32]{1,0:T(4,128)S(1)}, f32[4,32]{1,0:T(4,128)S(1)}, u32[]{:S(2)}, u32[]{:S(2)}) collective-permute-start(f32[4,32]{1,0:T(4,128)S(1)} %minimum_minimum_fusion.1), channel_id=1, source_target_pairs={{0,5},{1,4},{2,7},{3,6},{4,1},{5,0},{6,3},{7,2},{8,13},{9,12},{10,... | collective-permute-start | bytes 1544 | tf_op jit(solution)/shard_map/ppermute | solution.py:22
  35.6 0.0 collective-permute-done.12
  35.6 0.9 %collective-permute-done.11 = f32[4,32]{1,0:T(4,128)S(1)} collective-permute-done((f32[4,32]{1,0:T(4,128)S(1)}, f32[4,32]{1,0:T(4,128)S(1)}, u32[]{:S(2)}, u32[]{:S(2)}) %collective-permute-start.11) | collective-permute-done | bytes 544 | tf_op jit(solution)/shard_map/ppermute | solution.py:22
  36.5 1.3 %collective-permute-done.10 = f32[4,32]{1,0:T(4,128)S(1)} collective-permute-done((f32[4,32]{1,0:T(4,128)S(1)}, f32[4,32]{1,0:T(4,128)S(1)}, u32[]{:S(2)}, u32[]{:S(2)}) %collective-permute-start.10) | collective-permute-done | bytes 544 | tf_op jit(solution)/shard_map/ppermute | solution.py:22
  37.8 0.6 %minimum_minimum_fusion = f32[4,32]{1,0:T(4,128)} fusion(f32[4,32]{1,0:T(4,128)S(1)} %collective-permute-done.12, f32[4,32]{1,0:T(4,128)S(1)} %collective-permute-done.11, f32[4,32]{1,0:T(4,128)S(1)} %minimum_minimum_fusion.1, f32[4,32]{1,0:T(4,128)S(1)} %collective-permute-done.10), kind=kLoop, calls=%fused_computation.2 | loop fusion | flops 384 | bytes 2560 | tf_op jit(solution)/shard_map/min | solution.py:444
  (4 shorter events, 0.0 us)
Async XLA Ops:
  2.4 1.4 %collective-permute-start = (f32[32,512]{1,0:T(8,128)S(1)}, f32[32,512]{1,0:T(8,128)S(1)}, u32[]{:S(2)}, u32[]{:S(2)}) collective-permute-start(f32[32,512]{1,0:T(8,128)S(1)} %get-tuple-element.22), channel_id=1, source_target_pairs={{0,1},{1,0},{2,3},{3,2},{4,5},{5,4},{6,7},{7,6},{8,9},{9,8},{10,11... | collective-permute-start | bytes 196616 | tf_op jit(solution)/shard_map/ppermute | solution.py:22
  4.2 12.0 %collective-permute-start.4 = (f32[32,640]{1,0:T(8,128)S(1)}, f32[32,640]{1,0:T(8,128)S(1)}, u32[]{:S(2)}, u32[]{:S(2)}) collective-permute-start(f32[32,640]{1,0:T(8,128)S(1)} %get-tuple-element.30.refs_0_), channel_id=1, source_target_pairs={{0,12},{1,13},{2,14},{3,15},{4,8},{5,9},{6,10},{7,11},{8,4},{9,5},... | collective-permute-start | bytes 245768 | tf_op jit(solution)/shard_map/ppermute | solution.py:22
  9.3 7.5 %collective-permute-start.3 = (f32[32,640]{1,0:T(8,128)S(1)}, f32[32,640]{1,0:T(8,128)S(1)}, u32[]{:S(2)}, u32[]{:S(2)}) collective-permute-start(f32[32,640]{1,0:T(8,128)S(1)} %get-tuple-element.30.refs_0_), channel_id=1, source_target_pairs={{0,8},{1,9},{2,10},{3,11},{4,12},{5,13},{6,14},{7,15},{8,0},{9,1},... | collective-permute-start | bytes 245768 | tf_op jit(solution)/shard_map/ppermute | solution.py:22
  9.3 7.5 %collective-permute-start.2 = (f32[32,640]{1,0:T(8,128)S(1)}, f32[32,640]{1,0:T(8,128)S(1)}, u32[]{:S(2)}, u32[]{:S(2)}) collective-permute-start(f32[32,640]{1,0:T(8,128)S(1)} %get-tuple-element.30.refs_0_), channel_id=1, source_target_pairs={{0,4},{1,5},{2,6},{3,7},{4,0},{5,1},{6,2},{7,3},{8,12},{9,13},{10,... | collective-permute-start | bytes 245768 | tf_op jit(solution)/shard_map/ppermute | solution.py:22
  9.9 6.3 %collective-permute-start.1 = (f32[32,256]{1,0:T(8,128)S(1)}, f32[32,256]{1,0:T(8,128)S(1)}, u32[]{:S(2)}, u32[]{:S(2)}) collective-permute-start(f32[32,256]{1,0:T(8,128)S(1)} %slice_bitcast_fusion), channel_id=1, source_target_pairs={{0,14},{1,15},{2,0},{3,1},{4,2},{5,3},{6,4},{7,5},{8,6},{9,7},{10,... | collective-permute-start | bytes 98312 | tf_op jit(solution)/shard_map/ppermute | solution.py:357
  17.1 5.4 %collective-permute-start.5 = (f32[32,1280]{1,0:T(8,128)S(1)}, f32[32,1280]{1,0:T(8,128)S(1)}, u32[]{:S(2)}, u32[]{:S(2)}) collective-permute-start(f32[32,1280]{1,0:T(8,128)S(1)} %windows.1.refs_0_), channel_id=1, source_target_pairs={{0,2},{1,3},{2,0},{3,1},{4,6},{5,7},{6,4},{7,5},{8,10},{9,11},{10,... | collective-permute-start | bytes 491528 | tf_op jit(solution)/shard_map/ppermute | solution.py:22
  24.8 1.4 %collective-permute-start.6 = (f32[128,256]{1,0:T(8,128)S(1)}, f32[128,256]{1,0:T(8,128)S(1)}, u32[]{:S(2)}, u32[]{:S(2)}) collective-permute-start(f32[128,256]{1,0:T(8,128)S(1)} %get-tuple-element.35), channel_id=1, source_target_pairs={{0,1},{1,0},{2,3},{3,2},{4,5},{5,4},{6,7},{7,6},{8,9},{9,8},{10,11... | collective-permute-start | bytes 393224 | tf_op jit(solution)/shard_map/ppermute | solution.py:22
  26.9 3.0 %collective-permute-start.9 = (f32[4,32]{1,0:T(4,128)S(1)}, f32[4,32]{1,0:T(4,128)S(1)}, u32[]{:S(2)}, u32[]{:S(2)}) collective-permute-start(f32[4,32]{1,0:T(4,128)S(1)} %get-tuple-element.38), channel_id=1, source_target_pairs={{0,3},{1,2},{2,1},{3,0},{4,7},{5,6},{6,5},{7,4},{8,11},{9,10},{10,... | collective-permute-start | bytes 1544 | tf_op jit(solution)/shard_map/ppermute | solution.py:22
  27.9 3.6 %collective-permute-start.8 = (f32[4,32]{1,0:T(4,128)S(1)}, f32[4,32]{1,0:T(4,128)S(1)}, u32[]{:S(2)}, u32[]{:S(2)}) collective-permute-start(f32[4,32]{1,0:T(4,128)S(1)} %get-tuple-element.38), channel_id=1, source_target_pairs={{0,2},{1,3},{2,0},{3,1},{4,6},{5,7},{6,4},{7,5},{8,10},{9,11},{10,... | collective-permute-start | bytes 1544 | tf_op jit(solution)/shard_map/ppermute | solution.py:22
  28.7 2.9 %collective-permute-start.7 = (f32[4,32]{1,0:T(4,128)S(1)}, f32[4,32]{1,0:T(4,128)S(1)}, u32[]{:S(2)}, u32[]{:S(2)}) collective-permute-start(f32[4,32]{1,0:T(4,128)S(1)} %get-tuple-element.38), channel_id=1, source_target_pairs={{0,1},{1,0},{2,3},{3,2},{4,5},{5,4},{6,7},{7,6},{8,9},{9,8},{10,11... | collective-permute-start | bytes 1544 | tf_op jit(solution)/shard_map/ppermute | solution.py:22
  31.5 4.1 %collective-permute-start.12 = (f32[4,32]{1,0:T(4,128)S(1)}, f32[4,32]{1,0:T(4,128)S(1)}, u32[]{:S(2)}, u32[]{:S(2)}) collective-permute-start(f32[4,32]{1,0:T(4,128)S(1)} %minimum_minimum_fusion.1), channel_id=1, source_target_pairs={{0,9},{1,8},{2,11},{3,10},{4,13},{5,12},{6,15},{7,14},{8,1},{9,0},... | collective-permute-start | bytes 1544 | tf_op jit(solution)/shard_map/ppermute | solution.py:22
  31.6 4.9 %collective-permute-start.11 = (f32[4,32]{1,0:T(4,128)S(1)}, f32[4,32]{1,0:T(4,128)S(1)}, u32[]{:S(2)}, u32[]{:S(2)}) collective-permute-start(f32[4,32]{1,0:T(4,128)S(1)} %minimum_minimum_fusion.1), channel_id=1, source_target_pairs={{0,13},{1,12},{2,15},{3,14},{4,9},{5,8},{6,11},{7,10},{8,5},{9,4},... | collective-permute-start | bytes 1544 | tf_op jit(solution)/shard_map/ppermute | solution.py:22
  34.8 3.0 %collective-permute-start.10 = (f32[4,32]{1,0:T(4,128)S(1)}, f32[4,32]{1,0:T(4,128)S(1)}, u32[]{:S(2)}, u32[]{:S(2)}) collective-permute-start(f32[4,32]{1,0:T(4,128)S(1)} %minimum_minimum_fusion.1), channel_id=1, source_target_pairs={{0,5},{1,4},{2,7},{3,6},{4,1},{5,0},{6,3},{7,2},{8,13},{9,12},{10,... | collective-permute-start | bytes 1544 | tf_op jit(solution)/shard_map/ppermute | solution.py:22

commit v5 on v4

--- a/solution.py
+++ b/solution.py
@@ -217,15 +217,8 @@
             hankel[c, at : at + LANES, :] = base[:, high * LANES : high * LANES + width]
 
 
-def first_columns_kernel(both, hankel, scale_ref, offset_ref, band_ref, sums_ref, spread_ref):
-    spread_ref[...] = spread_matrix(spread_ref.shape)
-    band_ref[...] = band_matrix(band_ref.shape)
-    sums_ref[...] = column_band(sums_ref.shape)
-    segment_columns(both.at[0], both.at[1], sums_ref, hankel.at[0], scale_ref.at[0], offset_ref.at[0])
-
-
-def second_columns_kernel(
-    limit, starts, excl, both, following, sums_ref, hankel_in, scale_in, offset_in, hankel, scale_ref, offset_ref, banned, beyond
+def first_columns_kernel(
+    limit, starts, excl, both, hankel, scale_ref, offset_ref, band_ref, sums_ref, spread_ref, banned, beyond
 ):
     width = banned.shape[1]
     columns = lax.axis_index("col") * width + lax.broadcasted_iota(jnp.int32, (QB, width), 1)
@@ -235,6 +228,15 @@
         near = jnp.where(jnp.abs(apart + starts[turn]) < excl[0], 1.0, last)
         banned[turn * QB : (turn + 1) * QB, :] = near
     beyond[...] = last[:8]
+    spread_ref[...] = spread_matrix(spread_ref.shape)
+    band_ref[...] = band_matrix(band_ref.shape)
+    sums_ref[...] = column_band(sums_ref.shape)
+    segment_columns(both.at[0], both.at[1], sums_ref, hankel.at[0], scale_ref.at[0], offset_ref.at[0])
+
+
+def second_columns_kernel(
+    both, following, sums_ref, hankel_in, scale_in, offset_in, hankel, scale_ref, offset_ref
+):
     segment_columns(both.at[1], following, sums_ref, hankel.at[1], scale_ref.at[1], offset_ref.at[1])
 
 
@@ -364,8 +366,16 @@
     band = jax.ShapeDtypeStruct((LANES // QB * (M + QB), LANES), bf16)
     sums = jax.ShapeDtypeStruct((2 * seg_len, seg_len), bf16)
     spread = jax.ShapeDtypeStruct((2 * half, half * LANES), bf16)
-    *columns, band, sums, spread = call(
-        first_columns_kernel, "columns", [*side, band, sums, spread], "v", both, flops=10**8
+    masked = [jax.ShapeDtypeStruct((queries, seg_len), f32), jax.ShapeDtypeStruct((8, seg_len), f32)]
+    *columns, band, sums, spread, banned, beyond = call(
+        functools.partial(first_columns_kernel, limit),
+        "columns",
+        [*side, band, sums, spread, *masked],
+        "ssv",
+        starts,
+        excl,
+        both,
+        flops=10**8,
     )
 
     rounds = rounds_from(BASE, devices_col)
@@ -384,18 +394,16 @@
     )
     for others in rounds[1:]:
         total = sum([exchanged(total, mask) for mask in others], total)
-    *columns, banned, beyond = call(
-        functools.partial(second_columns_kernel, limit),
+    columns = call(
+        second_columns_kernel,
         "columns",
-        [*side, jax.ShapeDtypeStruct((queries, seg_len), f32), jax.ShapeDtypeStruct((8, seg_len), f32)],
-        "ssvvvaaa",
-        starts,
-        excl,
+        side,
+        "vvvaaa",
         both,
         following,
         sums,
         *columns,
-        input_output_aliases={5: 0, 6: 1, 7: 2},
+        input_output_aliases={3: 0, 4: 1, 5: 2},
         flops=10**8,
     )
     queried = call(
@@ -439,8 +447,8 @@
         banned,
         beyond,
     )
-    crossed = [[others[0] + 1, *(mask + 1 for mask in reversed(others[1:]))] for others in rounds]
-    for others in [[1, 2, 3], *crossed]:
+    crossed = [[mask + 1 for mask in (others[0], *reversed(others[1:]))] for others in rounds]
+    for others in [[1], [3], *crossed]:
         rows = functools.reduce(jnp.minimum, [exchanged(rows, mask) for mask in others], rows)
     return (rows, column.reshape(seg_len))
 

time: 38.9 us -> 37.8 us (0.972)
  starting transfers between devices: 18.1 us -> 15.4 us
  waiting for transfers between devices: 8.11 us -> 10 us
    ppermute x12 -> x11, starting transfers between devices: 13.4 us -> 10.7 us  [exchanged(): return lax.ppermute(block, 'col', [(i, i ^ mask) for i in devices])]
    ppermute x12 -> x11, waiting for transfers between devices: 7.91 us -> 9.99 us  [exchanged(): return lax.ppermute(block, 'col', [(i, i ^ mask) for i in devices])]
  transfers between devices with their start and end apart: 13 -> 12, of which waited for: 9 -> 8; matrix products, arithmetic and copies ran while one was open for 2% -> 2% of each run, Pallas kernels for 11% -> 11%
where the time goes in v5:
time: 37.8 us; the launch traced here: 37.6 us
  starting transfers between devices  15.4 us (41%)
  waiting for transfers between devices  10 us (26%)
  Pallas kernels  7.7 us (20%)
  other arithmetic  3.04 us (8%)
  between operations  1.39 us (4%)
    ppermute x11, starting transfers between devices, exchanged(): return lax.ppermute(block, 'col', [(i, i ^ mask) for i in devices])  10.7 us
    ppermute x11, waiting for transfers between devices, exchanged(): return lax.ppermute(block, 'col', [(i, i ^ mask) for i in devices])  9.99 us
    pallas_call x9, Pallas kernels, call(): pl.pallas_call(kernel, out_shape=out_shape, in_specs=[SPECS[space] for sp...  7.7 us
    ppermute x1, starting transfers between devices, shards(): following = lax.ppermute(both[0, :, :seg_len], 'col', back)  4.7 us
    select_n x1, other arithmetic, shards(): packed = jnp.where(which == 0, series[None], valid[None].astype(f32))  0.92 us
    convert_element_type x1, other arithmetic, shards(): packed = jnp.where(which == 0, series[None], valid[None].astype(f32))  0.85 us
  transfers between devices with their start and end apart: 12, of which 8 were waited for; matrix products, arithmetic and copies ran while one was open for 2% of the time, Pallas kernels for 11%

profile of v5, /device:TPU:0, one launch (start us, length us, event | category | flops | bytes accessed | tf_op | source)
XLA Modules:
  0.0 37.6 jit_solution(9024158799455948769)
XLA Ops:
  0.6 0.8 %convert_element_type.8 = f32[64,256]{1,0:T(8,128)S(1)} convert(s32[64,256]{1,0:T(8,128)} %param.6) | non-fusion elementwise | flops 16384 | bytes 131072 | tf_op jit(solution)/shard_map/convert_element_type | solution.py:343
  1.5 0.9 %broadcast_select_fusion.packed = f32[2,64,256]{2,1,0:T(8,128)S(1)} fusion(f32[64,256]{1,0:T(8,128)S(1)} %convert_element_type.8, f32[64,256]{1,0:T(8,128)} %param.5, pred[2]{0:T(512)(128)(4,1)S(1)} %iota_compare_fusion), kind=kLoop, calls=%fused_computation | loop fusion | flops 32768 | bytes 262146 | tf_op jit(solution)/shard_map/jit(_where)/select_n | solution.py:343
  2.4 0.5 %collective-permute-start = (f32[32,512]{1,0:T(8,128)S(1)}, f32[32,512]{1,0:T(8,128)S(1)}, u32[]{:S(2)}, u32[]{:S(2)}) collective-permute-start(f32[32,512]{1,0:T(8,128)S(1)} %get-tuple-element.22), channel_id=1, source_target_pairs={{0,1},{1,0},{2,3},{3,2},{4,5},{5,4},{6,7},{7,6},{8,9},{9,8},{10,11... | collective-permute-start | bytes 196616 | tf_op jit(solution)/shard_map/ppermute | solution.py:22
  3.0 0.7 %fusion = (f32[4]{0:T(128)S(1)}, s32[4]{0:T(128)S(1)}) fusion(s32[4]{0:T(128)} %param.8, s32[4]{0:T(128)} %param.7), kind=kLoop, calls=%fused_computation.5 | loop fusion | flops 16 | bytes 64 | tf_op jit(solution)/shard_map/convert_element_type | solution.py:340
  3.6 0.2 collective-permute-done.other
  3.9 0.1 broadcast_in_dim.24.starts_ref
  3.9 0.3 chip.1
  4.2 5.0 %collective-permute-start.4 = (f32[32,640]{1,0:T(8,128)S(1)}, f32[32,640]{1,0:T(8,128)S(1)}, u32[]{:S(2)}, u32[]{:S(2)}) collective-permute-start(f32[32,640]{1,0:T(8,128)S(1)} %get-tuple-element.30.refs_0_), channel_id=1, source_target_pairs={{0,12},{1,13},{2,14},{3,15},{4,8},{5,9},{6,10},{7,11},{8,4},{9,5},... | collective-permute-start | bytes 245768 | tf_op jit(solution)/shard_map/ppermute | solution.py:22
  9.3 0.0 collective-permute-start.3
  9.3 0.6 %collective-permute-start.2 = (f32[32,640]{1,0:T(8,128)S(1)}, f32[32,640]{1,0:T(8,128)S(1)}, u32[]{:S(2)}, u32[]{:S(2)}) collective-permute-start(f32[32,640]{1,0:T(8,128)S(1)} %get-tuple-element.30.refs_0_), channel_id=1, source_target_pairs={{0,4},{1,5},{2,6},{3,7},{4,0},{5,1},{6,2},{7,3},{8,12},{9,13},{10,... | collective-permute-start | bytes 245768 | tf_op jit(solution)/shard_map/ppermute | solution.py:22
  9.9 4.7 %collective-permute-start.1 = (f32[32,256]{1,0:T(8,128)S(1)}, f32[32,256]{1,0:T(8,128)S(1)}, u32[]{:S(2)}, u32[]{:S(2)}) collective-permute-start(f32[32,256]{1,0:T(8,128)S(1)} %slice_bitcast_fusion), channel_id=1, source_target_pairs={{0,14},{1,15},{2,0},{3,1},{4,2},{5,3},{6,4},{7,5},{8,6},{9,7},{10,... | collective-permute-start | bytes 98312 | tf_op jit(solution)/shard_map/ppermute | solution.py:359
  15.3 2.0 %columns.2 = (bf16[2,32,256,256]{3,2,1,0:T(8,128)(2,1)S(1)}, f32[2,32,256]{2,1,0:T(8,128)S(1)}, f32[2,32,256]{2,1,0:T(8,128)S(1)}, bf16[1152,128]{1,0:T(8,128)(2...) custom-call(s32[4]{0:T(128)S(1)} %get-tuple-element.41.starts, ...), custom_call_target="tpu_custom_call" | custom-call | flops 100000000 | bytes 1048576 | tf_op jit(solution)/shard_map/columns/pallas_call | solution.py:320
  17.2 0.0 collective-permute-done.1.following.after_too
  17.2 0.0 collective-permute-done.4.refs_3_
  17.2 0.0 collective-permute-done.3.refs_2_
  17.3 0.0 collective-permute-done.2.refs_1_
  17.3 0.3 windows.1.refs_0_
  17.6 0.8 %collective-permute-start.5 = (f32[32,1280]{1,0:T(8,128)S(1)}, f32[32,1280]{1,0:T(8,128)S(1)}, u32[]{:S(2)}, u32[]{:S(2)}) collective-permute-start(f32[32,1280]{1,0:T(8,128)S(1)} %windows.1.refs_0_), channel_id=1, source_target_pairs={{0,2},{1,3},{2,0},{3,1},{4,6},{5,7},{6,4},{7,5},{8,10},{9,11},{10,... | collective-permute-start | bytes 491528 | tf_op jit(solution)/shard_map/ppermute | solution.py:22
  18.3 1.2 %columns.3 = (bf16[2,32,256,256]{3,2,1,0:T(8,128)(2,1)S(1)}, f32[2,32,256]{2,1,0:T(8,128)S(1)}, f32[2,32,256]{2,1,0:T(8,128)S(1)}) custom-call(f32[2,32,512]{2,1,0:T(8,128)S(1)} %get-tuple-element.23.both, f32[32,256]{1,0:T(8,128)S(1)} %collective-permute-done.1.following.after_too, ...), custom_call_target="tpu_custom_call", output_to_operand_aliasing={{0}: (3, {}), {1}: (4, {}), {2}: (5, {})} | custom-call | flops 100000000 | bytes 1048576 | tf_op jit(solution)/shard_map/columns/pallas_call | solution.py:320
  19.6 3.4 %collective-permute-done.5.refs_1_ = f32[32,1280]{1,0:T(8,128)S(1)} collective-permute-done((f32[32,1280]{1,0:T(8,128)S(1)}, f32[32,1280]{1,0:T(8,128)S(1)}, u32[]{:S(2)}, u32[]{:S(2)}) %collective-permute-start.5) | collective-permute-done | bytes 163872 | tf_op jit(solution)/shard_map/ppermute | solution.py:22
  23.0 0.4 query_stats.1.y
  23.3 2.0 %other_core.1 = (f32[128,256]{1,0:T(8,128)S(1)}, bf16[32,128,256]{2,1,0:T(8,128)(2,1)S(1)}) custom-call(f32[32,1408]{1,0:T(8,128)S(1)} %query_stats.1.y, bf16[64,4096]{1,0:T(8,128)(2,1)S(1)} %get-tuple-element.31.spread_ref, bf16[2,32,256,256]{3,2,1,0:T(8,128)(2,1)S(1)} %get-tuple-element.32.hankel, f32[2,32,256]{2,1,0:T(8,128)S(1)} %get-tuple-element.28.after.scale_ref, ...), custom_call_target="tpu_custom_call" | custom-call | flops 1000000 | bytes 1048576 | tf_op jit(solution)/shard_map/other_core/pallas_call | solution.py:320
  25.3 0.1 collective-permute-start.6
  25.4 0.9 %own_core.1.own = f32[128,256]{1,0:T(8,128)S(1)} custom-call(f32[32,1408]{1,0:T(8,128)S(1)} %query_stats.1.y, bf16[32,128,256]{2,1,0:T(8,128)(2,1)S(1)} %get-tuple-element.34.windows_ref, bf16[2,32,256,256]{3,2,1,0:T(8,128)(2,1)S(1)} %get-tuple-element.32.hankel, f32[2,32,256]{2,1,0:T(8,128)S(1)} %get-tuple-element.28.after.scale_ref, ...), custom_call_target="tpu_custom_call" | custom-call | flops 500000000 | bytes 1048576 | tf_op jit(solution)/shard_map/own_core/pallas_call | solution.py:320
  26.3 0.4 %collective-permute-done.6.other = f32[128,256]{1,0:T(8,128)S(1)} collective-permute-done((f32[128,256]{1,0:T(8,128)S(1)}, f32[128,256]{1,0:T(8,128)S(1)}, u32[]{:S(2)}, u32[]{:S(2)}) %collective-permute-start.6) | collective-permute-done | bytes 131104 | tf_op jit(solution)/shard_map/ppermute | solution.py:22
  26.7 0.6 %minima.1 = (f32[4,32]{1,0:T(4,128)S(1)}, f32[1,256]{1,0:T(1,128)}) custom-call(f32[128,256]{1,0:T(8,128)S(1)} %own_core.1.own, f32[128,256]{1,0:T(8,128)S(1)} %collective-permute-done.6.other, f32[128,256]{1,0:T(8,128)S(1)} %get-tuple-element.36.banned, f32[8,256]{1,0:T(8,128)S(1)} %get-tuple-element.37.beyond), custom_call_target="tpu_custom_call" | custom-call | flops 1000000 | bytes 1048576 | tf_op jit(solution)/shard_map/minima/pallas_call | solution.py:320
  27.3 0.1 collective-permute-start.7
  27.5 1.0 %collective-permute-done.7 = f32[4,32]{1,0:T(4,128)S(1)} collective-permute-done((f32[4,32]{1,0:T(4,128)S(1)}, f32[4,32]{1,0:T(4,128)S(1)}, u32[]{:S(2)}, u32[]{:S(2)}) %collective-permute-start.7) | collective-permute-done | bytes 544 | tf_op jit(solution)/shard_map/ppermute | solution.py:22
  28.5 0.6 %collective-permute-start.8 = (f32[4,32]{1,0:T(4,128)S(1)}, f32[4,32]{1,0:T(4,128)S(1)}, u32[]{:S(2)}, u32[]{:S(2)}) collective-permute-start(f32[4,32]{1,0:T(4,128)S(1)} %min.15), channel_id=1, source_target_pairs={{0,3},{1,2},{2,1},{3,0},{4,7},{5,6},{6,5},{7,4},{8,11},{9,10},{10,... | collective-permute-start | bytes 1544 | tf_op jit(solution)/shard_map/ppermute | solution.py:22
  29.1 2.4 %collective-permute-done.8 = f32[4,32]{1,0:T(4,128)S(1)} collective-permute-done((f32[4,32]{1,0:T(4,128)S(1)}, f32[4,32]{1,0:T(4,128)S(1)}, u32[]{:S(2)}, u32[]{:S(2)}) %collective-permute-start.8) | collective-permute-done | bytes 544 | tf_op jit(solution)/shard_map/ppermute | solution.py:22
  31.5 0.0 collective-permute-start.11
  31.5 2.5 %collective-permute-start.10 = (f32[4,32]{1,0:T(4,128)S(1)}, f32[4,32]{1,0:T(4,128)S(1)}, u32[]{:S(2)}, u32[]{:S(2)}) collective-permute-start(f32[4,32]{1,0:T(4,128)S(1)} %min.16), channel_id=1, source_target_pairs={{0,13},{1,12},{2,15},{3,14},{4,9},{5,8},{6,11},{7,10},{8,5},{9,4},... | collective-permute-start | bytes 1544 | tf_op jit(solution)/shard_map/ppermute | solution.py:22
  34.0 0.5 %collective-permute-start.9 = (f32[4,32]{1,0:T(4,128)S(1)}, f32[4,32]{1,0:T(4,128)S(1)}, u32[]{:S(2)}, u32[]{:S(2)}) collective-permute-start(f32[4,32]{1,0:T(4,128)S(1)} %min.16), channel_id=1, source_target_pairs={{0,5},{1,4},{2,7},{3,6},{4,1},{5,0},{6,3},{7,2},{8,13},{9,12},{10,... | collective-permute-start | bytes 1544 | tf_op jit(solution)/shard_map/ppermute | solution.py:22
  34.5 0.9 %collective-permute-done.11 = f32[4,32]{1,0:T(4,128)S(1)} collective-permute-done((f32[4,32]{1,0:T(4,128)S(1)}, f32[4,32]{1,0:T(4,128)S(1)}, u32[]{:S(2)}, u32[]{:S(2)}) %collective-permute-start.11) | collective-permute-done | bytes 544 | tf_op jit(solution)/shard_map/ppermute | solution.py:22
  35.4 0.9 %collective-permute-done.10 = f32[4,32]{1,0:T(4,128)S(1)} collective-permute-done((f32[4,32]{1,0:T(4,128)S(1)}, f32[4,32]{1,0:T(4,128)S(1)}, u32[]{:S(2)}, u32[]{:S(2)}) %collective-permute-start.10) | collective-permute-done | bytes 544 | tf_op jit(solution)/shard_map/ppermute | solution.py:22
  36.3 0.7 %collective-permute-done.9 = f32[4,32]{1,0:T(4,128)S(1)} collective-permute-done((f32[4,32]{1,0:T(4,128)S(1)}, f32[4,32]{1,0:T(4,128)S(1)}, u32[]{:S(2)}, u32[]{:S(2)}) %collective-permute-start.9) | collective-permute-done | bytes 544 | tf_op jit(solution)/shard_map/ppermute | solution.py:22
  37.0 0.6 %minimum_minimum_fusion = f32[4,32]{1,0:T(4,128)} fusion(f32[4,32]{1,0:T(4,128)S(1)} %collective-permute-done.11, f32[4,32]{1,0:T(4,128)S(1)} %collective-permute-done.10, f32[4,32]{1,0:T(4,128)S(1)} %min.16, f32[4,32]{1,0:T(4,128)S(1)} %collective-permute-done.9), kind=kLoop, calls=%fused_computation.2 | loop fusion | flops 384 | bytes 2560 | tf_op jit(solution)/shard_map/min | solution.py:452
  (5 shorter events, 0.0 us)
Async XLA Ops:
  2.4 1.4 %collective-permute-start = (f32[32,512]{1,0:T(8,128)S(1)}, f32[32,512]{1,0:T(8,128)S(1)}, u32[]{:S(2)}, u32[]{:S(2)}) collective-permute-start(f32[32,512]{1,0:T(8,128)S(1)} %get-tuple-element.22), channel_id=1, source_target_pairs={{0,1},{1,0},{2,3},{3,2},{4,5},{5,4},{6,7},{7,6},{8,9},{9,8},{10,11... | collective-permute-start | bytes 196616 | tf_op jit(solution)/shard_map/ppermute | solution.py:22
  4.2 13.0 %collective-permute-start.4 = (f32[32,640]{1,0:T(8,128)S(1)}, f32[32,640]{1,0:T(8,128)S(1)}, u32[]{:S(2)}, u32[]{:S(2)}) collective-permute-start(f32[32,640]{1,0:T(8,128)S(1)} %get-tuple-element.30.refs_0_), channel_id=1, source_target_pairs={{0,12},{1,13},{2,14},{3,15},{4,8},{5,9},{6,10},{7,11},{8,4},{9,5},... | collective-permute-start | bytes 245768 | tf_op jit(solution)/shard_map/ppermute | solution.py:22
  9.3 8.0 %collective-permute-start.3 = (f32[32,640]{1,0:T(8,128)S(1)}, f32[32,640]{1,0:T(8,128)S(1)}, u32[]{:S(2)}, u32[]{:S(2)}) collective-permute-start(f32[32,640]{1,0:T(8,128)S(1)} %get-tuple-element.30.refs_0_), channel_id=1, source_target_pairs={{0,8},{1,9},{2,10},{3,11},{4,12},{5,13},{6,14},{7,15},{8,0},{9,1},... | collective-permute-start | bytes 245768 | tf_op jit(solution)/shard_map/ppermute | solution.py:22
  9.3 8.0 %collective-permute-start.2 = (f32[32,640]{1,0:T(8,128)S(1)}, f32[32,640]{1,0:T(8,128)S(1)}, u32[]{:S(2)}, u32[]{:S(2)}) collective-permute-start(f32[32,640]{1,0:T(8,128)S(1)} %get-tuple-element.30.refs_0_), channel_id=1, source_target_pairs={{0,4},{1,5},{2,6},{3,7},{4,0},{5,1},{6,2},{7,3},{8,12},{9,13},{10,... | collective-permute-start | bytes 245768 | tf_op jit(solution)/shard_map/ppermute | solution.py:22
  9.9 7.3 %collective-permute-start.1 = (f32[32,256]{1,0:T(8,128)S(1)}, f32[32,256]{1,0:T(8,128)S(1)}, u32[]{:S(2)}, u32[]{:S(2)}) collective-permute-start(f32[32,256]{1,0:T(8,128)S(1)} %slice_bitcast_fusion), channel_id=1, source_target_pairs={{0,14},{1,15},{2,0},{3,1},{4,2},{5,3},{6,4},{7,5},{8,6},{9,7},{10,... | collective-permute-start | bytes 98312 | tf_op jit(solution)/shard_map/ppermute | solution.py:359
  17.6 5.4 %collective-permute-start.5 = (f32[32,1280]{1,0:T(8,128)S(1)}, f32[32,1280]{1,0:T(8,128)S(1)}, u32[]{:S(2)}, u32[]{:S(2)}) collective-permute-start(f32[32,1280]{1,0:T(8,128)S(1)} %windows.1.refs_0_), channel_id=1, source_target_pairs={{0,2},{1,3},{2,0},{3,1},{4,6},{5,7},{6,4},{7,5},{8,10},{9,11},{10,... | collective-permute-start | bytes 491528 | tf_op jit(solution)/shard_map/ppermute | solution.py:22
  25.3 1.4 %collective-permute-start.6 = (f32[128,256]{1,0:T(8,128)S(1)}, f32[128,256]{1,0:T(8,128)S(1)}, u32[]{:S(2)}, u32[]{:S(2)}) collective-permute-start(f32[128,256]{1,0:T(8,128)S(1)} %get-tuple-element.35), channel_id=1, source_target_pairs={{0,1},{1,0},{2,3},{3,2},{4,5},{5,4},{6,7},{7,6},{8,9},{9,8},{10,11... | collective-permute-start | bytes 393224 | tf_op jit(solution)/shard_map/ppermute | solution.py:22
  27.3 1.2 %collective-permute-start.7 = (f32[4,32]{1,0:T(4,128)S(1)}, f32[4,32]{1,0:T(4,128)S(1)}, u32[]{:S(2)}, u32[]{:S(2)}) collective-permute-start(f32[4,32]{1,0:T(4,128)S(1)} %get-tuple-element.38), channel_id=1, source_target_pairs={{0,1},{1,0},{2,3},{3,2},{4,5},{5,4},{6,7},{7,6},{8,9},{9,8},{10,11... | collective-permute-start | bytes 1544 | tf_op jit(solution)/shard_map/ppermute | solution.py:22
  28.5 3.0 %collective-permute-start.8 = (f32[4,32]{1,0:T(4,128)S(1)}, f32[4,32]{1,0:T(4,128)S(1)}, u32[]{:S(2)}, u32[]{:S(2)}) collective-permute-start(f32[4,32]{1,0:T(4,128)S(1)} %min.15), channel_id=1, source_target_pairs={{0,3},{1,2},{2,1},{3,0},{4,7},{5,6},{6,5},{7,4},{8,11},{9,10},{10,... | collective-permute-start | bytes 1544 | tf_op jit(solution)/shard_map/ppermute | solution.py:22
  31.5 3.9 %collective-permute-start.11 = (f32[4,32]{1,0:T(4,128)S(1)}, f32[4,32]{1,0:T(4,128)S(1)}, u32[]{:S(2)}, u32[]{:S(2)}) collective-permute-start(f32[4,32]{1,0:T(4,128)S(1)} %min.16), channel_id=1, source_target_pairs={{0,9},{1,8},{2,11},{3,10},{4,13},{5,12},{6,15},{7,14},{8,1},{9,0},... | collective-permute-start | bytes 1544 | tf_op jit(solution)/shard_map/ppermute | solution.py:22
  31.5 4.8 %collective-permute-start.10 = (f32[4,32]{1,0:T(4,128)S(1)}, f32[4,32]{1,0:T(4,128)S(1)}, u32[]{:S(2)}, u32[]{:S(2)}) collective-permute-start(f32[4,32]{1,0:T(4,128)S(1)} %min.16), channel_id=1, source_target_pairs={{0,13},{1,12},{2,15},{3,14},{4,9},{5,8},{6,11},{7,10},{8,5},{9,4},... | collective-permute-start | bytes 1544 | tf_op jit(solution)/shard_map/ppermute | solution.py:22
  34.0 3.0 %collective-permute-start.9 = (f32[4,32]{1,0:T(4,128)S(1)}, f32[4,32]{1,0:T(4,128)S(1)}, u32[]{:S(2)}, u32[]{:S(2)}) collective-permute-start(f32[4,32]{1,0:T(4,128)S(1)} %min.16), channel_id=1, source_target_pairs={{0,5},{1,4},{2,7},{3,6},{4,1},{5,0},{6,3},{7,2},{8,13},{9,12},{10,... | collective-permute-start | bytes 1544 | tf_op jit(solution)/shard_map/ppermute | solution.py:22

commit v6 on v5

--- a/solution.py
+++ b/solution.py
@@ -11,6 +11,7 @@
 QB = 32
 CORES = 2
 BASE = 4
+SHARE_LIMIT = 56381931
 LANES = 128
 
 f32 = jnp.float32
@@ -44,12 +45,20 @@
     return pl.ds(pl.multiple_of(which * half, half), half)
 
 
-def share_kernel(packed, keep, send):
+def share_kernel(series, valid, keep, send, samples, flags, sems):
+    copies = [
+        pltpu.make_async_copy(source, target, sems.at[i])
+        for i, (source, target) in enumerate([(series, samples), (valid, flags)])
+    ]
+    for copy in copies:
+        copy.start()
+    for copy in copies:
+        copy.wait()
     core = lax.rem(lax.axis_index("col"), CORES)
-    width = packed.shape[2]
+    width = samples.shape[1]
     for which, out in ((core, keep), (1 - core, send)):
-        for i in range(packed.shape[0]):
-            out[:, i * width : (i + 1) * width] = packed[i, half_rows(out, which), :]
+        out[:, :width] = samples[half_rows(out, which), :]
+        out[:, width:] = flags[half_rows(out, which), :].astype(f32)
 
 
 def first_lane(ref):
@@ -315,14 +324,14 @@
 )
 
 
-def call(kernel, name, out_shape, spaces, *operands, flops=10**6, **options):
+def call(kernel, name, out_shape, spaces, *operands, flops=10**6, limit=40 * 2**20, **options):
     many = isinstance(out_shape, list)
     return pl.pallas_call(
         kernel,
         out_shape=out_shape,
         in_specs=[SPECS[space] for space in spaces],
         out_specs=[SPECS["v"]] * len(out_shape) if many else SPECS["v"],
-        compiler_params=pltpu.CompilerParams(vmem_limit_bytes=40 * 2**20),
+        compiler_params=pltpu.CompilerParams(vmem_limit_bytes=limit),
         cost_estimate=pl.CostEstimate(flops=flops, bytes_accessed=2**20, transcendentals=0),
         name=name,
         **options,
@@ -339,10 +348,21 @@
     starts = owners * seg_len + blocks * QB
     starts_vector = jnp.broadcast_to(starts.astype(f32)[:, None], (turns, LANES))
 
-    which = lax.broadcasted_iota(jnp.int32, (2, *series.shape), 0)
-    packed = jnp.where(which == 0, series[None], valid[None].astype(f32))
     part = jax.ShapeDtypeStruct((half, 2 * seg_len), f32)
-    keep, send = call(share_kernel, "share", [part] * 2, "v", packed)
+    keep, send = call(
+        share_kernel,
+        "share",
+        [part] * 2,
+        "aa",
+        series,
+        valid,
+        scratch_shapes=[
+            pltpu.VMEM(series.shape, f32),
+            pltpu.VMEM(valid.shape, jnp.int32),
+            pltpu.SemaphoreType.DMA((2,)),
+        ],
+        limit=SHARE_LIMIT,
+    )
     chip, both = call(
         chip_kernel,
         "chip",

time: 37.8 us -> 36.9 us (0.976)
  other arithmetic: 3.04 us -> 1.26 us
  Pallas kernels: 7.7 us -> 8.59 us
    select_n x1 -> x0, other arithmetic: 0.92 us -> none  [shards(): packed = jnp.where(which == 0, series[None], valid[None].astype(f32))]
    pallas_call x9, Pallas kernels: 7.7 us -> 8.59 us  [call(): pl.pallas_call(kernel, out_shape=out_shape, in_specs=[SPECS[space] for sp...]
    convert_element_type x1 -> x0, other arithmetic: 0.85 us -> none  [shards(): packed = jnp.where(which == 0, series[None], valid[None].astype(f32))]
where the time goes in v6:
time: 36.9 us; the launch traced here: 36.7 us
  starting transfers between devices  15.4 us (42%)
  waiting for transfers between devices  10 us (27%)
  Pallas kernels  8.59 us (23%)
  between operations  1.38 us (4%)
  other arithmetic  1.26 us (3%)
    ppermute x11, starting transfers between devices, exchanged(): return lax.ppermute(block, 'col', [(i, i ^ mask) for i in devices])  10.7 us
    ppermute x11, waiting for transfers between devices, exchanged(): return lax.ppermute(block, 'col', [(i, i ^ mask) for i in devices])  10 us
    pallas_call x9, Pallas kernels, call(): pl.pallas_call(kernel, out_shape=out_shape, in_specs=[SPECS[space] for sp...  8.59 us
    ppermute x1, starting transfers between devices, shards(): following = lax.ppermute(both[0, :, :seg_len], 'col', back)  4.7 us
  transfers between devices with their start and end apart: 12, of which 8 were waited for; matrix products, arithmetic and copies ran while one was open for 2% of the time, Pallas kernels for 11%

profile of v6, /device:TPU:0, one launch (start us, length us, event | category | flops | bytes accessed | tf_op | source)
XLA Modules:
  0.0 36.7 jit_solution(1959749462764163681)
XLA Ops:
  0.6 0.9 %share.1 = (f32[32,512]{1,0:T(8,128)S(1)}, f32[32,512]{1,0:T(8,128)S(1)}) custom-call(f32[64,256]{1,0:T(8,128)} %series.1, s32[64,256]{1,0:T(8,128)} %valid.1), custom_call_target="tpu_custom_call" | custom-call | flops 1000000 | bytes 1048576 | tf_op jit(solution)/shard_map/share/pallas_call | solution.py:329
  1.5 0.5 %collective-permute-start = (f32[32,512]{1,0:T(8,128)S(1)}, f32[32,512]{1,0:T(8,128)S(1)}, u32[]{:S(2)}, u32[]{:S(2)}) collective-permute-start(f32[32,512]{1,0:T(8,128)S(1)} %get-tuple-element.22), channel_id=1, source_target_pairs={{0,1},{1,0},{2,3},{3,2},{4,5},{5,4},{6,7},{7,6},{8,9},{9,8},{10,11... | collective-permute-start | bytes 196616 | tf_op jit(solution)/shard_map/ppermute | solution.py:23
  2.1 0.7 %fusion = (f32[4]{0:T(128)S(1)}, s32[4]{0:T(128)S(1)}) fusion(s32[4]{0:T(128)} %param.8, s32[4]{0:T(128)} %param.7), kind=kLoop, calls=%fused_computation.3 | loop fusion | flops 16 | bytes 64 | tf_op jit(solution)/shard_map/convert_element_type | solution.py:349
  2.7 0.2 collective-permute-done.other
  3.0 0.1 broadcast_in_dim.2.starts_ref
  3.0 0.3 chip.1
  3.3 5.0 %collective-permute-start.4 = (f32[32,640]{1,0:T(8,128)S(1)}, f32[32,640]{1,0:T(8,128)S(1)}, u32[]{:S(2)}, u32[]{:S(2)}) collective-permute-start(f32[32,640]{1,0:T(8,128)S(1)} %get-tuple-element.30.refs_0_), channel_id=1, source_target_pairs={{0,12},{1,13},{2,14},{3,15},{4,8},{5,9},{6,10},{7,11},{8,4},{9,5},... | collective-permute-start | bytes 245768 | tf_op jit(solution)/shard_map/ppermute | solution.py:23
  8.4 0.0 collective-permute-start.3
  8.4 0.6 %collective-permute-start.2 = (f32[32,640]{1,0:T(8,128)S(1)}, f32[32,640]{1,0:T(8,128)S(1)}, u32[]{:S(2)}, u32[]{:S(2)}) collective-permute-start(f32[32,640]{1,0:T(8,128)S(1)} %get-tuple-element.30.refs_0_), channel_id=1, source_target_pairs={{0,4},{1,5},{2,6},{3,7},{4,0},{5,1},{6,2},{7,3},{8,12},{9,13},{10,... | collective-permute-start | bytes 245768 | tf_op jit(solution)/shard_map/ppermute | solution.py:23
  9.0 4.7 %collective-permute-start.1 = (f32[32,256]{1,0:T(8,128)S(1)}, f32[32,256]{1,0:T(8,128)S(1)}, u32[]{:S(2)}, u32[]{:S(2)}) collective-permute-start(f32[32,256]{1,0:T(8,128)S(1)} %slice_bitcast_fusion), channel_id=1, source_target_pairs={{0,14},{1,15},{2,0},{3,1},{4,2},{5,3},{6,4},{7,5},{8,6},{9,7},{10,... | collective-permute-start | bytes 98312 | tf_op jit(solution)/shard_map/ppermute | solution.py:379
  14.4 2.0 %columns.2 = (bf16[2,32,256,256]{3,2,1,0:T(8,128)(2,1)S(1)}, f32[2,32,256]{2,1,0:T(8,128)S(1)}, f32[2,32,256]{2,1,0:T(8,128)S(1)}, bf16[1152,128]{1,0:T(8,128)(2...) custom-call(s32[4]{0:T(128)S(1)} %get-tuple-element.41.starts, ...), custom_call_target="tpu_custom_call" | custom-call | flops 100000000 | bytes 1048576 | tf_op jit(solution)/shard_map/columns/pallas_call | solution.py:329
  16.3 0.0 collective-permute-done.1.following.after_too
  16.3 0.0 collective-permute-done.4.refs_3_
  16.3 0.0 collective-permute-done.3.refs_2_
  16.4 0.0 collective-permute-done.2.refs_1_
  16.4 0.3 windows.1.refs_0_
  16.7 0.7 %collective-permute-start.5 = (f32[32,1280]{1,0:T(8,128)S(1)}, f32[32,1280]{1,0:T(8,128)S(1)}, u32[]{:S(2)}, u32[]{:S(2)}) collective-permute-start(f32[32,1280]{1,0:T(8,128)S(1)} %windows.1.refs_0_), channel_id=1, source_target_pairs={{0,2},{1,3},{2,0},{3,1},{4,6},{5,7},{6,4},{7,5},{8,10},{9,11},{10,... | collective-permute-start | bytes 491528 | tf_op jit(solution)/shard_map/ppermute | solution.py:23
  17.4 1.2 %columns.3 = (bf16[2,32,256,256]{3,2,1,0:T(8,128)(2,1)S(1)}, f32[2,32,256]{2,1,0:T(8,128)S(1)}, f32[2,32,256]{2,1,0:T(8,128)S(1)}) custom-call(f32[2,32,512]{2,1,0:T(8,128)S(1)} %get-tuple-element.23.both, f32[32,256]{1,0:T(8,128)S(1)} %collective-permute-done.1.following.after_too, ...), custom_call_target="tpu_custom_call", output_to_operand_aliasing={{0}: (3, {}), {1}: (4, {}), {2}: (5, {})} | custom-call | flops 100000000 | bytes 1048576 | tf_op jit(solution)/shard_map/columns/pallas_call | solution.py:329
  18.7 3.4 %collective-permute-done.5.refs_1_ = f32[32,1280]{1,0:T(8,128)S(1)} collective-permute-done((f32[32,1280]{1,0:T(8,128)S(1)}, f32[32,1280]{1,0:T(8,128)S(1)}, u32[]{:S(2)}, u32[]{:S(2)}) %collective-permute-start.5) | collective-permute-done | bytes 163872 | tf_op jit(solution)/shard_map/ppermute | solution.py:23
  22.1 0.4 query_stats.1.y
  22.4 2.0 %other_core.1 = (f32[128,256]{1,0:T(8,128)S(1)}, bf16[32,128,256]{2,1,0:T(8,128)(2,1)S(1)}) custom-call(f32[32,1408]{1,0:T(8,128)S(1)} %query_stats.1.y, bf16[64,4096]{1,0:T(8,128)(2,1)S(1)} %get-tuple-element.31.spread_ref, bf16[2,32,256,256]{3,2,1,0:T(8,128)(2,1)S(1)} %get-tuple-element.32.hankel, f32[2,32,256]{2,1,0:T(8,128)S(1)} %get-tuple-element.28.after.scale_ref, ...), custom_call_target="tpu_custom_call" | custom-call | flops 1000000 | bytes 1048576 | tf_op jit(solution)/shard_map/other_core/pallas_call | solution.py:329
  24.4 0.1 collective-permute-start.6
  24.5 0.9 %own_core.1.own = f32[128,256]{1,0:T(8,128)S(1)} custom-call(f32[32,1408]{1,0:T(8,128)S(1)} %query_stats.1.y, bf16[32,128,256]{2,1,0:T(8,128)(2,1)S(1)} %get-tuple-element.34.windows_ref, bf16[2,32,256,256]{3,2,1,0:T(8,128)(2,1)S(1)} %get-tuple-element.32.hankel, f32[2,32,256]{2,1,0:T(8,128)S(1)} %get-tuple-element.28.after.scale_ref, ...), custom_call_target="tpu_custom_call" | custom-call | flops 500000000 | bytes 1048576 | tf_op jit(solution)/shard_map/own_core/pallas_call | solution.py:329
  25.4 0.4 %collective-permute-done.6.other = f32[128,256]{1,0:T(8,128)S(1)} collective-permute-done((f32[128,256]{1,0:T(8,128)S(1)}, f32[128,256]{1,0:T(8,128)S(1)}, u32[]{:S(2)}, u32[]{:S(2)}) %collective-permute-start.6) | collective-permute-done | bytes 131104 | tf_op jit(solution)/shard_map/ppermute | solution.py:23
  25.8 0.6 %minima.1 = (f32[4,32]{1,0:T(4,128)S(1)}, f32[1,256]{1,0:T(1,128)}) custom-call(f32[128,256]{1,0:T(8,128)S(1)} %own_core.1.own, f32[128,256]{1,0:T(8,128)S(1)} %collective-permute-done.6.other, f32[128,256]{1,0:T(8,128)S(1)} %get-tuple-element.36.banned, f32[8,256]{1,0:T(8,128)S(1)} %get-tuple-element.37.beyond), custom_call_target="tpu_custom_call" | custom-call | flops 1000000 | bytes 1048576 | tf_op jit(solution)/shard_map/minima/pallas_call | solution.py:329
  26.4 0.1 collective-permute-start.7
  26.6 1.0 %collective-permute-done.7 = f32[4,32]{1,0:T(4,128)S(1)} collective-permute-done((f32[4,32]{1,0:T(4,128)S(1)}, f32[4,32]{1,0:T(4,128)S(1)}, u32[]{:S(2)}, u32[]{:S(2)}) %collective-permute-start.7) | collective-permute-done | bytes 544 | tf_op jit(solution)/shard_map/ppermute | solution.py:23
  27.6 0.6 %collective-permute-start.8 = (f32[4,32]{1,0:T(4,128)S(1)}, f32[4,32]{1,0:T(4,128)S(1)}, u32[]{:S(2)}, u32[]{:S(2)}) collective-permute-start(f32[4,32]{1,0:T(4,128)S(1)} %min.15), channel_id=1, source_target_pairs={{0,3},{1,2},{2,1},{3,0},{4,7},{5,6},{6,5},{7,4},{8,11},{9,10},{10,... | collective-permute-start | bytes 1544 | tf_op jit(solution)/shard_map/ppermute | solution.py:23
  28.2 2.4 %collective-permute-done.8 = f32[4,32]{1,0:T(4,128)S(1)} collective-permute-done((f32[4,32]{1,0:T(4,128)S(1)}, f32[4,32]{1,0:T(4,128)S(1)}, u32[]{:S(2)}, u32[]{:S(2)}) %collective-permute-start.8) | collective-permute-done | bytes 544 | tf_op jit(solution)/shard_map/ppermute | solution.py:23
  30.6 0.0 collective-permute-start.11
  30.6 2.5 %collective-permute-start.10 = (f32[4,32]{1,0:T(4,128)S(1)}, f32[4,32]{1,0:T(4,128)S(1)}, u32[]{:S(2)}, u32[]{:S(2)}) collective-permute-start(f32[4,32]{1,0:T(4,128)S(1)} %min.16), channel_id=1, source_target_pairs={{0,13},{1,12},{2,15},{3,14},{4,9},{5,8},{6,11},{7,10},{8,5},{9,4},... | collective-permute-start | bytes 1544 | tf_op jit(solution)/shard_map/ppermute | solution.py:23
  33.1 0.5 %collective-permute-start.9 = (f32[4,32]{1,0:T(4,128)S(1)}, f32[4,32]{1,0:T(4,128)S(1)}, u32[]{:S(2)}, u32[]{:S(2)}) collective-permute-start(f32[4,32]{1,0:T(4,128)S(1)} %min.16), channel_id=1, source_target_pairs={{0,5},{1,4},{2,7},{3,6},{4,1},{5,0},{6,3},{7,2},{8,13},{9,12},{10,... | collective-permute-start | bytes 1544 | tf_op jit(solution)/shard_map/ppermute | solution.py:23
  33.6 0.9 %collective-permute-done.11 = f32[4,32]{1,0:T(4,128)S(1)} collective-permute-done((f32[4,32]{1,0:T(4,128)S(1)}, f32[4,32]{1,0:T(4,128)S(1)}, u32[]{:S(2)}, u32[]{:S(2)}) %collective-permute-start.11) | collective-permute-done | bytes 544 | tf_op jit(solution)/shard_map/ppermute | solution.py:23
  34.5 0.9 %collective-permute-done.10 = f32[4,32]{1,0:T(4,128)S(1)} collective-permute-done((f32[4,32]{1,0:T(4,128)S(1)}, f32[4,32]{1,0:T(4,128)S(1)}, u32[]{:S(2)}, u32[]{:S(2)}) %collective-permute-start.10) | collective-permute-done | bytes 544 | tf_op jit(solution)/shard_map/ppermute | solution.py:23
  35.4 0.7 %collective-permute-done.9 = f32[4,32]{1,0:T(4,128)S(1)} collective-permute-done((f32[4,32]{1,0:T(4,128)S(1)}, f32[4,32]{1,0:T(4,128)S(1)}, u32[]{:S(2)}, u32[]{:S(2)}) %collective-permute-start.9) | collective-permute-done | bytes 544 | tf_op jit(solution)/shard_map/ppermute | solution.py:23
  36.1 0.6 %minimum_minimum_fusion = f32[4,32]{1,0:T(4,128)} fusion(f32[4,32]{1,0:T(4,128)S(1)} %collective-permute-done.11, f32[4,32]{1,0:T(4,128)S(1)} %collective-permute-done.10, f32[4,32]{1,0:T(4,128)S(1)} %min.16, f32[4,32]{1,0:T(4,128)S(1)} %collective-permute-done.9), kind=kLoop, calls=%fused_computation.1 | loop fusion | flops 384 | bytes 2560 | tf_op jit(solution)/shard_map/min | solution.py:472
  (3 shorter events, 0.0 us)
Async XLA Ops:
  1.5 1.4 %collective-permute-start = (f32[32,512]{1,0:T(8,128)S(1)}, f32[32,512]{1,0:T(8,128)S(1)}, u32[]{:S(2)}, u32[]{:S(2)}) collective-permute-start(f32[32,512]{1,0:T(8,128)S(1)} %get-tuple-element.22), channel_id=1, source_target_pairs={{0,1},{1,0},{2,3},{3,2},{4,5},{5,4},{6,7},{7,6},{8,9},{9,8},{10,11... | collective-permute-start | bytes 196616 | tf_op jit(solution)/shard_map/ppermute | solution.py:23
  3.3 13.0 %collective-permute-start.4 = (f32[32,640]{1,0:T(8,128)S(1)}, f32[32,640]{1,0:T(8,128)S(1)}, u32[]{:S(2)}, u32[]{:S(2)}) collective-permute-start(f32[32,640]{1,0:T(8,128)S(1)} %get-tuple-element.30.refs_0_), channel_id=1, source_target_pairs={{0,12},{1,13},{2,14},{3,15},{4,8},{5,9},{6,10},{7,11},{8,4},{9,5},... | collective-permute-start | bytes 245768 | tf_op jit(solution)/shard_map/ppermute | solution.py:23
  8.4 8.0 %collective-permute-start.3 = (f32[32,640]{1,0:T(8,128)S(1)}, f32[32,640]{1,0:T(8,128)S(1)}, u32[]{:S(2)}, u32[]{:S(2)}) collective-permute-start(f32[32,640]{1,0:T(8,128)S(1)} %get-tuple-element.30.refs_0_), channel_id=1, source_target_pairs={{0,8},{1,9},{2,10},{3,11},{4,12},{5,13},{6,14},{7,15},{8,0},{9,1},... | collective-permute-start | bytes 245768 | tf_op jit(solution)/shard_map/ppermute | solution.py:23
  8.4 8.0 %collective-permute-start.2 = (f32[32,640]{1,0:T(8,128)S(1)}, f32[32,640]{1,0:T(8,128)S(1)}, u32[]{:S(2)}, u32[]{:S(2)}) collective-permute-start(f32[32,640]{1,0:T(8,128)S(1)} %get-tuple-element.30.refs_0_), channel_id=1, source_target_pairs={{0,4},{1,5},{2,6},{3,7},{4,0},{5,1},{6,2},{7,3},{8,12},{9,13},{10,... | collective-permute-start | bytes 245768 | tf_op jit(solution)/shard_map/ppermute | solution.py:23
  9.0 7.3 %collective-permute-start.1 = (f32[32,256]{1,0:T(8,128)S(1)}, f32[32,256]{1,0:T(8,128)S(1)}, u32[]{:S(2)}, u32[]{:S(2)}) collective-permute-start(f32[32,256]{1,0:T(8,128)S(1)} %slice_bitcast_fusion), channel_id=1, source_target_pairs={{0,14},{1,15},{2,0},{3,1},{4,2},{5,3},{6,4},{7,5},{8,6},{9,7},{10,... | collective-permute-start | bytes 98312 | tf_op jit(solution)/shard_map/ppermute | solution.py:379
  16.7 5.4 %collective-permute-start.5 = (f32[32,1280]{1,0:T(8,128)S(1)}, f32[32,1280]{1,0:T(8,128)S(1)}, u32[]{:S(2)}, u32[]{:S(2)}) collective-permute-start(f32[32,1280]{1,0:T(8,128)S(1)} %windows.1.refs_0_), channel_id=1, source_target_pairs={{0,2},{1,3},{2,0},{3,1},{4,6},{5,7},{6,4},{7,5},{8,10},{9,11},{10,... | collective-permute-start | bytes 491528 | tf_op jit(solution)/shard_map/ppermute | solution.py:23
  24.4 1.4 %collective-permute-start.6 = (f32[128,256]{1,0:T(8,128)S(1)}, f32[128,256]{1,0:T(8,128)S(1)}, u32[]{:S(2)}, u32[]{:S(2)}) collective-permute-start(f32[128,256]{1,0:T(8,128)S(1)} %get-tuple-element.35), channel_id=1, source_target_pairs={{0,1},{1,0},{2,3},{3,2},{4,5},{5,4},{6,7},{7,6},{8,9},{9,8},{10,11... | collective-permute-start | bytes 393224 | tf_op jit(solution)/shard_map/ppermute | solution.py:23
  26.4 1.2 %collective-permute-start.7 = (f32[4,32]{1,0:T(4,128)S(1)}, f32[4,32]{1,0:T(4,128)S(1)}, u32[]{:S(2)}, u32[]{:S(2)}) collective-permute-start(f32[4,32]{1,0:T(4,128)S(1)} %get-tuple-element.38), channel_id=1, source_target_pairs={{0,1},{1,0},{2,3},{3,2},{4,5},{5,4},{6,7},{7,6},{8,9},{9,8},{10,11... | collective-permute-start | bytes 1544 | tf_op jit(solution)/shard_map/ppermute | solution.py:23
  27.6 3.0 %collective-permute-start.8 = (f32[4,32]{1,0:T(4,128)S(1)}, f32[4,32]{1,0:T(4,128)S(1)}, u32[]{:S(2)}, u32[]{:S(2)}) collective-permute-start(f32[4,32]{1,0:T(4,128)S(1)} %min.15), channel_id=1, source_target_pairs={{0,3},{1,2},{2,1},{3,0},{4,7},{5,6},{6,5},{7,4},{8,11},{9,10},{10,... | collective-permute-start | bytes 1544 | tf_op jit(solution)/shard_map/ppermute | solution.py:23
  30.6 3.9 %collective-permute-start.11 = (f32[4,32]{1,0:T(4,128)S(1)}, f32[4,32]{1,0:T(4,128)S(1)}, u32[]{:S(2)}, u32[]{:S(2)}) collective-permute-start(f32[4,32]{1,0:T(4,128)S(1)} %min.16), channel_id=1, source_target_pairs={{0,9},{1,8},{2,11},{3,10},{4,13},{5,12},{6,15},{7,14},{8,1},{9,0},... | collective-permute-start | bytes 1544 | tf_op jit(solution)/shard_map/ppermute | solution.py:23
  30.6 4.8 %collective-permute-start.10 = (f32[4,32]{1,0:T(4,128)S(1)}, f32[4,32]{1,0:T(4,128)S(1)}, u32[]{:S(2)}, u32[]{:S(2)}) collective-permute-start(f32[4,32]{1,0:T(4,128)S(1)} %min.16), channel_id=1, source_target_pairs={{0,13},{1,12},{2,15},{3,14},{4,9},{5,8},{6,11},{7,10},{8,5},{9,4},... | collective-permute-start | bytes 1544 | tf_op jit(solution)/shard_map/ppermute | solution.py:23
  33.1 3.0 %collective-permute-start.9 = (f32[4,32]{1,0:T(4,128)S(1)}, f32[4,32]{1,0:T(4,128)S(1)}, u32[]{:S(2)}, u32[]{:S(2)}) collective-permute-start(f32[4,32]{1,0:T(4,128)S(1)} %min.16), channel_id=1, source_target_pairs={{0,5},{1,4},{2,7},{3,6},{4,1},{5,0},{6,3},{7,2},{8,13},{9,12},{10,... | collective-permute-start | bytes 1544 | tf_op jit(solution)/shard_map/ppermute | solution.py:23

commit v7 on v6

--- a/solution.py
+++ b/solution.py
@@ -229,14 +229,17 @@
 def first_columns_kernel(
     limit, starts, excl, both, hankel, scale_ref, offset_ref, band_ref, sums_ref, spread_ref, banned, beyond
 ):
-    width = banned.shape[1]
-    columns = lax.axis_index("col") * width + lax.broadcasted_iota(jnp.int32, (QB, width), 1)
-    apart = lax.broadcasted_iota(jnp.int32, (QB, width), 0) - columns
-    last = jnp.where(columns > limit, 1.0, 0.0)
-    for turn in range(starts.shape[0]):
-        near = jnp.where(jnp.abs(apart + starts[turn]) < excl[0], 1.0, last)
-        banned[turn * QB : (turn + 1) * QB, :] = near
-    beyond[...] = last[:8]
+    width = beyond.shape[1]
+    here = lax.axis_index("col")
+    for i in range(CORES):
+        columns = (here ^ i) * width + lax.broadcasted_iota(jnp.int32, (QB, width), 1)
+        apart = lax.broadcasted_iota(jnp.int32, (QB, width), 0) - columns
+        last = jnp.where(columns > limit, 1.0, 0.0)
+        for turn in range(starts.shape[0]):
+            near = jnp.where(jnp.abs(apart + starts[turn]) < excl[0], 1.0, last)
+            banned[i, turn * QB : (turn + 1) * QB, :] = near
+        if i == 0:
+            beyond[...] = last[:8]
     spread_ref[...] = spread_matrix(spread_ref.shape)
     band_ref[...] = band_matrix(band_ref.shape)
     sums_ref[...] = column_band(sums_ref.shape)
@@ -305,16 +308,24 @@
     out[...] = covariances(offsets, windows_ref, hankel, scale_ref, offset_ref, which)
 
 
-def minima_kernel(turns, channels, own, other, banned, beyond, row_out, col_out):
+def allowed_minima(channels, which, own, other, banned):
     distance = 1.0 - (own[...] + other[...]) * (1.0 / (M * channels))
-    distance = jnp.where(banned[...] > 0.0, 4.0, distance)
-    width = distance.shape[1]
+    distance = jnp.where(banned[which] > 0.0, 4.0, distance)
+    narrow = distance[:, :LANES]
+    for at in range(LANES, distance.shape[1], LANES):
+        narrow = jnp.minimum(narrow, distance[:, at : at + LANES])
+    return distance, narrow
+
+
+def own_minima_kernel(channels, own, other, banned, beyond, narrow_out, col_out):
+    distance, narrow_out[...] = allowed_minima(channels, 0, own, other, banned)
     column_min = jnp.min(distance, axis=0, keepdims=True)
     col_out[...] = jnp.where(beyond[:1, :] > 0.0, 0.0, column_min)
-    narrow = distance[:, :LANES]
-    for at in range(LANES, width, LANES):
-        narrow = jnp.minimum(narrow, distance[:, at : at + LANES])
-    flat = jnp.min(jnp.transpose(narrow), axis=0, keepdims=True)
+
+
+def chip_minima_kernel(turns, channels, own, other, banned, narrow, row_out):
+    _, others = allowed_minima(channels, 1, own, other, banned)
+    flat = jnp.min(jnp.transpose(jnp.minimum(others, narrow[...])), axis=0, keepdims=True)
     for turn in range(turns):
         row_out[turn : turn + 1, :] = flat[:, turn * QB : (turn + 1) * QB]
 
@@ -386,7 +397,7 @@
     band = jax.ShapeDtypeStruct((LANES // QB * (M + QB), LANES), bf16)
     sums = jax.ShapeDtypeStruct((2 * seg_len, seg_len), bf16)
     spread = jax.ShapeDtypeStruct((2 * half, half * LANES), bf16)
-    masked = [jax.ShapeDtypeStruct((queries, seg_len), f32), jax.ShapeDtypeStruct((8, seg_len), f32)]
+    masked = [jax.ShapeDtypeStruct((CORES, queries, seg_len), f32), jax.ShapeDtypeStruct((8, seg_len), f32)]
     *columns, band, sums, spread, banned, beyond = call(
         functools.partial(first_columns_kernel, limit),
         "columns",
@@ -457,18 +468,29 @@
         *columns,
         flops=5 * 10**8,
     )
-    rows, column = call(
-        functools.partial(minima_kernel, turns, channels),
-        "minima",
-        [jax.ShapeDtypeStruct((turns, QB), f32), jax.ShapeDtypeStruct((1, seg_len), f32)],
+    narrow, column = call(
+        functools.partial(own_minima_kernel, channels),
+        "own_minima",
+        [jax.ShapeDtypeStruct((queries, LANES), f32), jax.ShapeDtypeStruct((1, seg_len), f32)],
         "vvvv",
         mine,
         exchanged(theirs, 1),
         banned,
         beyond,
     )
+    rows = call(
+        functools.partial(chip_minima_kernel, turns, channels),
+        "chip_minima",
+        jax.ShapeDtypeStruct((turns, QB), f32),
+        "vvvv",
+        theirs,
+        exchanged(mine, 1),
+        banned,
+        narrow,
+    )
+
     crossed = [[mask + 1 for mask in (others[0], *reversed(others[1:]))] for others in rounds]
-    for others in [[1], [3], *crossed]:
+    for others in [[3], *crossed]:
         rows = functools.reduce(jnp.minimum, [exchanged(rows, mask) for mask in others], rows)
     return (rows, column.reshape(seg_len))
 

time: 36.9 us -> 36.4 us (0.986)
  waiting for transfers between devices: 10 us -> 8.61 us
  starting transfers between devices: 15.4 us -> 16.2 us
    ppermute x11, waiting for transfers between devices: 10 us -> 8.61 us  [exchanged(): return lax.ppermute(block, 'col', [(i, i ^ mask) for i in devices])]
    ppermute x11, starting transfers between devices: 10.7 us -> 11.5 us  [exchanged(): return lax.ppermute(block, 'col', [(i, i ^ mask) for i in devices])]
    pallas_call x9 -> x10, Pallas kernels: 8.59 us -> 8.78 us  [call(): pl.pallas_call(kernel, out_shape=out_shape, in_specs=[SPECS[space] for sp...]
  transfers between devices with their start and end apart: 12 -> 12, of which waited for: 8 -> 7; matrix products, arithmetic and copies ran while one was open for 2% -> 2% of each run, Pallas kernels for 11% -> 13%
where the time goes in v7:
time: 36.4 us; the launch traced here: 36.3 us
  starting transfers between devices  16.2 us (45%)
  Pallas kernels  8.78 us (24%)
  waiting for transfers between devices  8.61 us (24%)
  between operations  1.38 us (4%)
  other arithmetic  1.26 us (3%)
    ppermute x11, starting transfers between devices, exchanged(): return lax.ppermute(block, 'col', [(i, i ^ mask) for i in devices])  11.5 us
    pallas_call x10, Pallas kernels, call(): pl.pallas_call(kernel, out_shape=out_shape, in_specs=[SPECS[space] for sp...  8.78 us
    ppermute x11, waiting for transfers between devices, exchanged(): return lax.ppermute(block, 'col', [(i, i ^ mask) for i in devices])  8.61 us
    ppermute x1, starting transfers between devices, shards(): following = lax.ppermute(both[0, :, :seg_len], 'col', back)  4.7 us
  transfers between devices with their start and end apart: 12, of which 7 were waited for; matrix products, arithmetic and copies ran while one was open for 2% of the time, Pallas kernels for 13%

profile of v7, /device:TPU:0, one launch (start us, length us, event | category | flops | bytes accessed | tf_op | source)
XLA Modules:
  0.0 36.3 jit_solution(18006350157479370945)
XLA Ops:
  0.6 0.9 %share.1 = (f32[32,512]{1,0:T(8,128)S(1)}, f32[32,512]{1,0:T(8,128)S(1)}) custom-call(f32[64,256]{1,0:T(8,128)} %series.1, s32[64,256]{1,0:T(8,128)} %valid.1), custom_call_target="tpu_custom_call" | custom-call | flops 1000000 | bytes 1048576 | tf_op jit(solution)/shard_map/share/pallas_call | solution.py:340
  1.5 0.5 %collective-permute-start = (f32[32,512]{1,0:T(8,128)S(1)}, f32[32,512]{1,0:T(8,128)S(1)}, u32[]{:S(2)}, u32[]{:S(2)}) collective-permute-start(f32[32,512]{1,0:T(8,128)S(1)} %get-tuple-element.22), channel_id=1, source_target_pairs={{0,1},{1,0},{2,3},{3,2},{4,5},{5,4},{6,7},{7,6},{8,9},{9,8},{10,11... | collective-permute-start | bytes 196616 | tf_op jit(solution)/shard_map/ppermute | solution.py:23
  2.1 0.7 %fusion = (f32[4]{0:T(128)S(1)}, s32[4]{0:T(128)S(1)}) fusion(s32[4]{0:T(128)} %param.8, s32[4]{0:T(128)} %param.7), kind=kLoop, calls=%fused_computation.3 | loop fusion | flops 16 | bytes 64 | tf_op jit(solution)/shard_map/convert_element_type | solution.py:360
  2.7 0.2 collective-permute-done.other
  3.0 0.1 broadcast_in_dim.2.starts_ref
  3.0 0.3 chip.1
  3.3 5.0 %collective-permute-start.4 = (f32[32,640]{1,0:T(8,128)S(1)}, f32[32,640]{1,0:T(8,128)S(1)}, u32[]{:S(2)}, u32[]{:S(2)}) collective-permute-start(f32[32,640]{1,0:T(8,128)S(1)} %get-tuple-element.30.refs_0_), channel_id=1, source_target_pairs={{0,12},{1,13},{2,14},{3,15},{4,8},{5,9},{6,10},{7,11},{8,4},{9,5},... | collective-permute-start | bytes 245768 | tf_op jit(solution)/shard_map/ppermute | solution.py:23
  8.4 0.0 collective-permute-start.3
  8.4 0.6 %collective-permute-start.2 = (f32[32,640]{1,0:T(8,128)S(1)}, f32[32,640]{1,0:T(8,128)S(1)}, u32[]{:S(2)}, u32[]{:S(2)}) collective-permute-start(f32[32,640]{1,0:T(8,128)S(1)} %get-tuple-element.30.refs_0_), channel_id=1, source_target_pairs={{0,4},{1,5},{2,6},{3,7},{4,0},{5,1},{6,2},{7,3},{8,12},{9,13},{10,... | collective-permute-start | bytes 245768 | tf_op jit(solution)/shard_map/ppermute | solution.py:23
  9.0 4.7 %collective-permute-start.1 = (f32[32,256]{1,0:T(8,128)S(1)}, f32[32,256]{1,0:T(8,128)S(1)}, u32[]{:S(2)}, u32[]{:S(2)}) collective-permute-start(f32[32,256]{1,0:T(8,128)S(1)} %slice_bitcast_fusion), channel_id=1, source_target_pairs={{0,14},{1,15},{2,0},{3,1},{4,2},{5,3},{6,4},{7,5},{8,6},{9,7},{10,... | collective-permute-start | bytes 98312 | tf_op jit(solution)/shard_map/ppermute | solution.py:390
  14.4 2.0 %columns.2 = (bf16[2,32,256,256]{3,2,1,0:T(8,128)(2,1)S(1)}, f32[2,32,256]{2,1,0:T(8,128)S(1)}, f32[2,32,256]{2,1,0:T(8,128)S(1)}, bf16[1152,128]{1,0:T(8,128)(2...) custom-call(s32[4]{0:T(128)S(1)} %get-tuple-element.41.starts, ...), custom_call_target="tpu_custom_call" | custom-call | flops 100000000 | bytes 1048576 | tf_op jit(solution)/shard_map/columns/pallas_call | solution.py:340
  16.3 0.0 collective-permute-done.1.following.after_too
  16.4 0.0 collective-permute-done.4.refs_3_
  16.4 0.0 collective-permute-done.3.refs_2_
  16.4 0.0 collective-permute-done.2.refs_1_
  16.4 0.3 windows.1.refs_0_
  16.7 0.7 %collective-permute-start.5 = (f32[32,1280]{1,0:T(8,128)S(1)}, f32[32,1280]{1,0:T(8,128)S(1)}, u32[]{:S(2)}, u32[]{:S(2)}) collective-permute-start(f32[32,1280]{1,0:T(8,128)S(1)} %windows.1.refs_0_), channel_id=1, source_target_pairs={{0,2},{1,3},{2,0},{3,1},{4,6},{5,7},{6,4},{7,5},{8,10},{9,11},{10,... | collective-permute-start | bytes 491528 | tf_op jit(solution)/shard_map/ppermute | solution.py:23
  17.4 1.2 %columns.3 = (bf16[2,32,256,256]{3,2,1,0:T(8,128)(2,1)S(1)}, f32[2,32,256]{2,1,0:T(8,128)S(1)}, f32[2,32,256]{2,1,0:T(8,128)S(1)}) custom-call(f32[2,32,512]{2,1,0:T(8,128)S(1)} %get-tuple-element.23.both, f32[32,256]{1,0:T(8,128)S(1)} %collective-permute-done.1.following.after_too, ...), custom_call_target="tpu_custom_call", output_to_operand_aliasing={{0}: (3, {}), {1}: (4, {}), {2}: (5, {})} | custom-call | flops 100000000 | bytes 1048576 | tf_op jit(solution)/shard_map/columns/pallas_call | solution.py:340
  18.7 3.4 %collective-permute-done.5.refs_1_ = f32[32,1280]{1,0:T(8,128)S(1)} collective-permute-done((f32[32,1280]{1,0:T(8,128)S(1)}, f32[32,1280]{1,0:T(8,128)S(1)}, u32[]{:S(2)}, u32[]{:S(2)}) %collective-permute-start.5) | collective-permute-done | bytes 163872 | tf_op jit(solution)/shard_map/ppermute | solution.py:23
  22.1 0.3 query_stats.1.y
  22.4 2.0 %other_core.1 = (f32[128,256]{1,0:T(8,128)S(1)}, bf16[32,128,256]{2,1,0:T(8,128)(2,1)S(1)}) custom-call(f32[32,1408]{1,0:T(8,128)S(1)} %query_stats.1.y, bf16[64,4096]{1,0:T(8,128)(2,1)S(1)} %get-tuple-element.31.spread_ref, bf16[2,32,256,256]{3,2,1,0:T(8,128)(2,1)S(1)} %get-tuple-element.32.hankel, f32[2,32,256]{2,1,0:T(8,128)S(1)} %get-tuple-element.28.after.scale_ref, ...), custom_call_target="tpu_custom_call" | custom-call | flops 1000000 | bytes 1048576 | tf_op jit(solution)/shard_map/other_core/pallas_call | solution.py:340
  24.4 0.1 collective-permute-start.7
  24.5 0.9 %own_core.1.own = f32[128,256]{1,0:T(8,128)S(1)} custom-call(f32[32,1408]{1,0:T(8,128)S(1)} %query_stats.1.y, bf16[32,128,256]{2,1,0:T(8,128)(2,1)S(1)} %get-tuple-element.35.windows_ref, bf16[2,32,256,256]{3,2,1,0:T(8,128)(2,1)S(1)} %get-tuple-element.32.hankel, f32[2,32,256]{2,1,0:T(8,128)S(1)} %get-tuple-element.28.after.scale_ref, ...), custom_call_target="tpu_custom_call" | custom-call | flops 500000000 | bytes 1048576 | tf_op jit(solution)/shard_map/own_core/pallas_call | solution.py:340
  25.4 0.6 %collective-permute-start.6 = (f32[128,256]{1,0:T(8,128)S(1)}, f32[128,256]{1,0:T(8,128)S(1)}, u32[]{:S(2)}, u32[]{:S(2)}) collective-permute-start(f32[128,256]{1,0:T(8,128)S(1)} %own_core.1.own), channel_id=1, source_target_pairs={{0,1},{1,0},{2,3},{3,2},{4,5},{5,4},{6,7},{7,6},{8,9},{9,8},{10,11... | collective-permute-start | bytes 393224 | tf_op jit(solution)/shard_map/ppermute | solution.py:23
  26.0 0.0 collective-permute-done.7.other
  26.0 0.6 %own_minima.1 = (f32[128,128]{1,0:T(8,128)S(1)}, f32[1,256]{1,0:T(1,128)}) custom-call(f32[128,256]{1,0:T(8,128)S(1)} %own_core.1.own, f32[128,256]{1,0:T(8,128)S(1)} %collective-permute-done.7.other, f32[2,128,256]{2,1,0:T(8,128)S(1)} %get-tuple-element.36.banned, f32[8,256]{1,0:T(8,128)S(1)} %get-tuple-element.37.beyond), custom_call_target="tpu_custom_call" | custom-call | flops 1000000 | bytes 1048576 | tf_op jit(solution)/shard_map/own_minima/pallas_call | solution.py:340
  26.6 0.4 %collective-permute-done.6.other = f32[128,256]{1,0:T(8,128)S(1)} collective-permute-done((f32[128,256]{1,0:T(8,128)S(1)}, f32[128,256]{1,0:T(8,128)S(1)}, u32[]{:S(2)}, u32[]{:S(2)}) %collective-permute-start.6) | collective-permute-done | bytes 131104 | tf_op jit(solution)/shard_map/ppermute | solution.py:23
  27.0 0.2 chip_minima.1
  27.1 0.8 %collective-permute-start.8 = (f32[4,32]{1,0:T(4,128)S(1)}, f32[4,32]{1,0:T(4,128)S(1)}, u32[]{:S(2)}, u32[]{:S(2)}) collective-permute-start(f32[4,32]{1,0:T(4,128)S(1)} %chip_minima.1), channel_id=1, source_target_pairs={{0,3},{1,2},{2,1},{3,0},{4,7},{5,6},{6,5},{7,4},{8,11},{9,10},{10,... | collective-permute-start | bytes 1544 | tf_op jit(solution)/shard_map/ppermute | solution.py:23
  27.9 2.3 %collective-permute-done.8 = f32[4,32]{1,0:T(4,128)S(1)} collective-permute-done((f32[4,32]{1,0:T(4,128)S(1)}, f32[4,32]{1,0:T(4,128)S(1)}, u32[]{:S(2)}, u32[]{:S(2)}) %collective-permute-start.8) | collective-permute-done | bytes 544 | tf_op jit(solution)/shard_map/ppermute | solution.py:23
  30.2 0.0 collective-permute-start.11
  30.2 2.5 %collective-permute-start.10 = (f32[4,32]{1,0:T(4,128)S(1)}, f32[4,32]{1,0:T(4,128)S(1)}, u32[]{:S(2)}, u32[]{:S(2)}) collective-permute-start(f32[4,32]{1,0:T(4,128)S(1)} %min.12), channel_id=1, source_target_pairs={{0,13},{1,12},{2,15},{3,14},{4,9},{5,8},{6,11},{7,10},{8,5},{9,4},... | collective-permute-start | bytes 1544 | tf_op jit(solution)/shard_map/ppermute | solution.py:23
  32.7 0.7 %collective-permute-start.9 = (f32[4,32]{1,0:T(4,128)S(1)}, f32[4,32]{1,0:T(4,128)S(1)}, u32[]{:S(2)}, u32[]{:S(2)}) collective-permute-start(f32[4,32]{1,0:T(4,128)S(1)} %min.12), channel_id=1, source_target_pairs={{0,5},{1,4},{2,7},{3,6},{4,1},{5,0},{6,3},{7,2},{8,13},{9,12},{10,... | collective-permute-start | bytes 1544 | tf_op jit(solution)/shard_map/ppermute | solution.py:23
  33.3 0.7 %collective-permute-done.11 = f32[4,32]{1,0:T(4,128)S(1)} collective-permute-done((f32[4,32]{1,0:T(4,128)S(1)}, f32[4,32]{1,0:T(4,128)S(1)}, u32[]{:S(2)}, u32[]{:S(2)}) %collective-permute-start.11) | collective-permute-done | bytes 544 | tf_op jit(solution)/shard_map/ppermute | solution.py:23
  34.1 0.9 %collective-permute-done.10 = f32[4,32]{1,0:T(4,128)S(1)} collective-permute-done((f32[4,32]{1,0:T(4,128)S(1)}, f32[4,32]{1,0:T(4,128)S(1)}, u32[]{:S(2)}, u32[]{:S(2)}) %collective-permute-start.10) | collective-permute-done | bytes 544 | tf_op jit(solution)/shard_map/ppermute | solution.py:23
  35.0 0.7 %collective-permute-done.9 = f32[4,32]{1,0:T(4,128)S(1)} collective-permute-done((f32[4,32]{1,0:T(4,128)S(1)}, f32[4,32]{1,0:T(4,128)S(1)}, u32[]{:S(2)}, u32[]{:S(2)}) %collective-permute-start.9) | collective-permute-done | bytes 544 | tf_op jit(solution)/shard_map/ppermute | solution.py:23
  35.7 0.6 %minimum_minimum_fusion = f32[4,32]{1,0:T(4,128)} fusion(f32[4,32]{1,0:T(4,128)S(1)} %collective-permute-done.11, f32[4,32]{1,0:T(4,128)S(1)} %collective-permute-done.10, f32[4,32]{1,0:T(4,128)S(1)} %min.12, f32[4,32]{1,0:T(4,128)S(1)} %collective-permute-done.9), kind=kLoop, calls=%fused_computation.1 | loop fusion | flops 384 | bytes 2560 | tf_op jit(solution)/shard_map/min | solution.py:494
  (2 shorter events, 0.0 us)
Async XLA Ops:
  1.5 1.4 %collective-permute-start = (f32[32,512]{1,0:T(8,128)S(1)}, f32[32,512]{1,0:T(8,128)S(1)}, u32[]{:S(2)}, u32[]{:S(2)}) collective-permute-start(f32[32,512]{1,0:T(8,128)S(1)} %get-tuple-element.22), channel_id=1, source_target_pairs={{0,1},{1,0},{2,3},{3,2},{4,5},{5,4},{6,7},{7,6},{8,9},{9,8},{10,11... | collective-permute-start | bytes 196616 | tf_op jit(solution)/shard_map/ppermute | solution.py:23
  3.3 13.0 %collective-permute-start.4 = (f32[32,640]{1,0:T(8,128)S(1)}, f32[32,640]{1,0:T(8,128)S(1)}, u32[]{:S(2)}, u32[]{:S(2)}) collective-permute-start(f32[32,640]{1,0:T(8,128)S(1)} %get-tuple-element.30.refs_0_), channel_id=1, source_target_pairs={{0,12},{1,13},{2,14},{3,15},{4,8},{5,9},{6,10},{7,11},{8,4},{9,5},... | collective-permute-start | bytes 245768 | tf_op jit(solution)/shard_map/ppermute | solution.py:23
  8.4 8.0 %collective-permute-start.3 = (f32[32,640]{1,0:T(8,128)S(1)}, f32[32,640]{1,0:T(8,128)S(1)}, u32[]{:S(2)}, u32[]{:S(2)}) collective-permute-start(f32[32,640]{1,0:T(8,128)S(1)} %get-tuple-element.30.refs_0_), channel_id=1, source_target_pairs={{0,8},{1,9},{2,10},{3,11},{4,12},{5,13},{6,14},{7,15},{8,0},{9,1},... | collective-permute-start | bytes 245768 | tf_op jit(solution)/shard_map/ppermute | solution.py:23
  8.4 8.0 %collective-permute-start.2 = (f32[32,640]{1,0:T(8,128)S(1)}, f32[32,640]{1,0:T(8,128)S(1)}, u32[]{:S(2)}, u32[]{:S(2)}) collective-permute-start(f32[32,640]{1,0:T(8,128)S(1)} %get-tuple-element.30.refs_0_), channel_id=1, source_target_pairs={{0,4},{1,5},{2,6},{3,7},{4,0},{5,1},{6,2},{7,3},{8,12},{9,13},{10,... | collective-permute-start | bytes 245768 | tf_op jit(solution)/shard_map/ppermute | solution.py:23
  9.0 7.3 %collective-permute-start.1 = (f32[32,256]{1,0:T(8,128)S(1)}, f32[32,256]{1,0:T(8,128)S(1)}, u32[]{:S(2)}, u32[]{:S(2)}) collective-permute-start(f32[32,256]{1,0:T(8,128)S(1)} %slice_bitcast_fusion), channel_id=1, source_target_pairs={{0,14},{1,15},{2,0},{3,1},{4,2},{5,3},{6,4},{7,5},{8,6},{9,7},{10,... | collective-permute-start | bytes 98312 | tf_op jit(solution)/shard_map/ppermute | solution.py:390
  16.7 5.4 %collective-permute-start.5 = (f32[32,1280]{1,0:T(8,128)S(1)}, f32[32,1280]{1,0:T(8,128)S(1)}, u32[]{:S(2)}, u32[]{:S(2)}) collective-permute-start(f32[32,1280]{1,0:T(8,128)S(1)} %windows.1.refs_0_), channel_id=1, source_target_pairs={{0,2},{1,3},{2,0},{3,1},{4,6},{5,7},{6,4},{7,5},{8,10},{9,11},{10,... | collective-permute-start | bytes 491528 | tf_op jit(solution)/shard_map/ppermute | solution.py:23
  24.4 1.5 %collective-permute-start.7 = (f32[128,256]{1,0:T(8,128)S(1)}, f32[128,256]{1,0:T(8,128)S(1)}, u32[]{:S(2)}, u32[]{:S(2)}) collective-permute-start(f32[128,256]{1,0:T(8,128)S(1)} %get-tuple-element.34.own), channel_id=1, source_target_pairs={{0,1},{1,0},{2,3},{3,2},{4,5},{5,4},{6,7},{7,6},{8,9},{9,8},{10,11... | collective-permute-start | bytes 393224 | tf_op jit(solution)/shard_map/ppermute | solution.py:23
  25.4 1.5 %collective-permute-start.6 = (f32[128,256]{1,0:T(8,128)S(1)}, f32[128,256]{1,0:T(8,128)S(1)}, u32[]{:S(2)}, u32[]{:S(2)}) collective-permute-start(f32[128,256]{1,0:T(8,128)S(1)} %own_core.1.own), channel_id=1, source_target_pairs={{0,1},{1,0},{2,3},{3,2},{4,5},{5,4},{6,7},{7,6},{8,9},{9,8},{10,11... | collective-permute-start | bytes 393224 | tf_op jit(solution)/shard_map/ppermute | solution.py:23
  27.1 3.0 %collective-permute-start.8 = (f32[4,32]{1,0:T(4,128)S(1)}, f32[4,32]{1,0:T(4,128)S(1)}, u32[]{:S(2)}, u32[]{:S(2)}) collective-permute-start(f32[4,32]{1,0:T(4,128)S(1)} %chip_minima.1), channel_id=1, source_target_pairs={{0,3},{1,2},{2,1},{3,0},{4,7},{5,6},{6,5},{7,4},{8,11},{9,10},{10,... | collective-permute-start | bytes 1544 | tf_op jit(solution)/shard_map/ppermute | solution.py:23
  30.2 3.9 %collective-permute-start.11 = (f32[4,32]{1,0:T(4,128)S(1)}, f32[4,32]{1,0:T(4,128)S(1)}, u32[]{:S(2)}, u32[]{:S(2)}) collective-permute-start(f32[4,32]{1,0:T(4,128)S(1)} %min.12), channel_id=1, source_target_pairs={{0,9},{1,8},{2,11},{3,10},{4,13},{5,12},{6,15},{7,14},{8,1},{9,0},... | collective-permute-start | bytes 1544 | tf_op jit(solution)/shard_map/ppermute | solution.py:23
  30.2 4.8 %collective-permute-start.10 = (f32[4,32]{1,0:T(4,128)S(1)}, f32[4,32]{1,0:T(4,128)S(1)}, u32[]{:S(2)}, u32[]{:S(2)}) collective-permute-start(f32[4,32]{1,0:T(4,128)S(1)} %min.12), channel_id=1, source_target_pairs={{0,13},{1,12},{2,15},{3,14},{4,9},{5,8},{6,11},{7,10},{8,5},{9,4},... | collective-permute-start | bytes 1544 | tf_op jit(solution)/shard_map/ppermute | solution.py:23
  32.7 3.0 %collective-permute-start.9 = (f32[4,32]{1,0:T(4,128)S(1)}, f32[4,32]{1,0:T(4,128)S(1)}, u32[]{:S(2)}, u32[]{:S(2)}) collective-permute-start(f32[4,32]{1,0:T(4,128)S(1)} %min.12), channel_id=1, source_target_pairs={{0,5},{1,4},{2,7},{3,6},{4,1},{5,0},{6,3},{7,2},{8,13},{9,12},{10,... | collective-permute-start | bytes 1544 | tf_op jit(solution)/shard_map/ppermute | solution.py:23
